TPU v7x, 32 devices: a whole 2x2x4 slice. The times are simulated.
32 devices in a mesh: groups: 2 (over y), seq: 4 (over z), head: 2 (over x), sub: 2 (over core).
Axes of the slice: x: 2, y: 2, z: 4, core: 2. Of those that a mesh axis runs over, the one named last changes fastest.
Arguments:
- queries: bfloat16 [128, 128, 16, 128], P(('groups', 'seq'), None, ('head', 'sub')), parts along dimension 0, may hold values from -6 to 6
- keys: bfloat16 [128, 128, 16, 128], P(('groups', 'seq'), None, ('head', 'sub')), parts along dimension 0, may hold values from -6 to 6
- values: bfloat16 [128, 128, 16, 2, 128], P(('groups', 'seq'), None, ('head', 'sub')), parts along dimension 0, may hold values from -6 to 6
- log_decay: bfloat16 [128, 128, 16, 2], P(('groups', 'seq'), None, ('head', 'sub')), parts along dimension 0, may hold values from -0.8 to 0
- write_rate: bfloat16 [128, 128, 16, 2], P(('groups', 'seq'), None, ('head', 'sub')), parts along dimension 0, may hold values from 0.049804688 to 0.94921875
- norm_gain: bfloat16 [128], replicated, may hold values from 0.25 to 1.75
- parent_cache: float32 [32, 16, 2, 128, 128], P(('groups', 'seq'), ('head', 'sub')), parts along dimension 0, may hold values from -3 to 3
- order: int32 [128], P('groups'), parts along dimension 0, may hold values from 0 to 63, as said below
- parent_owner: int32 [128], P('groups'), parts along dimension 0, may hold values from 0 to 3, as said below
- parent_slot: int32 [128], P('groups'), parts along dimension 0, may hold values from 0 to 3
- token_count: int32 [128], P('groups'), parts along dimension 0, may hold values from 64 to 128, as said below
Outputs:
- mixed: bfloat16 [128, 128, 16, 2, 128], P(('groups', 'seq'), None, ('head', 'sub')), parts along dimension 0
- final_state: float32 [128, 16, 2, 128, 128], P(('groups', 'seq'), ('head', 'sub')), parts along dimension 0
There are 2 independent parts, one for each index of `groups`. A program takes and returns all parts, laid end to end along the dimension named above; an argument that names none is the same for every part. Nothing has to cross between parts.
Inputs may be any that keep to these rules, and one draw needn't show every extreme that they name: A permutation; slot j = p * 16 + s * 4 + r with r < 4 is processed by seq device p and holds an expansion that arrives on seq device s, so order[j] // 16 = s. `parent_owner`: among the 16 expansions processed by one seq device at most 8 have their parent on one owner, and on some device exactly 8 do. `token_count`: multiples of 64; some expansion has 128 and some has 64.
All inputs are finite; a program needn't handle non-finite values.
Results may differ from a plain program's by a relative error of at most 0.001.
Values may be sent and summed in bfloat16 or wider, within the bound.
No kernel may reach another device: no remote copies, remote signals or barrier semaphores. Data moves between devices by JAX's collectives and lax.ppermute only.
A program may use at most 192 MiB of HBM per device.

v0:
```python
import functools

import jax
import jax.numpy as jnp
from jax import lax
from jax.experimental import pallas as pl
from jax.experimental.pallas import tpu as pltpu
from jax.sharding import PartitionSpec as P

F32 = jnp.float32
BF16 = jnp.bfloat16
HALF = 64
LEN = 128
EPS = 1e-06
TOP = 32512.0
BIAS = 32768.0
CODE = 64.0
VMEM_LIMIT = 60 * 1024 * 1024
PARTS = 2
CODE_ROWS = 8
TOGETHER = 2


def dot(a, b):
    return jnp.dot(a, b, preferred_element_type=F32)


def dot_nt(a, b):
    return lax.dot_general(a, b, (((1,), (1,)), ((), ())), preferred_element_type=F32)


def split(x):
    high = x.astype(BF16)
    return high, (x - high.astype(F32)).astype(BF16)


def iota(shape, dim):
    return lax.broadcasted_iota(jnp.int32, shape, dim)


def step_of(code):
    return jnp.exp2(code * (1.0 / CODE)) * (1.0 / TOP)


def encode(x):
    peak = jnp.maximum(jnp.max(jnp.abs(x), axis=0, keepdims=True), 1e-30)
    code = jnp.ceil(jnp.log2(peak) * CODE) + 1.0
    inverse_step = 1.0 / step_of(code)
    whole = (x * inverse_step + (BIAS + 0.5)).astype(jnp.int32)
    words = jnp.bitwise_or(lax.shift_left(whole[:HALF], 16), whole[HALF:])
    return words, code


def decode(words):
    top = lax.shift_right_logical(words, 16)
    bottom = jnp.bitwise_and(words, 0xFFFF)
    return jnp.concatenate([top, bottom], axis=0).astype(F32) - BIAS


def code_tile(codes):
    row = iota((CODE_ROWS, LEN), 0)
    tile = jnp.zeros((CODE_ROWS, LEN), F32)
    for at, code in enumerate(codes):
        tile = jnp.where(row == at, code, tile)
    return tile.astype(jnp.int32)


def store_packed(ref, states):
    codes = []
    for h, state in enumerate(states):
        words, code = encode(state)
        ref[0, h * HALF:(h + 1) * HALF, :] = words
        codes.append(code)
    at = len(states) * HALF
    ref[0, at:at + CODE_ROWS, :] = code_tile(codes)


def load_steps(ref, heads):
    codes = ref[0, heads * HALF:heads * HALF + CODE_ROWS, :].astype(F32)
    return step_of(codes)


def pack_kernel(state_ref, out_ref):
    store_packed(out_ref, [state_ref[0, h] for h in range(state_ref.shape[1])])


def pack_parents(parents, part, heads):
    count = parents.shape[0]
    rows = heads * HALF + CODE_ROWS
    return pl.pallas_call(
        pack_kernel,
        grid=(count,),
        in_specs=[pl.BlockSpec((1, heads, LEN, LEN), lambda i: (i, part, 0, 0))],
        out_specs=pl.BlockSpec((1, rows, LEN), lambda i: (i, 0, 0)),
        out_shape=jax.ShapeDtypeStruct((count, rows, LEN), jnp.int32),
        compiler_params=pltpu.CompilerParams(vmem_limit_bytes=VMEM_LIMIT),
    )(parents)


def block_diag(x, mask):
    return jnp.where(mask, jnp.concatenate([x, x], axis=0), jnp.zeros((), x.dtype))


def pair_kernel(part, q_ref, k_ref, rate_ref, *refs):
    inv_ref, am_ref = refs[-2:]
    expansions, key_heads = q_ref.shape[:2]
    heads = 2 * key_heads
    all_heads = rate_ref.shape[1] // 2
    row = iota((LEN, LEN), 0)
    col = iota((LEN, LEN), 1)
    incl = row >= col
    strict = row > col
    diag_mask = row == col
    prow = iota((HALF, LEN), 0)
    plane = iota((HALF, LEN), 1)
    pcol = jnp.bitwise_and(plane, HALF - 1)
    left = plane < HALF
    bd_mask = (row < HALF) == (col < HALF)
    eye = (prow == pcol).astype(F32)

    def same(size):
        return (prow // size) == (pcol // size)

    base_mask = same(8)
    off_masks = [jnp.logical_and(same(2 * s), jnp.logical_not(same(s))) for s in (8, 16, 32)]
    lower_ones = incl.astype(F32).astype(BF16)
    unit = diag_mask.astype(F32).astype(BF16)

    a_full, where_at = [], []
    for e in range(expansions):
        rates = rate_ref[e].astype(BF16)
        cols = dot_nt(jnp.concatenate([lower_ones, unit], axis=0), rates)
        g_cols = cols[:LEN]
        b_cols = cols[LEN:]
        g_rows = dot_nt(rates, lower_ones)
        for m in range(key_heads):
            k = k_ref[e, m]
            gram = dot_nt(jnp.concatenate([q_ref[e, m], k], axis=0), k)
            qk, kk = gram[:LEN], gram[LEN:]
            diagonal = jnp.where(diag_mask, kk, 0.0)
            norm_row = lax.rsqrt(jnp.sum(diagonal, axis=0, keepdims=True) + EPS)
            norm_col = lax.rsqrt(jnp.sum(diagonal, axis=1, keepdims=True) + EPS)
            qk = qk * norm_row
            kk = kk * norm_row
            for r in range(2):
                h = 2 * m + r
                at = part * heads + h
                g_c = g_cols[:, at:at + 1]
                g_r = g_rows[at:at + 1, :]
                pair = jnp.exp(jnp.where(incl, g_c - g_r, -1e4))
                mix = qk * pair
                b_c = b_cols[:, all_heads + at:all_heads + at + 1]
                lower = jnp.where(strict, kk * pair, 0.0) * (b_c * norm_col)
                lower_h, lower_l = split(lower)
                mix_h, mix_l = split(mix)
                am_ref[e, h, :LEN, :LEN] = lower_h
                am_ref[e, h, :LEN, LEN:] = lower_l
                am_ref[e, h, LEN:, :LEN] = mix_h
                am_ref[e, h, LEN:, LEN:] = mix_l
                a_full.append(lower)
                where_at.append((e, h))

    chains = range(len(a_full))
    packed = [jnp.where(left, a_full[c][:HALF], a_full[c][HALF:]) for c in chains]
    base = [jnp.where(base_mask, packed[c], 0.0) for c in chains]
    base_h = [base[c].astype(BF16) for c in chains]
    power = [dot(base_h[c], block_diag(base_h[c], bd_mask)).astype(BF16) for c in chains]
    x = [eye - base[c] for c in chains]
    both = [
        dot(jnp.concatenate([x[c].astype(BF16), power[c]], axis=0), block_diag(power[c], bd_mask))
        for c in chains
    ]
    x = [x[c] + both[c][:HALF] for c in chains]
    power = [both[c][HALF:].astype(BF16) for c in chains]
    x = [x[c] + dot(x[c].astype(BF16), block_diag(power[c], bd_mask)) for c in chains]
    for off in off_masks:
        x_h = [x[c].astype(BF16) for c in chains]
        t = [
            dot(jnp.where(off, packed[c], 0.0).astype(BF16), block_diag(x_h[c], bd_mask)).astype(BF16)
            for c in chains
        ]
        x = [x[c] - dot(x_h[c], block_diag(t[c], bd_mask)) for c in chains]
    x_h = [x[c].astype(BF16) for c in chains]
    t = [
        dot(jnp.where(left, a_full[c][HALF:], 0.0).astype(BF16), block_diag(x_h[c], bd_mask)).astype(BF16)
        for c in chains
    ]
    zero_h = jnp.zeros((HALF, LEN), BF16)
    corner = [dot(jnp.where(left, zero_h, x_h[c]), jnp.concatenate([t[c], t[c]], axis=0)) for c in chains]
    for c in chains:
        e, h = where_at[c]
        inv_ref[e, h, :HALF, :] = jnp.where(left, x[c], 0.0).astype(BF16)
        inv_ref[e, h, HALF:, :] = jnp.where(left, -corner[c], x[c]).astype(BF16)


def pair_parts(part, half, q, k, rates, earlier=None):
    count, all_key_heads = q.shape[:2]
    key_heads = all_key_heads // PARTS
    heads = 2 * key_heads
    block = TOGETHER
    turns = count // block // 2
    first = half * turns
    head_block = pl.BlockSpec((block, key_heads, LEN, LEN), lambda i: (first + i, part, 0, 0))
    in_specs = [
        head_block,
        head_block,
        pl.BlockSpec((block,) + rates.shape[1:], lambda i: (first + i, 0, 0)),
    ]
    operands = [q, k, rates]
    aliases = {}
    if earlier is not None:
        in_specs += [pl.BlockSpec(memory_space=pl.ANY)] * 2
        aliases = {3: 0, 4: 1}
        operands += list(earlier)
    return pl.pallas_call(
        functools.partial(pair_kernel, part),
        grid=(turns,),
        in_specs=in_specs,
        out_specs=[
            pl.BlockSpec((block, heads, LEN, LEN), lambda i: (first + i, 0, 0, 0)),
            pl.BlockSpec((block, heads, 2 * LEN, 2 * LEN), lambda i: (first + i, 0, 0, 0)),
        ],
        out_shape=[
            jax.ShapeDtypeStruct((count, heads, LEN, LEN), BF16),
            jax.ShapeDtypeStruct((count, heads, 2 * LEN, 2 * LEN), BF16),
        ],
        input_output_aliases=aliases,
        compiler_params=pltpu.CompilerParams(vmem_limit_bytes=VMEM_LIMIT),
        cost_estimate=pl.CostEstimate(flops=1000, bytes_accessed=1000, transcendentals=0),
    )(*operands)


def state_kernel(part, home, shards_held, together, table, gain_ref, *refs):
    per = 6
    inputs = [refs[per * e:per * (e + 1)] for e in range(together)]
    parents = refs[per * together:per * together + shards_held]
    mixed_hbm, state_ref, states_in, mixed_out, arrivals, leaving = refs[-6:]
    turn, turns = pl.program_id(0), pl.num_programs(0)
    key_heads = inputs[0][0].shape[1]
    heads = 2 * key_heads
    all_heads = inputs[0][3].shape[1] // 2

    def fetch(i, slot):
        for e in range(together):
            for off in range(shards_held):
                @pl.when(table[1, i * together + e] == off)
                def _():
                    pltpu.make_async_copy(
                        parents[off].at[table[4, i * together + e]],
                        states_in.at[slot, e],
                        arrivals.at[slot, e],
                    ).start()

    def leave(i, slot, e):
        return pltpu.make_async_copy(
            mixed_out.at[slot, e],
            mixed_hbm.at[table[0, i * together + e], pl.ds(part * key_heads, key_heads)],
            leaving.at[slot, e],
        )

    slot = lax.rem(turn, 2)

    @pl.when(turn == 0)
    def _():
        fetch(0, 0)

    @pl.when(turn + 1 < turns)
    def _():
        fetch(turn + 1, lax.rem(turn + 1, 2))

    for e in range(together):
        pltpu.make_async_copy(parents[0].at[0], states_in.at[slot, e], arrivals.at[slot, e]).wait()

    @pl.when(turn >= 2)
    def _():
        for e in range(together):
            leave(turn - 2, slot, e).wait()

    row = iota((LEN, LEN), 0)
    col = iota((LEN, LEN), 1)
    lower_ones = (row >= col).astype(F32).astype(BF16)
    unit = (row == col).astype(F32).astype(BF16)
    gain = gain_ref[...].astype(F32)

    state, products, n_cols, g_cols, b_cols, eg_cols, steps = [], [], [], [], [], [], []
    for e in range(together):
        q_ref, k_ref, v_ref, rate_ref, inv_ref, am_ref = inputs[e]
        cols = dot_nt(jnp.concatenate([lower_ones, unit], axis=0), rate_ref[0].astype(BF16))
        g_cols.append(cols[:LEN])
        b_cols.append(cols[LEN:])
        eg_cols.append(jnp.exp(cols[:LEN]))
        steps.append(load_steps(states_in.at[slot, pl.ds(e, 1)], heads))
        for m in range(key_heads):
            highs, lows = [], []
            for r in range(2):
                h = 2 * m + r
                whole = decode(states_in[slot, e, h * HALF:(h + 1) * HALF, :])
                high, low = split(whole)
                highs.append(high)
                lows.append(low)
                state.append(whole)
            rhs = jnp.concatenate(
                [jnp.concatenate(highs, axis=1), jnp.concatenate(lows, axis=1)], axis=0
            )
            lhs = jnp.concatenate([q_ref[0, m], k_ref[0, m]], axis=0)
            products.append(dot(jnp.concatenate([lhs, lhs], axis=1), rhs))
            keys = k_ref[0, m].astype(F32)
            n_cols.append(lax.rsqrt(jnp.sum(keys * keys, axis=1, keepdims=True) + EPS))

    every = [(e, h) for e in range(together) for h in range(heads)]

    def at_of(h):
        return part * heads + h

    def decay_at(e, h):
        return eg_cols[e][:, at_of(h):at_of(h) + 1]

    def product_at(e, h):
        lane = (h % 2) * LEN
        return products[e * key_heads + h // 2][:, lane:lane + LEN]

    right, first = [], []
    for e, h in every:
        v_ref, inv_ref = inputs[e][2], inputs[e][4]
        ks = product_at(e, h)[LEN:] * steps[e][h:h + 1, :]
        rate = b_cols[e][:, all_heads + at_of(h):all_heads + at_of(h) + 1]
        scale = decay_at(e, h) * n_cols[e * key_heads + h // 2]
        want = rate * (v_ref[0, h // 2, h % 2].astype(F32) - scale * ks)
        right.append(want)
        first.append(dot(inv_ref[0, h], want.astype(BF16)).astype(BF16))
    am_v = [
        dot(inputs[e][5][0, h], jnp.concatenate([first[c], first[c]], axis=0))
        for c, (e, h) in enumerate(every)
    ]
    delta = [
        dot(inputs[e][4][0, h], (right[c] - first[c].astype(F32) - am_v[c][:LEN]).astype(BF16))
        for c, (e, h) in enumerate(every)
    ]
    scaled = []
    for c, (e, h) in enumerate(every):
        g_c = g_cols[e][:, at_of(h):at_of(h) + 1]
        tail = jnp.exp(g_c[LEN - 1:LEN, :] - g_c) * n_cols[e * key_heads + h // 2]
        scaled.append(split(tail * (first[c].astype(F32) + delta[c])))
    finals = []
    for e in range(together):
        for m in range(key_heads):
            turned = jnp.transpose(inputs[e][1][0, m])
            c = e * heads + 2 * m
            rhs = jnp.concatenate(
                [jnp.concatenate([scaled[c][p], scaled[c + 1][p]], axis=1) for p in range(2)], axis=0
            )
            added = dot(jnp.concatenate([turned, turned], axis=1), rhs)
            for r in range(2):
                h = 2 * m + r
                keep = decay_at(e, h)[LEN - 1:LEN, :] * steps[e][h:h + 1, :]
                finals.append(keep * state[c + r] + added[:, r * LEN:(r + 1) * LEN])
    for c, (e, h) in enumerate(every):
        qs = product_at(e, h)[:LEN] * steps[e][h:h + 1, :]
        out = decay_at(e, h) * qs + am_v[c][LEN:]
        out = out + dot(inputs[e][5][0, h, LEN:, :LEN], delta[c].astype(BF16))
        mean_square = jnp.mean(out * out, axis=1, keepdims=True)
        live = iota((LEN, 1), 0) < table[2, turn * together + e]
        scale = jnp.where(live, lax.rsqrt(mean_square + EPS), 0.0)
        mixed_out[slot, e, h // 2, h % 2] = (out * scale * gain).astype(BF16)
    for e in range(together):
        leave(turn, slot, e).start()
    for e in range(together):
        mine = finals[e * heads:(e + 1) * heads]
        if home:
            for h in range(heads):
                state_ref[e, h] = mine[h]
        else:
            store_packed(state_ref.at[pl.ds(e, 1)], mine)

    @pl.when(turn == turns - 1)
    def _():
        for e in range(together):
            leave(turn, slot, e).wait()

    @pl.when(jnp.logical_and(turn == turns - 1, turn >= 1))
    def _():
        for e in range(together):
            leave(turn - 1, 1 - slot, e).wait()


def recurrence(part, table, q, k, v, rates, pairs, parents, gain, mixed, final_shape=None, final=None):
    count = table.shape[1]
    together = min(TOGETHER, count)
    key_heads = q.shape[1] // PARTS
    heads = 2 * key_heads
    rows = heads * HALF + CODE_ROWS
    in_specs = [pl.BlockSpec((1, LEN), lambda i, t: (0, 0))]
    operands = [gain]

    def one(shape, e, at):
        def index(i, t):
            return (t[0, i * together + e], at) + (0,) * (len(shape) - 2)

        return pl.BlockSpec(shape, index)

    for e in range(together):
        in_specs += [
            one((1, key_heads, LEN, LEN), e, part),
            one((1, key_heads, LEN, LEN), e, part),
            one((1, key_heads, 2, LEN, LEN), e, part),
            one((1,) + rates.shape[1:], e, 0),
            one((1, heads, LEN, LEN), e, 0),
            one((1, heads, 2 * LEN, 2 * LEN), e, 0),
        ]
        operands += [q, k, v, rates, *pairs]
    in_specs += [pl.BlockSpec(memory_space=pl.ANY)] * len(parents)
    operands += parents
    aliases = {}
    if mixed is not None:
        in_specs.append(pl.BlockSpec(memory_space=pl.ANY))
        aliases[1 + len(operands)] = 0
        operands.append(mixed)
    mixed_spec = pl.BlockSpec(memory_space=pl.ANY)
    mixed_shape = jax.ShapeDtypeStruct(v.shape, BF16)
    if final_shape is None:
        state_spec = pl.BlockSpec((together, rows, LEN), lambda i, t: (i, 0, 0))
        state_shape = jax.ShapeDtypeStruct((count, rows, LEN), jnp.int32)
    else:
        if final is not None:
            in_specs.append(pl.BlockSpec(memory_space=pl.ANY))
            aliases[1 + len(operands)] = 1
            operands.append(final)
        state_spec = pl.BlockSpec((together, heads, LEN, LEN), lambda i, t: (t[3, i], part, 0, 0))
        state_shape = jax.ShapeDtypeStruct(final_shape, F32)
    return pl.pallas_call(
        functools.partial(state_kernel, part, final_shape is not None, len(parents), together),
        grid_spec=pltpu.PrefetchScalarGridSpec(
            num_scalar_prefetch=1,
            grid=(count // together,),
            in_specs=in_specs,
            out_specs=[mixed_spec, state_spec],
            scratch_shapes=[
                pltpu.VMEM((2, together, rows, LEN), jnp.int32),
                pltpu.VMEM((2, together, key_heads, 2, LEN, LEN), BF16),
                pltpu.SemaphoreType.DMA((2, together)),
                pltpu.SemaphoreType.DMA((2, together)),
            ],
        ),
        out_shape=[mixed_shape, state_shape],
        input_output_aliases=aliases,
        compiler_params=pltpu.CompilerParams(vmem_limit_bytes=VMEM_LIMIT),
        cost_estimate=pl.CostEstimate(flops=1000, bytes_accessed=1000, transcendentals=0),
    )(table, *operands)


def unpack_kernel(table, packed_ref, old_ref, out_ref):
    count, heads = out_ref.shape[:2]
    for e in range(count):
        steps = load_steps(packed_ref.at[pl.ds(e, 1)], heads)
        for h in range(heads):
            out_ref[e, h] = decode(packed_ref[e, h * HALF:(h + 1) * HALF, :]) * steps[h:h + 1, :]


def unpack_states(part, table, packed, final):
    count, rows = packed.shape[:2]
    heads = final.shape[1] // PARTS
    block = max(1, count // 2)
    turns = count // block
    return pl.pallas_call(
        unpack_kernel,
        grid_spec=pltpu.PrefetchScalarGridSpec(
            num_scalar_prefetch=1,
            grid=(turns,),
            in_specs=[
                pl.BlockSpec((block, rows, LEN), lambda i, t: (i, 0, 0)),
                pl.BlockSpec(memory_space=pl.ANY),
            ],
            out_specs=pl.BlockSpec((block, heads, LEN, LEN), lambda i, t: (t[0] * turns + i, part, 0, 0)),
        ),
        out_shape=jax.ShapeDtypeStruct(final.shape, F32),
        input_output_aliases={2: 0},
        compiler_params=pltpu.CompilerParams(vmem_limit_bytes=VMEM_LIMIT),
        cost_estimate=pl.CostEstimate(flops=1000, bytes_accessed=1000, transcendentals=0),
    )(table, packed, final)


def shards(
    queries,
    keys,
    values,
    log_decay,
    write_rate,
    norm_gain,
    parent_cache,
    order,
    parent_owner,
    parent_slot,
    token_count,
):
    seq_count = lax.axis_size("seq")
    me = lax.axis_index("seq")
    per_device, length, key_heads, key_dim = queries.shape
    per_peer = per_device // seq_count
    cache_rows = parent_cache.shape[0]
    heads = 2 * key_heads
    part_heads = heads // PARTS

    parents = parent_cache.reshape((cache_rows, heads, key_dim, key_dim))
    own = [pack_parents(parents, part, part_heads) for part in range(PARTS)]

    def swap(tensor, off):
        return lax.ppermute(tensor, "seq", [(i, i ^ off) for i in range(seq_count)])

    def spread(held, off):
        while off:
            held = {**held, **{at ^ off: swap(held[at], off) for at in held}}
            off //= 2
        return held

    half_way = seq_count // 2
    far = swap(own[0], half_way)
    q = jnp.transpose(queries, (0, 2, 1, 3))
    k = jnp.transpose(keys, (0, 2, 1, 3))
    v = jnp.transpose(values, (0, 2, 3, 1, 4))

    def rows_of(tensor):
        return jnp.transpose(tensor, (0, 2, 3, 1)).reshape(per_device, heads, length).astype(F32)

    here_count = lax.dynamic_slice_in_dim(token_count, me * per_device, per_device)
    alive = jnp.arange(length, dtype=jnp.int32) < here_count[:, None, None]
    rates = jnp.where(alive, jnp.concatenate([rows_of(log_decay), rows_of(write_rate)], axis=1), 0.0)
    gain = norm_gain.reshape(1, -1)
    pairs = [None, None]
    own[0], q = lax.optimization_barrier((own[0], q))
    pairs[0] = pair_parts(0, 0, q, k, rates)
    pairs[0], v, far, own[1] = lax.optimization_barrier((pairs[0], v, far, own[1]))
    held_0 = spread({0: own[0], half_way: far}, half_way // 2)
    far_1 = swap(own[1], half_way)
    pairs[0] = pair_parts(0, 1, q, k, rates, pairs[0])
    rates, pairs[0] = lax.optimization_barrier((rates, pairs[0]))
    pairs[1] = pair_parts(1, 0, q, k, rates)
    pairs, held_0, far_1, own = lax.optimization_barrier((pairs, held_0, far_1, own))
    held_1 = spread({0: own[1], half_way: far_1}, half_way // 2)
    gathered = [[held[at] for at in range(seq_count)] for held in (held_0, held_1)]

    slot_grid = order.reshape(seq_count, seq_count, per_peer)
    local_ids = lax.dynamic_index_in_dim(slot_grid, me, 1, keepdims=False) - me * per_device
    here_owner = lax.dynamic_slice_in_dim(parent_owner, me * per_device, per_device)
    here_slot = lax.dynamic_slice_in_dim(parent_slot, me * per_device, per_device)

    def look_up(vector, ids):
        hit = ids[..., None] == jnp.arange(per_device, dtype=jnp.int32)
        return jnp.sum(jnp.where(hit, vector, 0), axis=-1)

    block = me * (per_peer // min(TOGETHER, per_peer))
    slots = block + jnp.broadcast_to(jnp.arange(per_peer, dtype=jnp.int32), local_ids.shape)
    tables = jnp.stack(
        [
            local_ids,
            jnp.bitwise_xor(look_up(here_owner, local_ids), me),
            look_up(here_count, local_ids),
            slots,
            look_up(here_slot, local_ids),
        ],
        axis=1,
    ).astype(jnp.int32)

    final_shape = (per_device, heads, key_dim, key_dim)
    mixed, final = None, None
    arrived = []
    crossing = list(reversed(range(half_way, seq_count)))
    near = list(reversed(range(1, half_way)))
    turns = [(part, away) for part in range(PARTS) for away in crossing + near]
    turns += [(part, 0) for part in range(PARTS)]
    for part, away in turns:
        peer = jnp.bitwise_xor(me, away)
        table = lax.dynamic_index_in_dim(tables, peer, 0, keepdims=False)
        if part == 0 and away == near[0]:
            rates, mixed, pairs[1] = lax.optimization_barrier((rates, mixed, pairs[1]))
            pairs[1] = pair_parts(1, 1, q, k, rates, pairs[1])
            mixed, pairs[1], gathered[1] = lax.optimization_barrier((mixed, pairs[1], gathered[1]))
        common = (part, table, q, k, v, rates, pairs[part], gathered[part], gain, mixed)
        if away:
            mixed, packed = recurrence(*common)
            sent = swap(packed, away)
            arrived.append((part, peer, sent))
        else:
            mixed, final = recurrence(*common, final_shape, final)
    for part, peer, packed in arrived:
        table = peer.reshape(1)
        final = unpack_states(part, table, packed, final)
    mixed_out = jnp.transpose(mixed, (0, 3, 1, 2, 4))
    final_out = final.reshape((per_device, key_heads, 2, key_dim, key_dim))
    return (mixed_out, final_out)


def solution(mesh):
    placed = (
        P(("groups", "seq"), None, ("head", "sub"), None),
        P(("groups", "seq"), None, ("head", "sub"), None),
        P(("groups", "seq"), None, ("head", "sub"), None, None),
        P(("groups", "seq"), None, ("head", "sub"), None),
        P(("groups", "seq"), None, ("head", "sub"), None),
        P(),
        P(("groups", "seq"), ("head", "sub"), None, None, None),
        P("groups"),
        P("groups"),
        P("groups"),
        P("groups"),
    )
    return jax.shard_map(
        shards,
        mesh=mesh,
        in_specs=placed,
        out_specs=(
            P(("groups", "seq"), None, ("head", "sub"), None, None),
            P(("groups", "seq"), ("head", "sub"), None, None, None),
        ),
        check_vma=False,
    )
```

profile of v0, /device:TPU:0, one launch (start us, length us, event | category | flops | bytes accessed | tf_op | source)
XLA Modules:
  0.0 184.3 jit_solution(4529246968730774402)
XLA Ops:
  0.6 3.4 %shard_map.122.refs_12_ = s32[4,264,128]{2,1,0:T(8,128)} custom-call(f32[4,8,128,128]{3,2,1,0:T(8,128)} %bitcast.98), custom_call_target="tpu_custom_call" | custom-call | tf_op jit(solution)/shard_map/pallas_call | solution.py:90
  4.1 4.1 %collective-permute-start = (s32[4,264,128]{2,1,0:T(8,128)}, s32[4,264,128]{2,1,0:T(8,128)S(1)}, u32[]{:S(2)}, u32[]{:S(2)}) collective-permute-start(s32[4,264,128]{2,1,0:T(8,128)} %shard_map.122.refs_12_), channel_id=1, source_target_pairs={{0,8},{4,12},{8,0},{12,4},{1,9},{5,13},{9,1},{13,5},{2,10},{6,14},... | collective-permute-start | bytes 1622024 | tf_op jit(solution)/shard_map/ppermute | solution.py:507
  8.2 3.5 %copy.78 = bf16[16,128,4,128]{3,1,2,0:T(8,128)(2,1)} copy(bf16[16,128,4,128]{3,2,1,0:T(4,128)(2,1)} %param.11) | data formatting | bytes 4194304 | tf_op args[0]
  13.3 3.5 %copy.77 = bf16[16,128,4,128]{3,1,2,0:T(8,128)(2,1)} copy(bf16[16,128,4,128]{3,2,1,0:T(4,128)(2,1)} %param.12) | data formatting | bytes 4194304 | tf_op args[1]
  17.7 11.3 %shard_map.123 = (bf16[16,4,128,128]{3,2,1,0:T(8,128)(2,1)}, bf16[16,4,256,256]{3,2,1,0:T(8,128)(2,1)}) custom-call(bf16[16,4,128,128]{3,2,1,0:T(8,128)(2,1)} %bitcast.56, bf16[16,4,128,128]{3,2,1,0:T(8,128)(2,1)} %bitcast.76, f32[16,16,128]{2,1,0:T(8,128)} %convert_select_fusion.rate_ref.refs_3_.refs_9_), custom_call_target="tpu_custom_call" | custom-call | flops 1000 | bytes 1000 | tf_op jit(solution)/shard_map/pallas_call | solution.py:215
  29.0 3.4 %shard_map.124.refs_12_ = s32[4,264,128]{2,1,0:T(8,128)} custom-call(f32[4,8,128,128]{3,2,1,0:T(8,128)} %bitcast.99), custom_call_target="tpu_custom_call" | custom-call | tf_op jit(solution)/shard_map/pallas_call | solution.py:90
  32.7 5.5 %copy.76 = bf16[16,128,4,2,128]{4,1,3,2,0:T(8,128)(2,1)} copy(bf16[16,128,4,2,128]{4,3,2,1,0:T(2,128)(2,1)} %param.13) | data formatting | bytes 8388608 | tf_op args[2]
  39.1 11.4 %shard_map.125 = (bf16[16,4,128,128]{3,2,1,0:T(8,128)(2,1)}, bf16[16,4,256,256]{3,2,1,0:T(8,128)(2,1)}) custom-call(bf16[16,4,128,128]{3,2,1,0:T(8,128)(2,1)} %bitcast.57, bf16[16,4,128,128]{3,2,1,0:T(8,128)(2,1)} %bitcast.77, f32[16,16,128]{2,1,0:T(8,128)} %convert_select_fusion.rate_ref.refs_3_.refs_9_, ...), custom_call_target="tpu_custom_call", output_to_operand_aliasing={{0}: (3, {}), {1}: (4, {})} | custom-call | flops 1000 | bytes 1000 | tf_op jit(solution)/shard_map/pallas_call | solution.py:215
  50.5 11.4 %shard_map.126 = (bf16[16,4,128,128]{3,2,1,0:T(8,128)(2,1)}, bf16[16,4,256,256]{3,2,1,0:T(8,128)(2,1)}) custom-call(bf16[16,4,128,128]{3,2,1,0:T(8,128)(2,1)} %bitcast.58, bf16[16,4,128,128]{3,2,1,0:T(8,128)(2,1)} %bitcast.78, f32[16,16,128]{2,1,0:T(8,128)} %convert_select_fusion.rate_ref.refs_3_.refs_9_), custom_call_target="tpu_custom_call" | custom-call | flops 1000 | bytes 1000 | tf_op jit(solution)/shard_map/pallas_call | solution.py:215
  62.1 2.4 %collective-permute-done.3.refs_14_ = s32[4,264,128]{2,1,0:T(8,128)S(1)} collective-permute-done((s32[4,264,128]{2,1,0:T(8,128)S(1)}, s32[4,264,128]{2,1,0:T(8,128)S(1)}, u32[]{:S(2)}, u32[]{:S(2)}) %collective-permute-start.3) | collective-permute-done | bytes 540704 | tf_op jit(solution)/shard_map/ppermute | solution.py:507
  64.4 2.0 %collective-permute-start.5 = (s32[4,264,128]{2,1,0:T(8,128)S(1)}, s32[4,264,128]{2,1,0:T(8,128)S(1)}, u32[]{:S(2)}, u32[]{:S(2)}) collective-permute-start(s32[4,264,128]{2,1,0:T(8,128)S(1)} %collective-permute-done.3.refs_14_), channel_id=1, source_target_pairs={{0,4},{4,0},{8,12},{12,8},{1,5},{5,1},{9,13},{13,9},{2,6},{6,2},{1... | collective-permute-start | bytes 1622024 | tf_op jit(solution)/shard_map/ppermute | solution.py:507
  67.1 8.3 %shard_map.127 = (bf16[16,4,2,128,128]{4,3,2,1,0:T(8,128)(2,1)}, s32[4,264,128]{2,1,0:T(8,128)}) custom-call(s32[5,4]{1,0:T(8,128)} %get-tuple-element.120.table, bf16[1,128]{1,0:T(2,128)(2,1)} %bitcast.100, bf16[16,4,128,128]{3,2,1,0:T(8,128)(2,1)} %bitcast.59, bf16[16,4,128,128]{3,2,1,0:T(8,128)(2,1)} %bitcast.79, bf16[16,4,2,128,128]{4,3,2,1,0:T(8,128)(2,1)} %bitcast.40, ...), custom_call_target="tpu_custom_call" | custom-call | flops 1000 | bytes 1000 | tf_op jit(solution)/shard_map/pallas_call | solution.py:430
  77.0 8.3 %shard_map.128 = (bf16[16,4,2,128,128]{4,3,2,1,0:T(8,128)(2,1)}, s32[4,264,128]{2,1,0:T(8,128)}) custom-call(s32[5,4]{1,0:T(8,128)} %get-tuple-element.121.table, bf16[1,128]{1,0:T(2,128)(2,1)} %bitcast.101, bf16[16,4,128,128]{3,2,1,0:T(8,128)(2,1)} %bitcast.61, bf16[16,4,128,128]{3,2,1,0:T(8,128)(2,1)} %bitcast.81, ...), custom_call_target="tpu_custom_call", output_to_operand_aliasing={{0}: (18, {})} | custom-call | flops 1000 | bytes 1000 | tf_op jit(solution)/shard_map/pallas_call | solution.py:430
  85.4 11.5 %shard_map.129 = (bf16[16,4,128,128]{3,2,1,0:T(8,128)(2,1)}, bf16[16,4,256,256]{3,2,1,0:T(8,128)(2,1)}) custom-call(bf16[16,4,128,128]{3,2,1,0:T(8,128)(2,1)} %bitcast.63, bf16[16,4,128,128]{3,2,1,0:T(8,128)(2,1)} %bitcast.83, f32[16,16,128]{2,1,0:T(8,128)} %convert_select_fusion.rate_ref.refs_3_.refs_9_, ...), custom_call_target="tpu_custom_call", output_to_operand_aliasing={{0}: (3, {}), {1}: (4, {})} | custom-call | flops 1000 | bytes 1000 | tf_op jit(solution)/shard_map/pallas_call | solution.py:215
  96.9 2.4 %collective-permute-done.5.refs_15_ = s32[4,264,128]{2,1,0:T(8,128)S(1)} collective-permute-done((s32[4,264,128]{2,1,0:T(8,128)S(1)}, s32[4,264,128]{2,1,0:T(8,128)S(1)}, u32[]{:S(2)}, u32[]{:S(2)}) %collective-permute-start.5) | collective-permute-done | bytes 540704 | tf_op jit(solution)/shard_map/ppermute | solution.py:507
  99.3 8.3 %shard_map.130 = (bf16[16,4,2,128,128]{4,3,2,1,0:T(8,128)(2,1)}, s32[4,264,128]{2,1,0:T(8,128)}) custom-call(s32[5,4]{1,0:T(8,128)} %get-tuple-element.119.table, bf16[1,128]{1,0:T(2,128)(2,1)} %bitcast.102, bf16[16,4,128,128]{3,2,1,0:T(8,128)(2,1)} %bitcast.64, bf16[16,4,128,128]{3,2,1,0:T(8,128)(2,1)} %bitcast.84, ...), custom_call_target="tpu_custom_call", output_to_operand_aliasing={{0}: (18, {})} | custom-call | flops 1000 | bytes 1000 | tf_op jit(solution)/shard_map/pallas_call | solution.py:430
  107.7 8.3 %shard_map.131 = (bf16[16,4,2,128,128]{4,3,2,1,0:T(8,128)(2,1)}, s32[4,264,128]{2,1,0:T(8,128)}) custom-call(s32[5,4]{1,0:T(8,128)} %get-tuple-element.120.table, bf16[1,128]{1,0:T(2,128)(2,1)} %bitcast.103, bf16[16,4,128,128]{3,2,1,0:T(8,128)(2,1)} %bitcast.66, bf16[16,4,128,128]{3,2,1,0:T(8,128)(2,1)} %bitcast.86, ...), custom_call_target="tpu_custom_call", output_to_operand_aliasing={{0}: (18, {})} | custom-call | flops 1000 | bytes 1000 | tf_op jit(solution)/shard_map/pallas_call | solution.py:430
  116.0 8.3 %shard_map.132 = (bf16[16,4,2,128,128]{4,3,2,1,0:T(8,128)(2,1)}, s32[4,264,128]{2,1,0:T(8,128)}) custom-call(s32[5,4]{1,0:T(8,128)} %get-tuple-element.121.table, bf16[1,128]{1,0:T(2,128)(2,1)} %bitcast.104, bf16[16,4,128,128]{3,2,1,0:T(8,128)(2,1)} %bitcast.68, bf16[16,4,128,128]{3,2,1,0:T(8,128)(2,1)} %bitcast.88, ...), custom_call_target="tpu_custom_call", output_to_operand_aliasing={{0}: (18, {})} | custom-call | flops 1000 | bytes 1000 | tf_op jit(solution)/shard_map/pallas_call | solution.py:430
  124.7 8.4 %shard_map.133 = (bf16[16,4,2,128,128]{4,3,2,1,0:T(8,128)(2,1)}, s32[4,264,128]{2,1,0:T(8,128)}) custom-call(s32[5,4]{1,0:T(8,128)} %get-tuple-element.119.table, bf16[1,128]{1,0:T(2,128)(2,1)} %bitcast.105, bf16[16,4,128,128]{3,2,1,0:T(8,128)(2,1)} %bitcast.70, bf16[16,4,128,128]{3,2,1,0:T(8,128)(2,1)} %bitcast.90, ...), custom_call_target="tpu_custom_call", output_to_operand_aliasing={{0}: (18, {})} | custom-call | flops 1000 | bytes 1000 | tf_op jit(solution)/shard_map/pallas_call | solution.py:430
  133.2 2.7 %collective-permute-start.8 = (s32[4,264,128]{2,1,0:T(8,128)}, s32[4,264,128]{2,1,0:T(8,128)S(1)}, u32[]{:S(2)}, u32[]{:S(2)}) collective-permute-start(s32[4,264,128]{2,1,0:T(8,128)} %get-tuple-element.107), channel_id=1, source_target_pairs={{0,12},{4,8},{8,4},{12,0},{1,13},{5,9},{9,5},{13,1},{2,14},{6,10},... | collective-permute-start | bytes 1622024 | tf_op jit(solution)/shard_map/ppermute | solution.py:507
  137.6 8.3 %shard_map.134 = (bf16[16,4,2,128,128]{4,3,2,1,0:T(8,128)(2,1)}, f32[16,8,128,128]{3,2,1,0:T(8,128)}) custom-call(s32[5,4]{1,0:T(8,128)} %get-tuple-element.122.table, bf16[1,128]{1,0:T(2,128)(2,1)} %bitcast.106, bf16[16,4,128,128]{3,2,1,0:T(8,128)(2,1)} %bitcast.72, bf16[16,4,128,128]{3,2,1,0:T(8,128)(2,1)} %bitcast.92, ...), custom_call_target="tpu_custom_call", output_to_operand_aliasing={{0}: (18, {})} | custom-call | flops 1000 | bytes 1000 | tf_op jit(solution)/shard_map/pallas_call | solution.py:430
  145.9 8.5 %shard_map.135 = (bf16[16,4,2,128,128]{4,3,2,1,0:T(8,128)(2,1)}, f32[16,8,128,128]{3,2,1,0:T(8,128)}) custom-call(s32[5,4]{1,0:T(8,128)} %get-tuple-element.122.table, bf16[1,128]{1,0:T(2,128)(2,1)} %bitcast.107, bf16[16,4,128,128]{3,2,1,0:T(8,128)(2,1)} %bitcast.74, ...), custom_call_target="tpu_custom_call", output_to_operand_aliasing={{0}: (18, {}), {1}: (19, {})} | custom-call | flops 1000 | bytes 1000 | tf_op jit(solution)/shard_map/pallas_call | solution.py:430
  159.3 8.5 %copy.68 = bf16[16,128,4,2,128]{4,3,2,1,0:T(2,128)(2,1)} copy(bf16[16,128,4,2,128]{4,1,3,2,0:T(8,128)(2,1)} %bitcast.97) | data formatting | bytes 8388608
  173.4 5.3 %collective-permute-done.7.packed_ref = s32[4,264,128]{2,1,0:T(8,128)S(1)} collective-permute-done((s32[4,264,128]{2,1,0:T(8,128)S(1)}, s32[4,264,128]{2,1,0:T(8,128)S(1)}, u32[]{:S(2)}, u32[]{:S(2)}) %collective-permute-start.7) | collective-permute-done | bytes 540704 | tf_op jit(solution)/shard_map/ppermute | solution.py:507
  (79 shorter events, 24.2 us)
Async XLA Ops:
  4.0 12.8 %copy-start.18 = (s32[64]{0:T(128)S(1)}, s32[64]{0:T(128)}, u32[]{:S(2)}) copy-start(s32[64]{0:T(128)} %param.21) | copy-start | bytes 772
  4.1 12.9 %copy-start.14 = (bf16[16,128,4,2]{1,3,2,0:T(2,128)(2,1)S(1)}, bf16[16,128,4,2]{1,3,2,0:T(2,128)(2,1)}, u32[]{:S(2)}) copy-start(bf16[16,128,4,2]{1,3,2,0:T(2,128)(2,1)} %param.15) | copy-start | bytes 98308
  4.1 12.9 %copy-start.15 = (bf16[16,128,4,2]{1,3,2,0:T(2,128)(2,1)S(1)}, bf16[16,128,4,2]{1,3,2,0:T(2,128)(2,1)}, u32[]{:S(2)}) copy-start(bf16[16,128,4,2]{1,3,2,0:T(2,128)(2,1)} %param.14) | copy-start | bytes 98308
  4.1 34.1 %collective-permute-start = (s32[4,264,128]{2,1,0:T(8,128)}, s32[4,264,128]{2,1,0:T(8,128)S(1)}, u32[]{:S(2)}, u32[]{:S(2)}) collective-permute-start(s32[4,264,128]{2,1,0:T(8,128)} %shard_map.122.refs_12_), channel_id=1, source_target_pairs={{0,8},{4,12},{8,0},{12,4},{1,9},{5,13},{9,1},{13,5},{2,10},{6,14},... | collective-permute-start | bytes 1622024 | tf_op jit(solution)/shard_map/ppermute | solution.py:507
  11.7 50.2 %collective-permute-start.1 = (s32[4,264,128]{2,1,0:T(8,128)S(1)}, s32[4,264,128]{2,1,0:T(8,128)S(1)}, u32[]{:S(2)}, u32[]{:S(2)}) collective-permute-start(s32[4,264,128]{2,1,0:T(8,128)S(1)} %copy-done), channel_id=1, source_target_pairs={{0,4},{4,0},{8,12},{12,8},{1,5},{5,1},{9,13},{13,9},{2,6},{6,2},{1... | collective-permute-start | bytes 1622024 | tf_op jit(solution)/shard_map/ppermute | solution.py:507
  16.8 15.6 %copy-start.19 = (s32[64]{0:T(128)S(1)}, s32[64]{0:T(128)}, u32[]{:S(2)}) copy-start(s32[64]{0:T(128)} %param.19) | copy-start | bytes 772
  16.8 15.7 %copy-start.20 = (s32[64]{0:T(128)S(1)}, s32[64]{0:T(128)}, u32[]{:S(2)}) copy-start(s32[64]{0:T(128)} %param.20) | copy-start | bytes 772
  16.8 15.8 %copy-start.16 = (s32[64]{0:T(128)S(1)}, s32[64]{0:T(128)}, u32[]{:S(2)}) copy-start(s32[64]{0:T(128)} %param.18) | copy-start | bytes 772
  38.2 12.3 %copy-start.2 = (s32[4,264,128]{2,1,0:T(8,128)}, s32[4,264,128]{2,1,0:T(8,128)S(1)}, u32[]{:S(2)}) copy-start(s32[4,264,128]{2,1,0:T(8,128)S(1)} %collective-permute-done.refs_14_) | copy-start | bytes 1622020
  38.2 23.9 %collective-permute-start.2 = (s32[4,264,128]{2,1,0:T(8,128)S(1)}, s32[4,264,128]{2,1,0:T(8,128)S(1)}, u32[]{:S(2)}, u32[]{:S(2)}) collective-permute-start(s32[4,264,128]{2,1,0:T(8,128)S(1)} %collective-permute-done.refs_14_), channel_id=1, source_target_pairs={{0,4},{4,0},{8,12},{12,8},{1,5},{5,1},{9,13},{13,9},{2,6},{6,2},{1... | collective-permute-start | bytes 1622024 | tf_op jit(solution)/shard_map/ppermute | solution.py:507
  38.7 25.8 %collective-permute-start.3 = (s32[4,264,128]{2,1,0:T(8,128)S(1)}, s32[4,264,128]{2,1,0:T(8,128)S(1)}, u32[]{:S(2)}, u32[]{:S(2)}) collective-permute-start(s32[4,264,128]{2,1,0:T(8,128)S(1)} %copy-done.1), channel_id=1, source_target_pairs={{0,8},{4,12},{8,0},{12,4},{1,9},{5,13},{9,1},{13,5},{2,10},{6,14},... | collective-permute-start | bytes 1622024 | tf_op jit(solution)/shard_map/ppermute | solution.py:507
  64.4 11.0 %copy-start.4 = (s32[4,264,128]{2,1,0:T(8,128)}, s32[4,264,128]{2,1,0:T(8,128)S(1)}, u32[]{:S(2)}) copy-start(s32[4,264,128]{2,1,0:T(8,128)S(1)} %collective-permute-done.3.refs_14_) | copy-start | bytes 1622020
  64.4 32.5 %collective-permute-start.4 = (s32[4,264,128]{2,1,0:T(8,128)S(1)}, s32[4,264,128]{2,1,0:T(8,128)S(1)}, u32[]{:S(2)}, u32[]{:S(2)}) collective-permute-start(s32[4,264,128]{2,1,0:T(8,128)S(1)} %copy-done.1), channel_id=1, source_target_pairs={{0,4},{4,0},{8,12},{12,8},{1,5},{5,1},{9,13},{13,9},{2,6},{6,2},{1... | collective-permute-start | bytes 1622024 | tf_op jit(solution)/shard_map/ppermute | solution.py:507
  64.4 34.9 %collective-permute-start.5 = (s32[4,264,128]{2,1,0:T(8,128)S(1)}, s32[4,264,128]{2,1,0:T(8,128)S(1)}, u32[]{:S(2)}, u32[]{:S(2)}) collective-permute-start(s32[4,264,128]{2,1,0:T(8,128)S(1)} %collective-permute-done.3.refs_14_), channel_id=1, source_target_pairs={{0,4},{4,0},{8,12},{12,8},{1,5},{5,1},{9,13},{13,9},{2,6},{6,2},{1... | collective-permute-start | bytes 1622024 | tf_op jit(solution)/shard_map/ppermute | solution.py:507
  75.4 61.1 %collective-permute-start.11 = (s32[4,264,128]{2,1,0:T(8,128)}, s32[4,264,128]{2,1,0:T(8,128)S(1)}, u32[]{:S(2)}, u32[]{:S(2)}) collective-permute-start(s32[4,264,128]{2,1,0:T(8,128)} %get-tuple-element.110), channel_id=1, source_target_pairs={{0,12},{4,8},{8,4},{12,0},{1,13},{5,9},{9,5},{13,1},{2,14},{6,10},... | collective-permute-start | bytes 1622024 | tf_op jit(solution)/shard_map/ppermute | solution.py:507
  85.2 71.2 %collective-permute-start.10 = (s32[4,264,128]{2,1,0:T(8,128)}, s32[4,264,128]{2,1,0:T(8,128)S(1)}, u32[]{:S(2)}, u32[]{:S(2)}) collective-permute-start(s32[4,264,128]{2,1,0:T(8,128)} %get-tuple-element.109), channel_id=1, source_target_pairs={{0,8},{4,12},{8,0},{12,4},{1,9},{5,13},{9,1},{13,5},{2,10},{6,14},... | collective-permute-start | bytes 1622024 | tf_op jit(solution)/shard_map/ppermute | solution.py:507
  96.9 10.7 %copy-start.6 = (s32[4,264,128]{2,1,0:T(8,128)}, s32[4,264,128]{2,1,0:T(8,128)S(1)}, u32[]{:S(2)}) copy-start(s32[4,264,128]{2,1,0:T(8,128)S(1)} %collective-permute-done.4.refs_13_) | copy-start | bytes 1622020
  99.3 8.3 %copy-start.7 = (s32[4,264,128]{2,1,0:T(8,128)}, s32[4,264,128]{2,1,0:T(8,128)S(1)}, u32[]{:S(2)}) copy-start(s32[4,264,128]{2,1,0:T(8,128)S(1)} %collective-permute-done.5.refs_15_) | copy-start | bytes 1622020
  124.3 43.5 %collective-permute-start.9 = (s32[4,264,128]{2,1,0:T(8,128)}, s32[4,264,128]{2,1,0:T(8,128)S(1)}, u32[]{:S(2)}, u32[]{:S(2)}) collective-permute-start(s32[4,264,128]{2,1,0:T(8,128)} %get-tuple-element.108), channel_id=1, source_target_pairs={{0,4},{4,0},{8,12},{12,8},{1,5},{5,1},{9,13},{13,9},{2,6},{6,2},{1... | collective-permute-start | bytes 1622024 | tf_op jit(solution)/shard_map/ppermute | solution.py:507
  124.7 11.1 %copy-start.17 = (s32[4,264,128]{2,1,0:T(8,128)S(1)}, s32[4,264,128]{2,1,0:T(8,128)}, u32[]{:S(2)}) copy-start(s32[4,264,128]{2,1,0:T(8,128)} %get-tuple-element.106) | copy-start | bytes 1622020
  133.2 37.4 %collective-permute-start.8 = (s32[4,264,128]{2,1,0:T(8,128)}, s32[4,264,128]{2,1,0:T(8,128)S(1)}, u32[]{:S(2)}, u32[]{:S(2)}) collective-permute-start(s32[4,264,128]{2,1,0:T(8,128)} %get-tuple-element.107), channel_id=1, source_target_pairs={{0,12},{4,8},{8,4},{12,0},{1,13},{5,9},{9,5},{13,1},{2,14},{6,10},... | collective-permute-start | bytes 1622024 | tf_op jit(solution)/shard_map/ppermute | solution.py:507
  135.9 42.9 %collective-permute-start.7 = (s32[4,264,128]{2,1,0:T(8,128)S(1)}, s32[4,264,128]{2,1,0:T(8,128)S(1)}, u32[]{:S(2)}, u32[]{:S(2)}) collective-permute-start(s32[4,264,128]{2,1,0:T(8,128)S(1)} %copy-done.17), channel_id=1, source_target_pairs={{0,8},{4,12},{8,0},{12,4},{1,9},{5,13},{9,1},{13,5},{2,10},{6,14},... | collective-permute-start | bytes 1622024 | tf_op jit(solution)/shard_map/ppermute | solution.py:507
  136.5 9.4 %copy-start.8 = (s32[4,264,128]{2,1,0:T(8,128)}, s32[4,264,128]{2,1,0:T(8,128)S(1)}, u32[]{:S(2)}) copy-start(s32[4,264,128]{2,1,0:T(8,128)S(1)} %collective-permute-done.11.packed_ref) | copy-start | bytes 1622020
  136.5 45.1 %collective-permute-start.6 = (s32[4,264,128]{2,1,0:T(8,128)}, s32[4,264,128]{2,1,0:T(8,128)S(1)}, u32[]{:S(2)}, u32[]{:S(2)}) collective-permute-start(s32[4,264,128]{2,1,0:T(8,128)} %get-tuple-element.105), channel_id=1, source_target_pairs={{0,4},{4,0},{8,12},{12,8},{1,5},{5,1},{9,13},{13,9},{2,6},{6,2},{1... | collective-permute-start | bytes 1622024 | tf_op jit(solution)/shard_map/ppermute | solution.py:507
  (9 other events, 27.8 us)
where the time goes:
time: 185 us; the launch traced here: 184 us
  Pallas kernels  131 us (71%)
  local copies, waits for them, and re-layouts  26.1 us (14%)
  starting transfers between devices  14.7 us (8%)
  waiting for transfers between devices  10.3 us (6%)
    pallas_call x8, Pallas kernels, recurrence(): pl.pallas_call(functools.partial(state_kernel, part, final_shape is not N...  66.8 us
    pallas_call x4, Pallas kernels, pair_parts(): pl.pallas_call(functools.partial(pair_kernel, part), grid=(turns,), in_sp...  45.7 us
    unnamed x46, local copies, waits for them, and re-layouts  25.2 us
    ppermute x12, starting transfers between devices, swap(): return lax.ppermute(tensor, 'seq', [(i, i ^ off) for i in range(seq_count)])  14.7 us
    pallas_call x6, Pallas kernels, unpack_states(): pl.pallas_call(unpack_kernel, grid_spec=pltpu.PrefetchScalarGridSpec(num_...  12 us
    ppermute x12, waiting for transfers between devices, swap(): return lax.ppermute(tensor, 'seq', [(i, i ^ off) for i in range(seq_count)])  10.3 us
    pallas_call x2, Pallas kernels, pack_parents(): pl.pallas_call(pack_kernel, grid=(count,), in_specs=[pl.BlockSpec((1, hea...  6.82 us
  transfers between devices with their start and end apart: 12, of which 4 were waited for; matrix products, arithmetic and copies ran while one was open for 13% of the time, Pallas kernels for 68%

commit v1 on v0

--- a/solution.py
+++ b/solution.py
@@ -15,7 +15,7 @@
 TOP = 32512.0
 BIAS = 32768.0
 CODE = 64.0
-VMEM_LIMIT = 60 * 1024 * 1024
+VMEM_LIMIT = 12 * 1024 * 1024
 PARTS = 2
 CODE_ROWS = 8
 TOGETHER = 2
@@ -80,19 +80,21 @@
     return step_of(codes)
 
 
-def pack_kernel(state_ref, out_ref):
-    store_packed(out_ref, [state_ref[0, h] for h in range(state_ref.shape[1])])
-
-
-def pack_parents(parents, part, heads):
-    count = parents.shape[0]
-    rows = heads * HALF + CODE_ROWS
+def pack_kernel(state_ref, *out_refs):
+    heads = state_ref.shape[1] // len(out_refs)
+    for part, out_ref in enumerate(out_refs):
+        store_packed(out_ref, [state_ref[0, part * heads + h] for h in range(heads)])
+
+
+def pack_parents(parents):
+    count, heads = parents.shape[:2]
+    rows = heads // PARTS * HALF + CODE_ROWS
     return pl.pallas_call(
         pack_kernel,
         grid=(count,),
-        in_specs=[pl.BlockSpec((1, heads, LEN, LEN), lambda i: (i, part, 0, 0))],
-        out_specs=pl.BlockSpec((1, rows, LEN), lambda i: (i, 0, 0)),
-        out_shape=jax.ShapeDtypeStruct((count, rows, LEN), jnp.int32),
+        in_specs=[pl.BlockSpec((1, heads, LEN, LEN), lambda i: (i, 0, 0, 0))],
+        out_specs=[pl.BlockSpec((1, rows, LEN), lambda i: (i, 0, 0))] * PARTS,
+        out_shape=[jax.ShapeDtypeStruct((count, rows, LEN), jnp.int32)] * PARTS,
         compiler_params=pltpu.CompilerParams(vmem_limit_bytes=VMEM_LIMIT),
     )(parents)
 
@@ -498,10 +500,9 @@
     per_peer = per_device // seq_count
     cache_rows = parent_cache.shape[0]
     heads = 2 * key_heads
-    part_heads = heads // PARTS
 
     parents = parent_cache.reshape((cache_rows, heads, key_dim, key_dim))
-    own = [pack_parents(parents, part, part_heads) for part in range(PARTS)]
+    own = list(pack_parents(parents))
 
     def swap(tensor, off):
         return lax.ppermute(tensor, "seq", [(i, i ^ off) for i in range(seq_count)])
@@ -532,9 +533,7 @@
     held_0 = spread({0: own[0], half_way: far}, half_way // 2)
     far_1 = swap(own[1], half_way)
     pairs[0] = pair_parts(0, 1, q, k, rates, pairs[0])
-    rates, pairs[0] = lax.optimization_barrier((rates, pairs[0]))
-    pairs[1] = pair_parts(1, 0, q, k, rates)
-    pairs, held_0, far_1, own = lax.optimization_barrier((pairs, held_0, far_1, own))
+    pairs[0], held_0, far_1, own, v = lax.optimization_barrier((pairs[0], held_0, far_1, own, v))
     held_1 = spread({0: own[1], half_way: far_1}, half_way // 2)
     gathered = [[held[at] for at in range(seq_count)] for held in (held_0, held_1)]
 
@@ -571,7 +570,8 @@
         peer = jnp.bitwise_xor(me, away)
         table = lax.dynamic_index_in_dim(tables, peer, 0, keepdims=False)
         if part == 0 and away == near[0]:
-            rates, mixed, pairs[1] = lax.optimization_barrier((rates, mixed, pairs[1]))
+            rates, mixed = lax.optimization_barrier((rates, mixed))
+            pairs[1] = pair_parts(1, 0, q, k, rates)
             pairs[1] = pair_parts(1, 1, q, k, rates, pairs[1])
             mixed, pairs[1], gathered[1] = lax.optimization_barrier((mixed, pairs[1], gathered[1]))
         common = (part, table, q, k, v, rates, pairs[part], gathered[part], gain, mixed)

time: 185 us -> 182 us (0.984)
  Pallas kernels: 131 us -> 102 us
  local copies, waits for them, and re-layouts: 26.1 us -> 43.8 us
  waiting for transfers between devices: 10.3 us -> 17.6 us
  starting transfers between devices: 14.7 us -> 16.8 us
    unnamed x46 -> x50, local copies, waits for them, and re-layouts: 25.2 us -> 43.4 us
    pallas_call x8, Pallas kernels: 66.8 us -> 51.7 us  [recurrence(): pl.pallas_call(functools.partial(state_kernel, part, final_shape is not N...]
    ppermute x12, waiting for transfers between devices: 10.3 us -> 17.6 us  [swap(): return lax.ppermute(tensor, 'seq', [(i, i ^ off) for i in range(seq_count)])]
    pallas_call x4, Pallas kernels: 45.7 us -> 39.1 us  [pair_parts(): pl.pallas_call(functools.partial(pair_kernel, part), grid=(turns,), in_sp...]
    pallas_call x2 -> x1, Pallas kernels: 6.82 us -> 0.61 us  [pack_parents(): pl.pallas_call(pack_kernel, grid=(count,), in_specs=[pl.BlockSpec((1, hea...]
    ppermute x12, starting transfers between devices: 14.7 us -> 16.8 us  [swap(): return lax.ppermute(tensor, 'seq', [(i, i ^ off) for i in range(seq_count)])]
  transfers between devices with their start and end apart: 12 -> 12, of which waited for: 4 -> 3; matrix products, arithmetic and copies ran while one was open for 13% -> 10% of each run, Pallas kernels for 68% -> 55%
where the time goes in v1:
time: 182 us; the launch traced here: 181 us
  Pallas kernels  102 us (56%)
  local copies, waits for them, and re-layouts  43.8 us (24%)
  waiting for transfers between devices  17.6 us (10%)
  starting transfers between devices  16.8 us (9%)
    pallas_call x8, Pallas kernels, recurrence(): pl.pallas_call(functools.partial(state_kernel, part, final_shape is not N...  51.7 us
    unnamed x50, local copies, waits for them, and re-layouts  43.4 us
    pallas_call x4, Pallas kernels, pair_parts(): pl.pallas_call(functools.partial(pair_kernel, part), grid=(turns,), in_sp...  39.1 us
    ppermute x12, waiting for transfers between devices, swap(): return lax.ppermute(tensor, 'seq', [(i, i ^ off) for i in range(seq_count)])  17.6 us
    ppermute x12, starting transfers between devices, swap(): return lax.ppermute(tensor, 'seq', [(i, i ^ off) for i in range(seq_count)])  16.8 us
    pallas_call x6, Pallas kernels, unpack_states(): pl.pallas_call(unpack_kernel, grid_spec=pltpu.PrefetchScalarGridSpec(num_...  10.2 us
  transfers between devices with their start and end apart: 12, of which 3 were waited for; matrix products, arithmetic and copies ran while one was open for 10% of the time, Pallas kernels for 55%

profile of v1, /device:TPU:0, one launch (start us, length us, event | category | flops | bytes accessed | tf_op | source)
XLA Modules:
  0.0 181.2 jit_solution(11462936415212916699)
XLA Ops:
  2.9 4.1 %collective-permute-start = (s32[4,264,128]{2,1,0:T(8,128)S(1)}, s32[4,264,128]{2,1,0:T(8,128)}, u32[]{:S(2)}, u32[]{:S(2)}) collective-permute-start(s32[4,264,128]{2,1,0:T(8,128)S(1)} %get-tuple-element.69.refs_12_), channel_id=1, source_target_pairs={{0,8},{4,12},{8,0},{12,4},{1,9},{5,13},{9,1},{13,5},{2,10},{6,14},... | collective-permute-start | bytes 1622024 | tf_op jit(solution)/shard_map/ppermute | solution.py:508
  10.8 3.6 %copy.77 = bf16[16,128,4,128]{3,1,2,0:T(8,128)(2,1)} copy(bf16[16,128,4,128]{3,2,1,0:T(4,128)(2,1)} %param.12) | data formatting | bytes 4194304 | tf_op args[1]
  16.1 9.7 %shard_map.123 = (bf16[16,4,128,128]{3,2,1,0:T(8,128)(2,1)S(1)}, bf16[16,4,256,256]{3,2,1,0:T(8,128)(2,1)S(1)}) custom-call(bf16[16,4,128,128]{3,2,1,0:T(8,128)(2,1)S(1)} %bitcast.56, bf16[16,4,128,128]{3,2,1,0:T(8,128)(2,1)S(1)} %bitcast.76, f32[16,16,128]{2,1,0:T(8,128)S(1)} %convert_select_fusion.rate_ref.refs_3_.refs_9_), custom_call_target="tpu_custom_call" | custom-call | flops 1000 | bytes 1000 | tf_op jit(solution)/shard_map/pallas_call | solution.py:217
  25.8 3.4 %copy-done.3 = bf16[16,4,256,256]{3,2,1,0:T(8,128)(2,1)} copy-done((bf16[16,4,256,256]{3,2,1,0:T(8,128)(2,1)}, bf16[16,4,256,256]{3,2,1,0:T(8,128)(2,1)S(1)}, u32[]{:S(2)}) %copy-start.3) | copy-done | bytes 8388632
  30.8 5.5 %copy.76 = bf16[16,128,4,2,128]{4,1,3,2,0:T(8,128)(2,1)} copy(bf16[16,128,4,2,128]{4,3,2,1,0:T(2,128)(2,1)} %param.13) | data formatting | bytes 8388608 | tf_op args[2]
  38.7 3.4 %copy-done.4 = bf16[16,4,256,256]{3,2,1,0:T(8,128)(2,1)S(1)} copy-done((bf16[16,4,256,256]{3,2,1,0:T(8,128)(2,1)S(1)}, bf16[16,4,256,256]{3,2,1,0:T(8,128)(2,1)}, u32[]{:S(2)}) %copy-start.4) | copy-done | bytes 8388632
  43.7 9.8 %shard_map.124 = (bf16[16,4,128,128]{3,2,1,0:T(8,128)(2,1)S(1)}, bf16[16,4,256,256]{3,2,1,0:T(8,128)(2,1)S(1)}) custom-call(bf16[16,4,128,128]{3,2,1,0:T(8,128)(2,1)S(1)} %bitcast.57, bf16[16,4,128,128]{3,2,1,0:T(8,128)(2,1)S(1)} %bitcast.77, ...), custom_call_target="tpu_custom_call", output_to_operand_aliasing={{0}: (3, {}), {1}: (4, {})} | custom-call | flops 1000 | bytes 1000 | tf_op jit(solution)/shard_map/pallas_call | solution.py:217
  53.5 3.4 %copy-done.5 = bf16[16,4,256,256]{3,2,1,0:T(8,128)(2,1)} copy-done((bf16[16,4,256,256]{3,2,1,0:T(8,128)(2,1)}, bf16[16,4,256,256]{3,2,1,0:T(8,128)(2,1)S(1)}, u32[]{:S(2)}) %copy-start.5) | copy-done | bytes 8388632
  56.9 3.7 %collective-permute-done.2.refs_15_ = s32[4,264,128]{2,1,0:T(8,128)} collective-permute-done((s32[4,264,128]{2,1,0:T(8,128)}, s32[4,264,128]{2,1,0:T(8,128)}, u32[]{:S(2)}, u32[]{:S(2)}) %collective-permute-start.2) | collective-permute-done | bytes 540704 | tf_op jit(solution)/shard_map/ppermute | solution.py:508
  64.6 3.4 %copy-done.6 = bf16[16,4,256,256]{3,2,1,0:T(8,128)(2,1)S(1)} copy-done((bf16[16,4,256,256]{3,2,1,0:T(8,128)(2,1)S(1)}, bf16[16,4,256,256]{3,2,1,0:T(8,128)(2,1)}, u32[]{:S(2)}) %copy-start.6) | copy-done | bytes 8388632
  67.9 5.8 %shard_map.125 = (bf16[16,4,2,128,128]{4,3,2,1,0:T(8,128)(2,1)S(1)}, s32[4,264,128]{2,1,0:T(8,128)S(1)}) custom-call(s32[5,4]{1,0:T(8,128)S(1)} %get-tuple-element.112.table, bf16[1,128]{1,0:T(2,128)(2,1)S(1)} %bitcast.100, bf16[16,4,128,128]{3,2,1,0:T(8,128)(2,1)S(1)} %bitcast.58, bf16[16,4,128,128]{3,2,1,0:T(8,128)(2,1)S(1)} %bitcast.78, ...), custom_call_target="tpu_custom_call" | custom-call | flops 1000 | bytes 1000 | tf_op jit(solution)/shard_map/pallas_call | solution.py:432
  73.9 6.0 %shard_map.126 = (bf16[16,4,2,128,128]{4,3,2,1,0:T(8,128)(2,1)S(1)}, s32[4,264,128]{2,1,0:T(8,128)S(1)}) custom-call(s32[5,4]{1,0:T(8,128)S(1)} %get-tuple-element.113.table, bf16[1,128]{1,0:T(2,128)(2,1)S(1)} %bitcast.101, bf16[16,4,128,128]{3,2,1,0:T(8,128)(2,1)S(1)} %bitcast.60, ...), custom_call_target="tpu_custom_call", output_to_operand_aliasing={{0}: (18, {})} | custom-call | flops 1000 | bytes 1000 | tf_op jit(solution)/shard_map/pallas_call | solution.py:432
  83.1 9.7 %shard_map.127 = (bf16[16,4,128,128]{3,2,1,0:T(8,128)(2,1)S(1)}, bf16[16,4,256,256]{3,2,1,0:T(8,128)(2,1)S(1)}) custom-call(bf16[16,4,128,128]{3,2,1,0:T(8,128)(2,1)S(1)} %bitcast.62, bf16[16,4,128,128]{3,2,1,0:T(8,128)(2,1)S(1)} %bitcast.82, f32[16,16,128]{2,1,0:T(8,128)S(1)} %convert_select_fusion.rate_ref.refs_3_.refs_9_), custom_call_target="tpu_custom_call" | custom-call | flops 1000 | bytes 1000 | tf_op jit(solution)/shard_map/pallas_call | solution.py:217
  92.8 10.0 %shard_map.128 = (bf16[16,4,128,128]{3,2,1,0:T(8,128)(2,1)S(1)}, bf16[16,4,256,256]{3,2,1,0:T(8,128)(2,1)S(1)}) custom-call(bf16[16,4,128,128]{3,2,1,0:T(8,128)(2,1)S(1)} %bitcast.63, bf16[16,4,128,128]{3,2,1,0:T(8,128)(2,1)S(1)} %bitcast.83, ...), custom_call_target="tpu_custom_call", output_to_operand_aliasing={{0}: (3, {}), {1}: (4, {})} | custom-call | flops 1000 | bytes 1000 | tf_op jit(solution)/shard_map/pallas_call | solution.py:217
  102.9 6.7 %shard_map.129 = (bf16[16,4,2,128,128]{4,3,2,1,0:T(8,128)(2,1)S(1)}, s32[4,264,128]{2,1,0:T(8,128)}) custom-call(s32[5,4]{1,0:T(8,128)S(1)} %get-tuple-element.111.table, bf16[1,128]{1,0:T(2,128)(2,1)S(1)} %bitcast.102, bf16[16,4,128,128]{3,2,1,0:T(8,128)(2,1)S(1)} %bitcast.64, ...), custom_call_target="tpu_custom_call", output_to_operand_aliasing={{0}: (18, {})} | custom-call | flops 1000 | bytes 1000 | tf_op jit(solution)/shard_map/pallas_call | solution.py:432
  109.5 6.8 %shard_map.130 = (bf16[16,4,2,128,128]{4,3,2,1,0:T(8,128)(2,1)S(1)}, s32[4,264,128]{2,1,0:T(8,128)}) custom-call(s32[5,4]{1,0:T(8,128)S(1)} %get-tuple-element.112.table, bf16[1,128]{1,0:T(2,128)(2,1)S(1)} %bitcast.103, bf16[16,4,128,128]{3,2,1,0:T(8,128)(2,1)S(1)} %bitcast.66, ...), custom_call_target="tpu_custom_call", output_to_operand_aliasing={{0}: (18, {})} | custom-call | flops 1000 | bytes 1000 | tf_op jit(solution)/shard_map/pallas_call | solution.py:432
  116.4 6.5 %shard_map.131 = (bf16[16,4,2,128,128]{4,3,2,1,0:T(8,128)(2,1)S(1)}, s32[4,264,128]{2,1,0:T(8,128)}) custom-call(s32[5,4]{1,0:T(8,128)S(1)} %get-tuple-element.113.table, bf16[1,128]{1,0:T(2,128)(2,1)S(1)} %bitcast.104, bf16[16,4,128,128]{3,2,1,0:T(8,128)(2,1)S(1)} %bitcast.68, ...), custom_call_target="tpu_custom_call", output_to_operand_aliasing={{0}: (18, {})} | custom-call | flops 1000 | bytes 1000 | tf_op jit(solution)/shard_map/pallas_call | solution.py:432
  122.9 2.7 %collective-permute-start.9 = (s32[4,264,128]{2,1,0:T(8,128)}, s32[4,264,128]{2,1,0:T(8,128)}, u32[]{:S(2)}, u32[]{:S(2)}) collective-permute-start(s32[4,264,128]{2,1,0:T(8,128)} %get-tuple-element.100), channel_id=1, source_target_pairs={{0,4},{4,0},{8,12},{12,8},{1,5},{5,1},{9,13},{13,9},{2,6},{6,2},{1... | collective-permute-start | bytes 1622024 | tf_op jit(solution)/shard_map/ppermute | solution.py:508
  125.6 6.3 %shard_map.132 = (bf16[16,4,2,128,128]{4,3,2,1,0:T(8,128)(2,1)S(1)}, s32[4,264,128]{2,1,0:T(8,128)}) custom-call(s32[5,4]{1,0:T(8,128)S(1)} %get-tuple-element.111.table, bf16[1,128]{1,0:T(2,128)(2,1)S(1)} %bitcast.105, bf16[16,4,128,128]{3,2,1,0:T(8,128)(2,1)S(1)} %bitcast.70, ...), custom_call_target="tpu_custom_call", output_to_operand_aliasing={{0}: (18, {})} | custom-call | flops 1000 | bytes 1000 | tf_op jit(solution)/shard_map/pallas_call | solution.py:432
  134.0 2.4 %collective-permute-start.6 = (s32[4,264,128]{2,1,0:T(8,128)}, s32[4,264,128]{2,1,0:T(8,128)}, u32[]{:S(2)}, u32[]{:S(2)}) collective-permute-start(s32[4,264,128]{2,1,0:T(8,128)} %get-tuple-element.97), channel_id=1, source_target_pairs={{0,4},{4,0},{8,12},{12,8},{1,5},{5,1},{9,13},{13,9},{2,6},{6,2},{1... | collective-permute-start | bytes 1622024 | tf_op jit(solution)/shard_map/ppermute | solution.py:508
  136.4 6.7 %shard_map.133 = (bf16[16,4,2,128,128]{4,3,2,1,0:T(8,128)(2,1)S(1)}, f32[16,8,128,128]{3,2,1,0:T(8,128)}) custom-call(s32[5,4]{1,0:T(8,128)S(1)} %get-tuple-element.114.table, bf16[1,128]{1,0:T(2,128)(2,1)S(1)} %bitcast.106, bf16[16,4,128,128]{3,2,1,0:T(8,128)(2,1)S(1)} %bitcast.72, ...), custom_call_target="tpu_custom_call", output_to_operand_aliasing={{0}: (18, {})} | custom-call | flops 1000 | bytes 1000 | tf_op jit(solution)/shard_map/pallas_call | solution.py:432
  143.1 7.0 %shard_map.134 = (bf16[16,4,2,128,128]{4,3,2,1,0:T(8,128)(2,1)S(1)}, f32[16,8,128,128]{3,2,1,0:T(8,128)}) custom-call(s32[5,4]{1,0:T(8,128)S(1)} %get-tuple-element.114.table, bf16[1,128]{1,0:T(2,128)(2,1)S(1)} %bitcast.107, bf16[16,4,128,128]{3,2,1,0:T(8,128)(2,1)S(1)} %bitcast.74, ...), custom_call_target="tpu_custom_call", output_to_operand_aliasing={{0}: (18, {}), {1}: (19, {})} | custom-call | flops 1000 | bytes 1000 | tf_op jit(solution)/shard_map/pallas_call | solution.py:432
  154.9 6.3 %copy.68 = bf16[16,128,4,2,128]{4,3,2,1,0:T(2,128)(2,1)} copy(bf16[16,128,4,2,128]{4,1,3,2,0:T(8,128)(2,1)S(1)} %bitcast.98) | data formatting | bytes 8388608
  165.3 11.9 %collective-permute-done.7.packed_ref = s32[4,264,128]{2,1,0:T(8,128)} collective-permute-done((s32[4,264,128]{2,1,0:T(8,128)}, s32[4,264,128]{2,1,0:T(8,128)}, u32[]{:S(2)}, u32[]{:S(2)}) %collective-permute-start.7) | collective-permute-done | bytes 540704 | tf_op jit(solution)/shard_map/ppermute | solution.py:508
  (83 shorter events, 35.7 us)
Async XLA Ops:
  2.8 11.5 %copy-start.18 = (s32[64]{0:T(128)S(1)}, s32[64]{0:T(128)}, u32[]{:S(2)}) copy-start(s32[64]{0:T(128)} %param.21) | copy-start | bytes 772
  2.9 11.6 %copy-start.15 = (bf16[16,128,4,2]{1,3,2,0:T(2,128)(2,1)S(1)}, bf16[16,128,4,2]{1,3,2,0:T(2,128)(2,1)}, u32[]{:S(2)}) copy-start(bf16[16,128,4,2]{1,3,2,0:T(2,128)(2,1)} %param.15) | copy-start | bytes 98308
  2.9 11.6 %copy-start.16 = (bf16[16,128,4,2]{1,3,2,0:T(2,128)(2,1)S(1)}, bf16[16,128,4,2]{1,3,2,0:T(2,128)(2,1)}, u32[]{:S(2)}) copy-start(bf16[16,128,4,2]{1,3,2,0:T(2,128)(2,1)} %param.14) | copy-start | bytes 98308
  2.9 33.4 %collective-permute-start = (s32[4,264,128]{2,1,0:T(8,128)S(1)}, s32[4,264,128]{2,1,0:T(8,128)}, u32[]{:S(2)}, u32[]{:S(2)}) collective-permute-start(s32[4,264,128]{2,1,0:T(8,128)S(1)} %get-tuple-element.69.refs_12_), channel_id=1, source_target_pairs={{0,8},{4,12},{8,0},{12,4},{1,9},{5,13},{9,1},{13,5},{2,10},{6,14},... | collective-permute-start | bytes 1622024 | tf_op jit(solution)/shard_map/ppermute | solution.py:508
  9.1 47.8 %collective-permute-start.1 = (s32[4,264,128]{2,1,0:T(8,128)S(1)}, s32[4,264,128]{2,1,0:T(8,128)}, u32[]{:S(2)}, u32[]{:S(2)}) collective-permute-start(s32[4,264,128]{2,1,0:T(8,128)S(1)} %get-tuple-element.69.refs_12_), channel_id=1, source_target_pairs={{0,4},{4,0},{8,12},{12,8},{1,5},{5,1},{9,13},{13,9},{2,6},{6,2},{1... | collective-permute-start | bytes 1622024 | tf_op jit(solution)/shard_map/ppermute | solution.py:508
  10.8 19.8 %copy-start.19 = (s32[64]{0:T(128)S(1)}, s32[64]{0:T(128)}, u32[]{:S(2)}) copy-start(s32[64]{0:T(128)} %param.19) | copy-start | bytes 772
  10.8 19.8 %copy-start.20 = (s32[64]{0:T(128)S(1)}, s32[64]{0:T(128)}, u32[]{:S(2)}) copy-start(s32[64]{0:T(128)} %param.20) | copy-start | bytes 772
  10.8 19.9 %copy-start.17 = (s32[64]{0:T(128)S(1)}, s32[64]{0:T(128)}, u32[]{:S(2)}) copy-start(s32[64]{0:T(128)} %param.18) | copy-start | bytes 772
  36.3 24.3 %collective-permute-start.2 = (s32[4,264,128]{2,1,0:T(8,128)}, s32[4,264,128]{2,1,0:T(8,128)}, u32[]{:S(2)}, u32[]{:S(2)}) collective-permute-start(s32[4,264,128]{2,1,0:T(8,128)} %collective-permute-done.refs_14_), channel_id=1, source_target_pairs={{0,4},{4,0},{8,12},{12,8},{1,5},{5,1},{9,13},{13,9},{2,6},{6,2},{1... | collective-permute-start | bytes 1622024 | tf_op jit(solution)/shard_map/ppermute | solution.py:508
  36.7 25.8 %collective-permute-start.3 = (s32[4,264,128]{2,1,0:T(8,128)S(1)}, s32[4,264,128]{2,1,0:T(8,128)}, u32[]{:S(2)}, u32[]{:S(2)}) collective-permute-start(s32[4,264,128]{2,1,0:T(8,128)S(1)} %get-tuple-element.85.refs_12_), channel_id=1, source_target_pairs={{0,8},{4,12},{8,0},{12,4},{1,9},{5,13},{9,1},{13,5},{2,10},{6,14},... | collective-permute-start | bytes 1622024 | tf_op jit(solution)/shard_map/ppermute | solution.py:508
  43.7 20.9 %copy-start = (bf16[16,128,4,2,128]{4,1,3,2,0:T(8,128)(2,1)S(1)}, bf16[16,128,4,2,128]{4,1,3,2,0:T(8,128)(2,1)}, u32[]{:S(2)}) copy-start(bf16[16,128,4,2,128]{4,1,3,2,0:T(8,128)(2,1)} %copy.76) | copy-start | bytes 12582916
  43.7 20.9 %copy-start.14 = (bf16[128]{0:T(256)(128)(2,1)S(1)}, bf16[128]{0:T(256)(128)(2,1)}, u32[]{:S(2)}) copy-start(bf16[128]{0:T(256)(128)(2,1)} %param.16) | copy-start | bytes 772
  53.5 3.4 %copy-start.5 = (bf16[16,4,256,256]{3,2,1,0:T(8,128)(2,1)}, bf16[16,4,256,256]{3,2,1,0:T(8,128)(2,1)S(1)}, u32[]{:S(2)}) copy-start(bf16[16,4,256,256]{3,2,1,0:T(8,128)(2,1)S(1)} %get-tuple-element.68.refs_5_.refs_11_) | copy-start | bytes 25165828
  62.5 40.3 %collective-permute-start.4 = (s32[4,264,128]{2,1,0:T(8,128)S(1)}, s32[4,264,128]{2,1,0:T(8,128)S(1)}, u32[]{:S(2)}, u32[]{:S(2)}) collective-permute-start(s32[4,264,128]{2,1,0:T(8,128)S(1)} %get-tuple-element.85.refs_12_), channel_id=1, source_target_pairs={{0,4},{4,0},{8,12},{12,8},{1,5},{5,1},{9,13},{13,9},{2,6},{6,2},{1... | collective-permute-start | bytes 1622024 | tf_op jit(solution)/shard_map/ppermute | solution.py:508
  62.5 40.3 %collective-permute-start.5 = (s32[4,264,128]{2,1,0:T(8,128)}, s32[4,264,128]{2,1,0:T(8,128)S(1)}, u32[]{:S(2)}, u32[]{:S(2)}) collective-permute-start(s32[4,264,128]{2,1,0:T(8,128)} %collective-permute-done.3.refs_14_), channel_id=1, source_target_pairs={{0,4},{4,0},{8,12},{12,8},{1,5},{5,1},{9,13},{13,9},{2,6},{6,2},{1... | collective-permute-start | bytes 1622024 | tf_op jit(solution)/shard_map/ppermute | solution.py:508
  73.8 60.2 %collective-permute-start.11 = (s32[4,264,128]{2,1,0:T(8,128)S(1)}, s32[4,264,128]{2,1,0:T(8,128)S(1)}, u32[]{:S(2)}, u32[]{:S(2)}) collective-permute-start(s32[4,264,128]{2,1,0:T(8,128)S(1)} %get-tuple-element.102), channel_id=1, source_target_pairs={{0,12},{4,8},{8,4},{12,0},{1,13},{5,9},{9,5},{13,1},{2,14},{6,10},... | collective-permute-start | bytes 1622024 | tf_op jit(solution)/shard_map/ppermute | solution.py:508
  81.8 70.5 %collective-permute-start.10 = (s32[4,264,128]{2,1,0:T(8,128)S(1)}, s32[4,264,128]{2,1,0:T(8,128)S(1)}, u32[]{:S(2)}, u32[]{:S(2)}) collective-permute-start(s32[4,264,128]{2,1,0:T(8,128)S(1)} %get-tuple-element.101), channel_id=1, source_target_pairs={{0,8},{4,12},{8,0},{12,4},{1,9},{5,13},{9,1},{13,5},{2,10},{6,14},... | collective-permute-start | bytes 1622024 | tf_op jit(solution)/shard_map/ppermute | solution.py:508
  83.1 19.7 %slice-start = ((s8[8388608]{0:T(1024)(128)(4,1)}), s8[4194304]{0:T(1024)(128)(4,1)S(1)}, s32[]{:S(2)}) async-start(s8[8388608]{0:T(1024)(128)(4,1)} %bitcast.96), calls=%async_computation | async-start | bytes 8388608
  92.8 10.0 %slice-start.1 = ((s8[8388608]{0:T(1024)(128)(4,1)}), s8[4194304]{0:T(1024)(128)(4,1)S(1)}, s32[]{:S(2)}) async-start(s8[8388608]{0:T(1024)(128)(4,1)} %bitcast.96), calls=%async_computation.1 | async-start | bytes 8388608
  92.8 10.0 %copy-start.8 = (bf16[16,4,2,128,128]{4,3,2,1,0:T(8,128)(2,1)S(1)}, bf16[16,4,2,128,128]{4,3,2,1,0:T(8,128)(2,1)}, u32[]{:S(2)}) copy-start(bf16[16,4,2,128,128]{4,3,2,1,0:T(8,128)(2,1)} %copy-done.7) | copy-start | bytes 12582916
  122.9 38.4 %collective-permute-start.9 = (s32[4,264,128]{2,1,0:T(8,128)}, s32[4,264,128]{2,1,0:T(8,128)}, u32[]{:S(2)}, u32[]{:S(2)}) collective-permute-start(s32[4,264,128]{2,1,0:T(8,128)} %get-tuple-element.100), channel_id=1, source_target_pairs={{0,4},{4,0},{8,12},{12,8},{1,5},{5,1},{9,13},{13,9},{2,6},{6,2},{1... | collective-permute-start | bytes 1622024 | tf_op jit(solution)/shard_map/ppermute | solution.py:508
  131.9 31.4 %collective-permute-start.8 = (s32[4,264,128]{2,1,0:T(8,128)}, s32[4,264,128]{2,1,0:T(8,128)}, u32[]{:S(2)}, u32[]{:S(2)}) collective-permute-start(s32[4,264,128]{2,1,0:T(8,128)} %get-tuple-element.99), channel_id=1, source_target_pairs={{0,12},{4,8},{8,4},{12,0},{1,13},{5,9},{9,5},{13,1},{2,14},{6,10},... | collective-permute-start | bytes 1622024 | tf_op jit(solution)/shard_map/ppermute | solution.py:508
  132.6 44.6 %collective-permute-start.7 = (s32[4,264,128]{2,1,0:T(8,128)}, s32[4,264,128]{2,1,0:T(8,128)}, u32[]{:S(2)}, u32[]{:S(2)}) collective-permute-start(s32[4,264,128]{2,1,0:T(8,128)} %get-tuple-element.98), channel_id=1, source_target_pairs={{0,8},{4,12},{8,0},{12,4},{1,9},{5,13},{9,1},{13,5},{2,10},{6,14},... | collective-permute-start | bytes 1622024 | tf_op jit(solution)/shard_map/ppermute | solution.py:508
  134.0 45.2 %collective-permute-start.6 = (s32[4,264,128]{2,1,0:T(8,128)}, s32[4,264,128]{2,1,0:T(8,128)}, u32[]{:S(2)}, u32[]{:S(2)}) collective-permute-start(s32[4,264,128]{2,1,0:T(8,128)} %get-tuple-element.97), channel_id=1, source_target_pairs={{0,4},{4,0},{8,12},{12,8},{1,5},{5,1},{9,13},{13,9},{2,6},{6,2},{1... | collective-permute-start | bytes 1622024 | tf_op jit(solution)/shard_map/ppermute | solution.py:508
  (11 other events, 24.8 us)

commit v2 on v1

--- a/solution.py
+++ b/solution.py
@@ -1,4 +1,5 @@
 import functools
+from typing import NamedTuple
 
 import jax
 import jax.numpy as jnp
@@ -15,7 +16,7 @@
 TOP = 32512.0
 BIAS = 32768.0
 CODE = 64.0
-VMEM_LIMIT = 12 * 1024 * 1024
+VMEM_LIMIT = 8 * 1024 * 1024
 PARTS = 2
 CODE_ROWS = 8
 TOGETHER = 2
@@ -78,6 +79,40 @@
 def load_steps(ref, heads):
     codes = ref[0, heads * HALF:heads * HALF + CODE_ROWS, :].astype(F32)
     return step_of(codes)
+
+
+class Plan(NamedTuple):
+    group: int
+    per_device: int
+    per_peer: int
+
+    @staticmethod
+    def build(order, owner, slot, tokens, me):
+        return jnp.concatenate([order, owner, slot, tokens, me.reshape(1)]).astype(jnp.int32)
+
+    def me(self, flat):
+        return flat[4 * self.group]
+
+    def peer(self, flat, away):
+        return jnp.bitwise_xor(self.me(flat), away)
+
+    def number(self, flat, away, i):
+        return flat[self.peer(flat, away) * self.per_device + self.me(flat) * self.per_peer + i]
+
+    def local(self, flat, away, i):
+        return self.number(flat, away, i) - self.me(flat) * self.per_device
+
+    def shard(self, flat, away, i):
+        return jnp.bitwise_xor(flat[self.group + self.number(flat, away, i)], self.me(flat))
+
+    def row(self, flat, away, i):
+        return flat[2 * self.group + self.number(flat, away, i)]
+
+    def tokens(self, flat, away, i):
+        return flat[3 * self.group + self.number(flat, away, i)]
+
+    def tokens_here(self, flat, e):
+        return flat[3 * self.group + self.me(flat) * self.per_device + e]
 
 
 def pack_kernel(state_ref, *out_refs):
@@ -103,7 +138,11 @@
     return jnp.where(mask, jnp.concatenate([x, x], axis=0), jnp.zeros((), x.dtype))
 
 
-def pair_kernel(part, q_ref, k_ref, rate_ref, *refs):
+def live_rates(rates, tokens):
+    return jnp.where(iota(rates.shape, 1) < tokens, rates, 0.0).astype(BF16)
+
+
+def pair_kernel(part, first, plan, flat, q_ref, k_ref, rate_ref, *refs):
     inv_ref, am_ref = refs[-2:]
     expansions, key_heads = q_ref.shape[:2]
     heads = 2 * key_heads
@@ -130,7 +169,8 @@
 
     a_full, where_at = [], []
     for e in range(expansions):
-        rates = rate_ref[e].astype(BF16)
+        number = (first + pl.program_id(0)) * expansions + e
+        rates = live_rates(rate_ref[e], plan.tokens_here(flat, number))
         cols = dot_nt(jnp.concatenate([lower_ones, unit], axis=0), rates)
         g_cols = cols[:LEN]
         b_cols = cols[LEN:]
@@ -195,33 +235,36 @@
         inv_ref[e, h, HALF:, :] = jnp.where(left, -corner[c], x[c]).astype(BF16)
 
 
-def pair_parts(part, half, q, k, rates, earlier=None):
+def pair_parts(part, half, plan, flat, q, k, rates, earlier=None):
     count, all_key_heads = q.shape[:2]
     key_heads = all_key_heads // PARTS
     heads = 2 * key_heads
     block = TOGETHER
     turns = count // block // 2
     first = half * turns
-    head_block = pl.BlockSpec((block, key_heads, LEN, LEN), lambda i: (first + i, part, 0, 0))
+    head_block = pl.BlockSpec((block, key_heads, LEN, LEN), lambda i, t: (first + i, part, 0, 0))
     in_specs = [
         head_block,
         head_block,
-        pl.BlockSpec((block,) + rates.shape[1:], lambda i: (first + i, 0, 0)),
+        pl.BlockSpec((block,) + rates.shape[1:], lambda i, t: (first + i, 0, 0)),
     ]
     operands = [q, k, rates]
     aliases = {}
     if earlier is not None:
         in_specs += [pl.BlockSpec(memory_space=pl.ANY)] * 2
-        aliases = {3: 0, 4: 1}
+        aliases = {4: 0, 5: 1}
         operands += list(earlier)
     return pl.pallas_call(
-        functools.partial(pair_kernel, part),
-        grid=(turns,),
-        in_specs=in_specs,
-        out_specs=[
-            pl.BlockSpec((block, heads, LEN, LEN), lambda i: (first + i, 0, 0, 0)),
-            pl.BlockSpec((block, heads, 2 * LEN, 2 * LEN), lambda i: (first + i, 0, 0, 0)),
-        ],
+        functools.partial(pair_kernel, part, first, plan),
+        grid_spec=pltpu.PrefetchScalarGridSpec(
+            num_scalar_prefetch=1,
+            grid=(turns,),
+            in_specs=in_specs,
+            out_specs=[
+                pl.BlockSpec((block, heads, LEN, LEN), lambda i, t: (first + i, 0, 0, 0)),
+                pl.BlockSpec((block, heads, 2 * LEN, 2 * LEN), lambda i, t: (first + i, 0, 0, 0)),
+            ],
+        ),
         out_shape=[
             jax.ShapeDtypeStruct((count, heads, LEN, LEN), BF16),
             jax.ShapeDtypeStruct((count, heads, 2 * LEN, 2 * LEN), BF16),
@@ -229,10 +272,10 @@
         input_output_aliases=aliases,
         compiler_params=pltpu.CompilerParams(vmem_limit_bytes=VMEM_LIMIT),
         cost_estimate=pl.CostEstimate(flops=1000, bytes_accessed=1000, transcendentals=0),
-    )(*operands)
-
-
-def state_kernel(part, home, shards_held, together, table, gain_ref, *refs):
+    )(flat, *operands)
+
+
+def state_kernel(part, away, plan, shards_held, together, flat, gain_ref, *refs):
     per = 6
     inputs = [refs[per * e:per * (e + 1)] for e in range(together)]
     parents = refs[per * together:per * together + shards_held]
@@ -244,11 +287,12 @@
 
     def fetch(i, slot):
         for e in range(together):
+            shard = plan.shard(flat, away, i * together + e)
             for off in range(shards_held):
-                @pl.when(table[1, i * together + e] == off)
+                @pl.when(shard == off)
                 def _():
                     pltpu.make_async_copy(
-                        parents[off].at[table[4, i * together + e]],
+                        parents[off].at[plan.row(flat, away, i * together + e)],
                         states_in.at[slot, e],
                         arrivals.at[slot, e],
                     ).start()
@@ -256,7 +300,7 @@
     def leave(i, slot, e):
         return pltpu.make_async_copy(
             mixed_out.at[slot, e],
-            mixed_hbm.at[table[0, i * together + e], pl.ds(part * key_heads, key_heads)],
+            mixed_hbm.at[plan.local(flat, away, i * together + e), pl.ds(part * key_heads, key_heads)],
             leaving.at[slot, e],
         )
 
@@ -287,7 +331,8 @@
     state, products, n_cols, g_cols, b_cols, eg_cols, steps = [], [], [], [], [], [], []
     for e in range(together):
         q_ref, k_ref, v_ref, rate_ref, inv_ref, am_ref = inputs[e]
-        cols = dot_nt(jnp.concatenate([lower_ones, unit], axis=0), rate_ref[0].astype(BF16))
+        rates = live_rates(rate_ref[0], plan.tokens(flat, away, turn * together + e))
+        cols = dot_nt(jnp.concatenate([lower_ones, unit], axis=0), rates)
         g_cols.append(cols[:LEN])
         b_cols.append(cols[LEN:])
         eg_cols.append(jnp.exp(cols[:LEN]))
@@ -361,14 +406,14 @@
         out = decay_at(e, h) * qs + am_v[c][LEN:]
         out = out + dot(inputs[e][5][0, h, LEN:, :LEN], delta[c].astype(BF16))
         mean_square = jnp.mean(out * out, axis=1, keepdims=True)
-        live = iota((LEN, 1), 0) < table[2, turn * together + e]
+        live = iota((LEN, 1), 0) < plan.tokens(flat, away, turn * together + e)
         scale = jnp.where(live, lax.rsqrt(mean_square + EPS), 0.0)
         mixed_out[slot, e, h // 2, h % 2] = (out * scale * gain).astype(BF16)
     for e in range(together):
         leave(turn, slot, e).start()
     for e in range(together):
         mine = finals[e * heads:(e + 1) * heads]
-        if home:
+        if away == 0:
             for h in range(heads):
                 state_ref[e, h] = mine[h]
         else:
@@ -385,9 +430,10 @@
             leave(turn - 1, 1 - slot, e).wait()
 
 
-def recurrence(part, table, q, k, v, rates, pairs, parents, gain, mixed, final_shape=None, final=None):
-    count = table.shape[1]
+def recurrence(part, away, plan, flat, q, k, v, rates, pairs, parents, gain, mixed, final_shape=None, final=None):
+    count = plan.per_peer
     together = min(TOGETHER, count)
+    turns = count // together
     key_heads = q.shape[1] // PARTS
     heads = 2 * key_heads
     rows = heads * HALF + CODE_ROWS
@@ -396,7 +442,7 @@
 
     def one(shape, e, at):
         def index(i, t):
-            return (t[0, i * together + e], at) + (0,) * (len(shape) - 2)
+            return (plan.local(t, away, i * together + e), at) + (0,) * (len(shape) - 2)
 
         return pl.BlockSpec(shape, index)
 
@@ -427,13 +473,13 @@
             in_specs.append(pl.BlockSpec(memory_space=pl.ANY))
             aliases[1 + len(operands)] = 1
             operands.append(final)
-        state_spec = pl.BlockSpec((together, heads, LEN, LEN), lambda i, t: (t[3, i], part, 0, 0))
+        state_spec = pl.BlockSpec((together, heads, LEN, LEN), lambda i, t: (plan.me(t) * turns + i, part, 0, 0))
         state_shape = jax.ShapeDtypeStruct(final_shape, F32)
     return pl.pallas_call(
-        functools.partial(state_kernel, part, final_shape is not None, len(parents), together),
+        functools.partial(state_kernel, part, away, plan, len(parents), together),
         grid_spec=pltpu.PrefetchScalarGridSpec(
             num_scalar_prefetch=1,
-            grid=(count // together,),
+            grid=(turns,),
             in_specs=in_specs,
             out_specs=[mixed_spec, state_spec],
             scratch_shapes=[
@@ -447,10 +493,10 @@
         input_output_aliases=aliases,
         compiler_params=pltpu.CompilerParams(vmem_limit_bytes=VMEM_LIMIT),
         cost_estimate=pl.CostEstimate(flops=1000, bytes_accessed=1000, transcendentals=0),
-    )(table, *operands)
-
-
-def unpack_kernel(table, packed_ref, old_ref, out_ref):
+    )(flat, *operands)
+
+
+def unpack_kernel(flat, packed_ref, old_ref, out_ref):
     count, heads = out_ref.shape[:2]
     for e in range(count):
         steps = load_steps(packed_ref.at[pl.ds(e, 1)], heads)
@@ -458,7 +504,7 @@
             out_ref[e, h] = decode(packed_ref[e, h * HALF:(h + 1) * HALF, :]) * steps[h:h + 1, :]
 
 
-def unpack_states(part, table, packed, final):
+def unpack_states(part, away, plan, flat, packed, final):
     count, rows = packed.shape[:2]
     heads = final.shape[1] // PARTS
     block = max(1, count // 2)
@@ -472,13 +518,13 @@
                 pl.BlockSpec((block, rows, LEN), lambda i, t: (i, 0, 0)),
                 pl.BlockSpec(memory_space=pl.ANY),
             ],
-            out_specs=pl.BlockSpec((block, heads, LEN, LEN), lambda i, t: (t[0] * turns + i, part, 0, 0)),
+            out_specs=pl.BlockSpec((block, heads, LEN, LEN), lambda i, t: (plan.peer(t, away) * turns + i, part, 0, 0)),
         ),
         out_shape=jax.ShapeDtypeStruct(final.shape, F32),
         input_output_aliases={2: 0},
         compiler_params=pltpu.CompilerParams(vmem_limit_bytes=VMEM_LIMIT),
         cost_estimate=pl.CostEstimate(flops=1000, bytes_accessed=1000, transcendentals=0),
-    )(table, packed, final)
+    )(flat, packed, final)
 
 
 def shards(
@@ -522,68 +568,45 @@
     def rows_of(tensor):
         return jnp.transpose(tensor, (0, 2, 3, 1)).reshape(per_device, heads, length).astype(F32)
 
-    here_count = lax.dynamic_slice_in_dim(token_count, me * per_device, per_device)
-    alive = jnp.arange(length, dtype=jnp.int32) < here_count[:, None, None]
-    rates = jnp.where(alive, jnp.concatenate([rows_of(log_decay), rows_of(write_rate)], axis=1), 0.0)
+    rates = jnp.concatenate([rows_of(log_decay), rows_of(write_rate)], axis=1)
     gain = norm_gain.reshape(1, -1)
-    pairs = [None, None]
+    plan = Plan(order.shape[0], per_device, per_peer)
+    flat = Plan.build(order, parent_owner, parent_slot, token_count, me)
+
     own[0], q = lax.optimization_barrier((own[0], q))
-    pairs[0] = pair_parts(0, 0, q, k, rates)
-    pairs[0], v, far, own[1] = lax.optimization_barrier((pairs[0], v, far, own[1]))
+    q, k, v, rates, gain, flat = lax.optimization_barrier((q, k, v, rates, gain, flat))
+
+    pairs = [pair_parts(0, 0, plan, flat, q, k, rates), None]
+    pairs[0], far, own[1] = lax.optimization_barrier((pairs[0], far, own[1]))
     held_0 = spread({0: own[0], half_way: far}, half_way // 2)
     far_1 = swap(own[1], half_way)
-    pairs[0] = pair_parts(0, 1, q, k, rates, pairs[0])
-    pairs[0], held_0, far_1, own, v = lax.optimization_barrier((pairs[0], held_0, far_1, own, v))
+    pairs[0] = pair_parts(0, 1, plan, flat, q, k, rates, pairs[0])
+    rates, pairs[0] = lax.optimization_barrier((rates, pairs[0]))
+    pairs[1] = pair_parts(1, 0, plan, flat, q, k, rates)
+    pairs, held_0, far_1, own = lax.optimization_barrier((pairs, held_0, far_1, own))
     held_1 = spread({0: own[1], half_way: far_1}, half_way // 2)
     gathered = [[held[at] for at in range(seq_count)] for held in (held_0, held_1)]
 
-    slot_grid = order.reshape(seq_count, seq_count, per_peer)
-    local_ids = lax.dynamic_index_in_dim(slot_grid, me, 1, keepdims=False) - me * per_device
-    here_owner = lax.dynamic_slice_in_dim(parent_owner, me * per_device, per_device)
-    here_slot = lax.dynamic_slice_in_dim(parent_slot, me * per_device, per_device)
-
-    def look_up(vector, ids):
-        hit = ids[..., None] == jnp.arange(per_device, dtype=jnp.int32)
-        return jnp.sum(jnp.where(hit, vector, 0), axis=-1)
-
-    block = me * (per_peer // min(TOGETHER, per_peer))
-    slots = block + jnp.broadcast_to(jnp.arange(per_peer, dtype=jnp.int32), local_ids.shape)
-    tables = jnp.stack(
-        [
-            local_ids,
-            jnp.bitwise_xor(look_up(here_owner, local_ids), me),
-            look_up(here_count, local_ids),
-            slots,
-            look_up(here_slot, local_ids),
-        ],
-        axis=1,
-    ).astype(jnp.int32)
-
     final_shape = (per_device, heads, key_dim, key_dim)
-    mixed, final = None, None
-    arrived = []
     crossing = list(reversed(range(half_way, seq_count)))
     near = list(reversed(range(1, half_way)))
-    turns = [(part, away) for part in range(PARTS) for away in crossing + near]
+    turns = [(part, away) for part in range(PARTS) for away in crossing]
+    turns += [(part, away) for part in range(PARTS) for away in near]
     turns += [(part, 0) for part in range(PARTS)]
+    mixed, final = None, None
+    arrived = {}
     for part, away in turns:
-        peer = jnp.bitwise_xor(me, away)
-        table = lax.dynamic_index_in_dim(tables, peer, 0, keepdims=False)
-        if part == 0 and away == near[0]:
-            rates, mixed = lax.optimization_barrier((rates, mixed))
-            pairs[1] = pair_parts(1, 0, q, k, rates)
-            pairs[1] = pair_parts(1, 1, q, k, rates, pairs[1])
-            mixed, pairs[1], gathered[1] = lax.optimization_barrier((mixed, pairs[1], gathered[1]))
-        common = (part, table, q, k, v, rates, pairs[part], gathered[part], gain, mixed)
+        if part == 1 and away == crossing[0]:
+            rates, mixed, pairs[1] = lax.optimization_barrier((rates, mixed, pairs[1]))
+            pairs[1] = pair_parts(1, 1, plan, flat, q, k, rates, pairs[1])
+        common = (part, away, plan, flat, q, k, v, rates, pairs[part], gathered[part], gain, mixed)
         if away:
             mixed, packed = recurrence(*common)
-            sent = swap(packed, away)
-            arrived.append((part, peer, sent))
+            arrived[part, away] = swap(packed, away)
         else:
             mixed, final = recurrence(*common, final_shape, final)
-    for part, peer, packed in arrived:
-        table = peer.reshape(1)
-        final = unpack_states(part, table, packed, final)
+    for part, away in [(0, away) for away in crossing + near] + [(1, away) for away in near + crossing]:
+        final = unpack_states(part, away, plan, flat, arrived[part, away], final)
     mixed_out = jnp.transpose(mixed, (0, 3, 1, 2, 4))
     final_out = final.reshape((per_device, key_heads, 2, key_dim, key_dim))
     return (mixed_out, final_out)

time: 182 us -> 178 us (0.978)
  local copies, waits for them, and re-layouts: 43.8 us -> 19.8 us
  waiting for transfers between devices: 17.6 us -> 29.6 us
  Pallas kernels: 102 us -> 107 us
  starting transfers between devices: 16.8 us -> 19.5 us
    unnamed x50 -> x30, local copies, waits for them, and re-layouts: 43.4 us -> 19.7 us
    ppermute x12, waiting for transfers between devices: 17.6 us -> 29.6 us  [swap(): return lax.ppermute(tensor, 'seq', [(i, i ^ off) for i in range(seq_count)])]
    pallas_call x6, Pallas kernels: 10.2 us -> 14 us  [unpack_states(): pl.pallas_call(unpack_kernel, grid_spec=pltpu.PrefetchScalarGridSpec(num_...]
    ppermute x12, starting transfers between devices: 16.8 us -> 19.5 us  [swap(): return lax.ppermute(tensor, 'seq', [(i, i ^ off) for i in range(seq_count)])]
    pallas_call x12, Pallas kernels: 90.8 us -> 92.7 us  [the longest x8 51.2 us: recurrence(): pl.pallas_call(functools.partial(state_kernel, part, away, plan, len(pare...]
  transfers between devices with their start and end apart: 12 -> 12, of which waited for: 3 -> 5; matrix products, arithmetic and copies ran while one was open for 10% -> 9% of each run, Pallas kernels for 55% -> 59%
where the time goes in v2:
time: 178 us; the launch traced here: 177 us
  Pallas kernels  107 us (60%)
  waiting for transfers between devices  29.6 us (17%)
  local copies, waits for them, and re-layouts  19.8 us (11%)
  starting transfers between devices  19.5 us (11%)
    pallas_call x8, Pallas kernels, recurrence(): pl.pallas_call(functools.partial(state_kernel, part, away, plan, len(pare...  51.2 us
    pallas_call x4, Pallas kernels, pair_parts(): pl.pallas_call(functools.partial(pair_kernel, part, first, plan), grid_sp...  41.5 us
    ppermute x12, waiting for transfers between devices, swap(): return lax.ppermute(tensor, 'seq', [(i, i ^ off) for i in range(seq_count)])  29.6 us
    unnamed x30, local copies, waits for them, and re-layouts  19.7 us
    ppermute x12, starting transfers between devices, swap(): return lax.ppermute(tensor, 'seq', [(i, i ^ off) for i in range(seq_count)])  19.5 us
    pallas_call x6, Pallas kernels, unpack_states(): pl.pallas_call(unpack_kernel, grid_spec=pltpu.PrefetchScalarGridSpec(num_...  14 us
  transfers between devices with their start and end apart: 12, of which 5 were waited for; matrix products, arithmetic and copies ran while one was open for 9% of the time, Pallas kernels for 59%

profile of v2, /device:TPU:0, one launch (start us, length us, event | category | flops | bytes accessed | tf_op | source)
XLA Modules:
  0.0 177.2 jit_solution(8033343222871180914)
XLA Ops:
  2.8 4.1 %collective-permute-start = (s32[4,264,128]{2,1,0:T(8,128)S(1)}, s32[4,264,128]{2,1,0:T(8,128)}, u32[]{:S(2)}, u32[]{:S(2)}) collective-permute-start(s32[4,264,128]{2,1,0:T(8,128)S(1)} %get-tuple-element.82.refs_12_), channel_id=1, source_target_pairs={{0,8},{4,12},{8,0},{12,4},{1,9},{5,13},{9,1},{13,5},{2,10},{6,14},... | collective-permute-start | bytes 1622024 | tf_op jit(solution)/shard_map/ppermute | solution.py:554
  10.7 3.6 %copy.39 = bf16[16,128,4,128]{3,1,2,0:T(8,128)(2,1)} copy(bf16[16,128,4,128]{3,2,1,0:T(4,128)(2,1)} %param.12) | data formatting | bytes 4194304 | tf_op args[1]
  14.4 3.3 %copy.38 = bf16[16,128,4,2,128]{4,1,3,2,0:T(8,128)(2,1)} copy(bf16[16,128,4,2,128]{4,3,2,1,0:T(2,128)(2,1)S(1)} %copy-done.6) | data formatting | bytes 8388608 | tf_op args[2]
  19.4 10.3 %shard_map.123 = (bf16[16,4,128,128]{3,2,1,0:T(8,128)(2,1)S(1)}, bf16[16,4,256,256]{3,2,1,0:T(8,128)(2,1)S(1)}) custom-call(s32[257]{0:T(512)S(1)} %concatenate.11.flat, bf16[16,4,128,128]{3,2,1,0:T(8,128)(2,1)S(1)} %bitcast.36, bf16[16,4,128,128]{3,2,1,0:T(8,128)(2,1)S(1)} %bitcast.56, f32[16,16,128]{2,1,0:T(8,128)S(1)} %maximum_convert_fusion.rate_ref.refs_3_.refs_9_), custom_call_target="tpu_custom_call" | custom-call | flops 1000 | bytes 1000 | tf_op jit(solution)/shard_map/pallas_call | solution.py:257
  31.6 3.5 %collective-permute-start.3 = (s32[4,264,128]{2,1,0:T(8,128)S(1)}, s32[4,264,128]{2,1,0:T(8,128)S(1)}, u32[]{:S(2)}, u32[]{:S(2)}) collective-permute-start(s32[4,264,128]{2,1,0:T(8,128)S(1)} %get-tuple-element.95.refs_12_), channel_id=1, source_target_pairs={{0,8},{4,12},{8,0},{12,4},{1,9},{5,13},{9,1},{13,5},{2,10},{6,14},... | collective-permute-start | bytes 1622024 | tf_op jit(solution)/shard_map/ppermute | solution.py:554
  35.1 10.3 %shard_map.124 = (bf16[16,4,128,128]{3,2,1,0:T(8,128)(2,1)S(1)}, bf16[16,4,256,256]{3,2,1,0:T(8,128)(2,1)S(1)}) custom-call(s32[257]{0:T(512)S(1)} %concatenate.11.flat, bf16[16,4,128,128]{3,2,1,0:T(8,128)(2,1)S(1)} %bitcast.37, bf16[16,4,128,128]{3,2,1,0:T(8,128)(2,1)S(1)} %bitcast.57, ...), custom_call_target="tpu_custom_call", output_to_operand_aliasing={{0}: (4, {}), {1}: (5, {})} | custom-call | flops 1000 | bytes 1000 | tf_op jit(solution)/shard_map/pallas_call | solution.py:257
  45.5 10.3 %shard_map.125 = (bf16[16,4,128,128]{3,2,1,0:T(8,128)(2,1)S(1)}, bf16[16,4,256,256]{3,2,1,0:T(8,128)(2,1)S(1)}) custom-call(s32[257]{0:T(512)S(1)} %concatenate.11.flat, bf16[16,4,128,128]{3,2,1,0:T(8,128)(2,1)S(1)} %bitcast.38, bf16[16,4,128,128]{3,2,1,0:T(8,128)(2,1)S(1)} %bitcast.58, f32[16,16,128]{2,1,0:T(8,128)S(1)} %maximum_convert_fusion.rate_ref.refs_3_.refs_9_), custom_call_target="tpu_custom_call" | custom-call | flops 1000 | bytes 1000 | tf_op jit(solution)/shard_map/pallas_call | solution.py:257
  60.9 6.1 %shard_map.126 = (bf16[16,4,2,128,128]{4,3,2,1,0:T(8,128)(2,1)S(1)}, s32[4,264,128]{2,1,0:T(8,128)S(1)}) custom-call(s32[257]{0:T(512)S(1)} %concatenate.11.flat, bf16[1,128]{1,0:T(2,128)(2,1)S(1)} %bitcast.78, bf16[16,4,128,128]{3,2,1,0:T(8,128)(2,1)S(1)} %bitcast.39, bf16[16,4,128,128]{3,2,1,0:T(8,128)(2,1)S(1)} %bitcast.59, ...), custom_call_target="tpu_custom_call" | custom-call | flops 1000 | bytes 1000 | tf_op jit(solution)/shard_map/pallas_call | solution.py:478
  69.1 5.8 %shard_map.127 = (bf16[16,4,2,128,128]{4,3,2,1,0:T(8,128)(2,1)S(1)}, s32[4,264,128]{2,1,0:T(8,128)S(1)}) custom-call(s32[257]{0:T(512)S(1)} %concatenate.11.flat, bf16[1,128]{1,0:T(2,128)(2,1)S(1)} %bitcast.79, bf16[16,4,128,128]{3,2,1,0:T(8,128)(2,1)S(1)} %bitcast.41, bf16[16,4,128,128]{3,2,1,0:T(8,128)(2,1)S(1)} %bitcast.61, ...), custom_call_target="tpu_custom_call", output_to_operand_aliasing={{0}: (18, {})} | custom-call | flops 1000 | bytes 1000 | tf_op jit(solution)/shard_map/pallas_call | solution.py:478
  75.0 10.5 %shard_map.128 = (bf16[16,4,128,128]{3,2,1,0:T(8,128)(2,1)S(1)}, bf16[16,4,256,256]{3,2,1,0:T(8,128)(2,1)S(1)}) custom-call(s32[257]{0:T(512)S(1)} %concatenate.11.flat, bf16[16,4,128,128]{3,2,1,0:T(8,128)(2,1)S(1)} %bitcast.43, bf16[16,4,128,128]{3,2,1,0:T(8,128)(2,1)S(1)} %bitcast.63, ...), custom_call_target="tpu_custom_call", output_to_operand_aliasing={{0}: (4, {}), {1}: (5, {})} | custom-call | flops 1000 | bytes 1000 | tf_op jit(solution)/shard_map/pallas_call | solution.py:257
  85.6 13.3 %collective-permute-done.5.refs_15_ = s32[4,264,128]{2,1,0:T(8,128)S(1)} collective-permute-done((s32[4,264,128]{2,1,0:T(8,128)S(1)}, s32[4,264,128]{2,1,0:T(8,128)S(1)}, u32[]{:S(2)}, u32[]{:S(2)}) %collective-permute-start.5) | collective-permute-done | bytes 540704 | tf_op jit(solution)/shard_map/ppermute | solution.py:554
  98.9 6.5 %shard_map.129 = (bf16[16,4,2,128,128]{4,3,2,1,0:T(8,128)(2,1)S(1)}, s32[4,264,128]{2,1,0:T(8,128)}) custom-call(s32[257]{0:T(512)S(1)} %concatenate.11.flat, bf16[1,128]{1,0:T(2,128)(2,1)S(1)} %bitcast.80, bf16[16,4,128,128]{3,2,1,0:T(8,128)(2,1)S(1)} %bitcast.44, bf16[16,4,128,128]{3,2,1,0:T(8,128)(2,1)S(1)} %bitcast.64, ...), custom_call_target="tpu_custom_call", output_to_operand_aliasing={{0}: (18, {})} | custom-call | flops 1000 | bytes 1000 | tf_op jit(solution)/shard_map/pallas_call | solution.py:478
  105.4 6.5 %shard_map.130 = (bf16[16,4,2,128,128]{4,3,2,1,0:T(8,128)(2,1)S(1)}, s32[4,264,128]{2,1,0:T(8,128)}) custom-call(s32[257]{0:T(512)S(1)} %concatenate.11.flat, bf16[1,128]{1,0:T(2,128)(2,1)S(1)} %bitcast.81, bf16[16,4,128,128]{3,2,1,0:T(8,128)(2,1)S(1)} %bitcast.46, bf16[16,4,128,128]{3,2,1,0:T(8,128)(2,1)S(1)} %bitcast.66, ...), custom_call_target="tpu_custom_call", output_to_operand_aliasing={{0}: (18, {})} | custom-call | flops 1000 | bytes 1000 | tf_op jit(solution)/shard_map/pallas_call | solution.py:478
  111.9 6.6 %shard_map.131 = (bf16[16,4,2,128,128]{4,3,2,1,0:T(8,128)(2,1)S(1)}, s32[4,264,128]{2,1,0:T(8,128)}) custom-call(s32[257]{0:T(512)S(1)} %concatenate.11.flat, bf16[1,128]{1,0:T(2,128)(2,1)S(1)} %bitcast.82, bf16[16,4,128,128]{3,2,1,0:T(8,128)(2,1)S(1)} %bitcast.48, bf16[16,4,128,128]{3,2,1,0:T(8,128)(2,1)S(1)} %bitcast.68, ...), custom_call_target="tpu_custom_call", output_to_operand_aliasing={{0}: (18, {})} | custom-call | flops 1000 | bytes 1000 | tf_op jit(solution)/shard_map/pallas_call | solution.py:478
  118.6 6.5 %shard_map.132 = (bf16[16,4,2,128,128]{4,3,2,1,0:T(8,128)(2,1)S(1)}, s32[4,264,128]{2,1,0:T(8,128)}) custom-call(s32[257]{0:T(512)S(1)} %concatenate.11.flat, bf16[1,128]{1,0:T(2,128)(2,1)S(1)} %bitcast.83, bf16[16,4,128,128]{3,2,1,0:T(8,128)(2,1)S(1)} %bitcast.50, bf16[16,4,128,128]{3,2,1,0:T(8,128)(2,1)S(1)} %bitcast.70, ...), custom_call_target="tpu_custom_call", output_to_operand_aliasing={{0}: (18, {})} | custom-call | flops 1000 | bytes 1000 | tf_op jit(solution)/shard_map/pallas_call | solution.py:478
  127.2 3.3 %collective-permute-start.7 = (s32[4,264,128]{2,1,0:T(8,128)}, s32[4,264,128]{2,1,0:T(8,128)}, u32[]{:S(2)}, u32[]{:S(2)}) collective-permute-start(s32[4,264,128]{2,1,0:T(8,128)} %get-tuple-element.106), channel_id=1, source_target_pairs={{0,12},{4,8},{8,4},{12,0},{1,13},{5,9},{9,5},{13,1},{2,14},{6,10},... | collective-permute-start | bytes 1622024 | tf_op jit(solution)/shard_map/ppermute | solution.py:554
  130.5 6.4 %shard_map.133 = (bf16[16,4,2,128,128]{4,3,2,1,0:T(8,128)(2,1)S(1)}, f32[16,8,128,128]{3,2,1,0:T(8,128)}) custom-call(s32[257]{0:T(512)S(1)} %concatenate.11.flat, bf16[1,128]{1,0:T(2,128)(2,1)S(1)} %bitcast.84, bf16[16,4,128,128]{3,2,1,0:T(8,128)(2,1)S(1)} %bitcast.52, bf16[16,4,128,128]{3,2,1,0:T(8,128)(2,1)S(1)} %bitcast.72, ...), custom_call_target="tpu_custom_call", output_to_operand_aliasing={{0}: (18, {})} | custom-call | flops 1000 | bytes 1000 | tf_op jit(solution)/shard_map/pallas_call | solution.py:478
  137.0 6.7 %shard_map.134 = (bf16[16,4,2,128,128]{4,3,2,1,0:T(8,128)(2,1)S(1)}, f32[16,8,128,128]{3,2,1,0:T(8,128)}) custom-call(s32[257]{0:T(512)S(1)} %concatenate.11.flat, bf16[1,128]{1,0:T(2,128)(2,1)S(1)} %bitcast.85, bf16[16,4,128,128]{3,2,1,0:T(8,128)(2,1)S(1)} %bitcast.54, ...), custom_call_target="tpu_custom_call", output_to_operand_aliasing={{0}: (18, {}), {1}: (19, {})} | custom-call | flops 1000 | bytes 1000 | tf_op jit(solution)/shard_map/pallas_call | solution.py:478
  148.6 6.3 %copy.34 = bf16[16,128,4,2,128]{4,3,2,1,0:T(2,128)(2,1)} copy(bf16[16,128,4,2,128]{4,1,3,2,0:T(8,128)(2,1)S(1)} %bitcast.76) | data formatting | bytes 8388608
  154.9 2.6 %shard_map.137.old_ref = f32[16,8,128,128]{3,2,1,0:T(8,128)} custom-call(s32[257]{0:T(512)S(1)} %concatenate.11.flat, s32[4,264,128]{2,1,0:T(8,128)} %collective-permute-done.9.packed_ref, f32[16,8,128,128]{3,2,1,0:T(8,128)} %shard_map.136.old_ref), custom_call_target="tpu_custom_call", output_to_operand_aliasing={{}: (2, {})} | custom-call | flops 1000 | bytes 1000 | tf_op jit(solution)/shard_map/pallas_call | solution.py:512
  157.5 2.6 %shard_map.138.old_ref = f32[16,8,128,128]{3,2,1,0:T(8,128)} custom-call(s32[257]{0:T(512)S(1)} %concatenate.11.flat, s32[4,264,128]{2,1,0:T(8,128)} %collective-permute-done.8.packed_ref, f32[16,8,128,128]{3,2,1,0:T(8,128)} %shard_map.137.old_ref), custom_call_target="tpu_custom_call", output_to_operand_aliasing={{}: (2, {})} | custom-call | flops 1000 | bytes 1000 | tf_op jit(solution)/shard_map/pallas_call | solution.py:512
  160.1 2.6 %shard_map.139.old_ref = f32[16,8,128,128]{3,2,1,0:T(8,128)} custom-call(s32[257]{0:T(512)S(1)} %concatenate.11.flat, s32[4,264,128]{2,1,0:T(8,128)} %collective-permute-done.7.packed_ref, f32[16,8,128,128]{3,2,1,0:T(8,128)} %shard_map.138.old_ref), custom_call_target="tpu_custom_call", output_to_operand_aliasing={{}: (2, {})} | custom-call | flops 1000 | bytes 1000 | tf_op jit(solution)/shard_map/pallas_call | solution.py:512
  162.6 12.0 %collective-permute-done.6.packed_ref = s32[4,264,128]{2,1,0:T(8,128)} collective-permute-done((s32[4,264,128]{2,1,0:T(8,128)}, s32[4,264,128]{2,1,0:T(8,128)}, u32[]{:S(2)}, u32[]{:S(2)}) %collective-permute-start.6) | collective-permute-done | bytes 540704 | tf_op jit(solution)/shard_map/ppermute | solution.py:554
  174.6 2.6 %shard_map.140 = f32[16,8,128,128]{3,2,1,0:T(8,128)} custom-call(s32[257]{0:T(512)S(1)} %concatenate.11.flat, s32[4,264,128]{2,1,0:T(8,128)} %collective-permute-done.6.packed_ref, f32[16,8,128,128]{3,2,1,0:T(8,128)} %shard_map.139.old_ref), custom_call_target="tpu_custom_call", output_to_operand_aliasing={{}: (2, {})} | custom-call | flops 1000 | bytes 1000 | tf_op jit(solution)/shard_map/pallas_call | solution.py:512
  (51 shorter events, 23.9 us)
Async XLA Ops:
  2.8 28.2 %collective-permute-start = (s32[4,264,128]{2,1,0:T(8,128)S(1)}, s32[4,264,128]{2,1,0:T(8,128)}, u32[]{:S(2)}, u32[]{:S(2)}) collective-permute-start(s32[4,264,128]{2,1,0:T(8,128)S(1)} %get-tuple-element.82.refs_12_), channel_id=1, source_target_pairs={{0,8},{4,12},{8,0},{12,4},{1,9},{5,13},{9,1},{13,5},{2,10},{6,14},... | collective-permute-start | bytes 1622024 | tf_op jit(solution)/shard_map/ppermute | solution.py:554
  9.1 46.7 %collective-permute-start.1 = (s32[4,264,128]{2,1,0:T(8,128)S(1)}, s32[4,264,128]{2,1,0:T(8,128)}, u32[]{:S(2)}, u32[]{:S(2)}) collective-permute-start(s32[4,264,128]{2,1,0:T(8,128)S(1)} %get-tuple-element.82.refs_12_), channel_id=1, source_target_pairs={{0,4},{4,0},{8,12},{12,8},{1,5},{5,1},{9,13},{13,9},{2,6},{6,2},{1... | collective-permute-start | bytes 1622024 | tf_op jit(solution)/shard_map/ppermute | solution.py:554
  10.7 3.6 %copy-start.6 = (bf16[16,128,4,2,128]{4,3,2,1,0:T(2,128)(2,1)S(1)}, bf16[16,128,4,2,128]{4,3,2,1,0:T(2,128)(2,1)}, u32[]{:S(2)}) copy-start(bf16[16,128,4,2,128]{4,3,2,1,0:T(2,128)(2,1)} %param.13) | copy-start | bytes 12582916
  14.4 3.3 %copy-start.9 = (s32[64]{0:T(128)S(1)}, s32[64]{0:T(128)}, u32[]{:S(2)}) copy-start(s32[64]{0:T(128)} %param.18) | copy-start | bytes 772
  14.4 3.3 %copy-start.10 = (s32[64]{0:T(128)S(1)}, s32[64]{0:T(128)}, u32[]{:S(2)}) copy-start(s32[64]{0:T(128)} %param.19) | copy-start | bytes 772
  14.4 3.3 %copy-start.11 = (s32[64]{0:T(128)S(1)}, s32[64]{0:T(128)}, u32[]{:S(2)}) copy-start(s32[64]{0:T(128)} %param.20) | copy-start | bytes 772
  14.4 3.3 %copy-start.12 = (s32[64]{0:T(128)S(1)}, s32[64]{0:T(128)}, u32[]{:S(2)}) copy-start(s32[64]{0:T(128)} %param.21) | copy-start | bytes 772
  14.4 3.4 %copy-start.7 = (bf16[16,128,4,2]{1,3,2,0:T(2,128)(2,1)S(1)}, bf16[16,128,4,2]{1,3,2,0:T(2,128)(2,1)}, u32[]{:S(2)}) copy-start(bf16[16,128,4,2]{1,3,2,0:T(2,128)(2,1)} %param.15) | copy-start | bytes 98308
  14.4 3.4 %copy-start.8 = (bf16[16,128,4,2]{1,3,2,0:T(2,128)(2,1)S(1)}, bf16[16,128,4,2]{1,3,2,0:T(2,128)(2,1)}, u32[]{:S(2)}) copy-start(bf16[16,128,4,2]{1,3,2,0:T(2,128)(2,1)} %param.14) | copy-start | bytes 98308
  17.8 1.6 copy-start.1
  31.0 25.5 %collective-permute-start.2 = (s32[4,264,128]{2,1,0:T(8,128)}, s32[4,264,128]{2,1,0:T(8,128)S(1)}, u32[]{:S(2)}, u32[]{:S(2)}) collective-permute-start(s32[4,264,128]{2,1,0:T(8,128)} %collective-permute-done.refs_14_), channel_id=1, source_target_pairs={{0,4},{4,0},{8,12},{12,8},{1,5},{5,1},{9,13},{13,9},{2,6},{6,2},{1... | collective-permute-start | bytes 1622024 | tf_op jit(solution)/shard_map/ppermute | solution.py:554
  31.6 27.3 %collective-permute-start.3 = (s32[4,264,128]{2,1,0:T(8,128)S(1)}, s32[4,264,128]{2,1,0:T(8,128)S(1)}, u32[]{:S(2)}, u32[]{:S(2)}) collective-permute-start(s32[4,264,128]{2,1,0:T(8,128)S(1)} %get-tuple-element.95.refs_12_), channel_id=1, source_target_pairs={{0,8},{4,12},{8,0},{12,4},{1,9},{5,13},{9,1},{13,5},{2,10},{6,14},... | collective-permute-start | bytes 1622024 | tf_op jit(solution)/shard_map/ppermute | solution.py:554
  45.5 15.4 %copy-start = (bf16[16,128,4,2,128]{4,1,3,2,0:T(8,128)(2,1)S(1)}, bf16[16,128,4,2,128]{4,1,3,2,0:T(8,128)(2,1)}, u32[]{:S(2)}) copy-start(bf16[16,128,4,2,128]{4,1,3,2,0:T(8,128)(2,1)} %copy.38) | copy-start | bytes 12582916
  45.5 15.4 %copy-start.5 = (bf16[128]{0:T(256)(128)(2,1)S(1)}, bf16[128]{0:T(256)(128)(2,1)}, u32[]{:S(2)}) copy-start(bf16[128]{0:T(256)(128)(2,1)} %param.16) | copy-start | bytes 772
  58.9 26.7 %collective-permute-start.4 = (s32[4,264,128]{2,1,0:T(8,128)S(1)}, s32[4,264,128]{2,1,0:T(8,128)S(1)}, u32[]{:S(2)}, u32[]{:S(2)}) collective-permute-start(s32[4,264,128]{2,1,0:T(8,128)S(1)} %get-tuple-element.95.refs_12_), channel_id=1, source_target_pairs={{0,4},{4,0},{8,12},{12,8},{1,5},{5,1},{9,13},{13,9},{2,6},{6,2},{1... | collective-permute-start | bytes 1622024 | tf_op jit(solution)/shard_map/ppermute | solution.py:554
  59.4 39.4 %collective-permute-start.5 = (s32[4,264,128]{2,1,0:T(8,128)S(1)}, s32[4,264,128]{2,1,0:T(8,128)S(1)}, u32[]{:S(2)}, u32[]{:S(2)}) collective-permute-start(s32[4,264,128]{2,1,0:T(8,128)S(1)} %collective-permute-done.3.refs_14_), channel_id=1, source_target_pairs={{0,4},{4,0},{8,12},{12,8},{1,5},{5,1},{9,13},{13,9},{2,6},{6,2},{1... | collective-permute-start | bytes 1622024 | tf_op jit(solution)/shard_map/ppermute | solution.py:554
  67.0 63.5 %collective-permute-start.11 = (s32[4,264,128]{2,1,0:T(8,128)S(1)}, s32[4,264,128]{2,1,0:T(8,128)S(1)}, u32[]{:S(2)}, u32[]{:S(2)}) collective-permute-start(s32[4,264,128]{2,1,0:T(8,128)S(1)} %get-tuple-element.110), channel_id=1, source_target_pairs={{0,12},{4,8},{8,4},{12,0},{1,13},{5,9},{9,5},{13,1},{2,14},{6,10},... | collective-permute-start | bytes 1622024 | tf_op jit(solution)/shard_map/ppermute | solution.py:554
  75.0 71.1 %collective-permute-start.10 = (s32[4,264,128]{2,1,0:T(8,128)S(1)}, s32[4,264,128]{2,1,0:T(8,128)S(1)}, u32[]{:S(2)}, u32[]{:S(2)}) collective-permute-start(s32[4,264,128]{2,1,0:T(8,128)S(1)} %get-tuple-element.109), channel_id=1, source_target_pairs={{0,8},{4,12},{8,0},{12,4},{1,9},{5,13},{9,1},{13,5},{2,10},{6,14},... | collective-permute-start | bytes 1622024 | tf_op jit(solution)/shard_map/ppermute | solution.py:554
  118.5 36.4 %collective-permute-start.9 = (s32[4,264,128]{2,1,0:T(8,128)}, s32[4,264,128]{2,1,0:T(8,128)}, u32[]{:S(2)}, u32[]{:S(2)}) collective-permute-start(s32[4,264,128]{2,1,0:T(8,128)} %get-tuple-element.108), channel_id=1, source_target_pairs={{0,4},{4,0},{8,12},{12,8},{1,5},{5,1},{9,13},{13,9},{2,6},{6,2},{1... | collective-permute-start | bytes 1622024 | tf_op jit(solution)/shard_map/ppermute | solution.py:554
  125.2 32.3 %collective-permute-start.8 = (s32[4,264,128]{2,1,0:T(8,128)}, s32[4,264,128]{2,1,0:T(8,128)}, u32[]{:S(2)}, u32[]{:S(2)}) collective-permute-start(s32[4,264,128]{2,1,0:T(8,128)} %get-tuple-element.107), channel_id=1, source_target_pairs={{0,4},{4,0},{8,12},{12,8},{1,5},{5,1},{9,13},{13,9},{2,6},{6,2},{1... | collective-permute-start | bytes 1622024 | tf_op jit(solution)/shard_map/ppermute | solution.py:554
  127.2 32.8 %collective-permute-start.7 = (s32[4,264,128]{2,1,0:T(8,128)}, s32[4,264,128]{2,1,0:T(8,128)}, u32[]{:S(2)}, u32[]{:S(2)}) collective-permute-start(s32[4,264,128]{2,1,0:T(8,128)} %get-tuple-element.106), channel_id=1, source_target_pairs={{0,12},{4,8},{8,4},{12,0},{1,13},{5,9},{9,5},{13,1},{2,14},{6,10},... | collective-permute-start | bytes 1622024 | tf_op jit(solution)/shard_map/ppermute | solution.py:554
  130.5 44.1 %collective-permute-start.6 = (s32[4,264,128]{2,1,0:T(8,128)}, s32[4,264,128]{2,1,0:T(8,128)}, u32[]{:S(2)}, u32[]{:S(2)}) collective-permute-start(s32[4,264,128]{2,1,0:T(8,128)} %get-tuple-element.105), channel_id=1, source_target_pairs={{0,8},{4,12},{8,0},{12,4},{1,9},{5,13},{9,1},{13,5},{2,10},{6,14},... | collective-permute-start | bytes 1622024 | tf_op jit(solution)/shard_map/ppermute | solution.py:554
  143.7 2.3 %copy-start.2 = (bf16[16,4,2,128,128]{4,3,2,1,0:T(8,128)(2,1)}, bf16[16,4,2,128,128]{4,3,2,1,0:T(8,128)(2,1)S(1)}, u32[]{:S(2)}) copy-start(bf16[16,4,2,128,128]{4,3,2,1,0:T(8,128)(2,1)S(1)} %get-tuple-element.104) | copy-start | bytes 12582916
  146.0 2.6 %copy-start.3 = (bf16[16,4,2,128,128]{4,3,2,1,0:T(8,128)(2,1)S(1)}, bf16[16,4,2,128,128]{4,3,2,1,0:T(8,128)(2,1)}, u32[]{:S(2)}) copy-start(bf16[16,4,2,128,128]{4,3,2,1,0:T(8,128)(2,1)} %copy-done.2) | copy-start | bytes 12582916
  (1 other events, 1.6 us)

commit v3 on v2

--- a/solution.py
+++ b/solution.py
@@ -275,36 +275,51 @@
     )(flat, *operands)
 
 
-def state_kernel(part, away, plan, shards_held, together, flat, gain_ref, *refs):
+def turn_of(aways, each, turn):
+    if len(aways) == 1:
+        return aways[0], turn
+    number = turn // each
+    away = aways[-1]
+    for at in reversed(range(len(aways) - 1)):
+        away = jnp.where(number == at, aways[at], away)
+    return away, turn - number * each
+
+
+def state_kernel(part, aways, plan, shards_held, together, flat, gain_ref, *refs):
     per = 6
     inputs = [refs[per * e:per * (e + 1)] for e in range(together)]
     parents = refs[per * together:per * together + shards_held]
-    mixed_hbm, state_ref, states_in, mixed_out, arrivals, leaving = refs[-6:]
+    states_in, mixed_out, arrivals, leaving = refs[-4:]
+    mixed_hbm, *state_refs = refs[-5 - len(aways):-4]
     turn, turns = pl.program_id(0), pl.num_programs(0)
+    each = plan.per_peer // together
     key_heads = inputs[0][0].shape[1]
     heads = 2 * key_heads
     all_heads = inputs[0][3].shape[1] // 2
 
     def fetch(i, slot):
         for e in range(together):
-            shard = plan.shard(flat, away, i * together + e)
+            away, at = turn_of(aways, each, i)
+            shard = plan.shard(flat, away, at * together + e)
             for off in range(shards_held):
                 @pl.when(shard == off)
                 def _():
                     pltpu.make_async_copy(
-                        parents[off].at[plan.row(flat, away, i * together + e)],
+                        parents[off].at[plan.row(flat, away, at * together + e)],
                         states_in.at[slot, e],
                         arrivals.at[slot, e],
                     ).start()
 
     def leave(i, slot, e):
+        away, at = turn_of(aways, each, i)
         return pltpu.make_async_copy(
             mixed_out.at[slot, e],
-            mixed_hbm.at[plan.local(flat, away, i * together + e), pl.ds(part * key_heads, key_heads)],
+            mixed_hbm.at[plan.local(flat, away, at * together + e), pl.ds(part * key_heads, key_heads)],
             leaving.at[slot, e],
         )
 
     slot = lax.rem(turn, 2)
+    my_away, my_turn = turn_of(aways, each, turn)
 
     @pl.when(turn == 0)
     def _():
@@ -331,7 +346,7 @@
     state, products, n_cols, g_cols, b_cols, eg_cols, steps = [], [], [], [], [], [], []
     for e in range(together):
         q_ref, k_ref, v_ref, rate_ref, inv_ref, am_ref = inputs[e]
-        rates = live_rates(rate_ref[0], plan.tokens(flat, away, turn * together + e))
+        rates = live_rates(rate_ref[0], plan.tokens(flat, my_away, my_turn * together + e))
         cols = dot_nt(jnp.concatenate([lower_ones, unit], axis=0), rates)
         g_cols.append(cols[:LEN])
         b_cols.append(cols[LEN:])
@@ -406,18 +421,26 @@
         out = decay_at(e, h) * qs + am_v[c][LEN:]
         out = out + dot(inputs[e][5][0, h, LEN:, :LEN], delta[c].astype(BF16))
         mean_square = jnp.mean(out * out, axis=1, keepdims=True)
-        live = iota((LEN, 1), 0) < plan.tokens(flat, away, turn * together + e)
+        live = iota((LEN, 1), 0) < plan.tokens(flat, my_away, my_turn * together + e)
         scale = jnp.where(live, lax.rsqrt(mean_square + EPS), 0.0)
         mixed_out[slot, e, h // 2, h % 2] = (out * scale * gain).astype(BF16)
     for e in range(together):
         leave(turn, slot, e).start()
-    for e in range(together):
-        mine = finals[e * heads:(e + 1) * heads]
-        if away == 0:
-            for h in range(heads):
-                state_ref[e, h] = mine[h]
+
+    def store(ref, away):
+        for e in range(together):
+            mine = finals[e * heads:(e + 1) * heads]
+            if away:
+                store_packed(ref.at[pl.ds(e, 1)], mine)
+            else:
+                for h in range(heads):
+                    ref[e, h] = mine[h]
+
+    for number, away in enumerate(aways):
+        if len(aways) == 1:
+            store(state_refs[0], away)
         else:
-            store_packed(state_ref.at[pl.ds(e, 1)], mine)
+            pl.when(turn // each == number)(functools.partial(store, state_refs[number], away))
 
     @pl.when(turn == turns - 1)
     def _():
@@ -430,7 +453,7 @@
             leave(turn - 1, 1 - slot, e).wait()
 
 
-def recurrence(part, away, plan, flat, q, k, v, rates, pairs, parents, gain, mixed, final_shape=None, final=None):
+def recurrence(part, aways, plan, flat, q, k, v, rates, pairs, parents, gain, mixed, final_shape, final):
     count = plan.per_peer
     together = min(TOGETHER, count)
     turns = count // together
@@ -442,7 +465,8 @@
 
     def one(shape, e, at):
         def index(i, t):
-            return (plan.local(t, away, i * together + e), at) + (0,) * (len(shape) - 2)
+            away, turn = turn_of(aways, turns, i)
+            return (plan.local(t, away, turn * together + e), at) + (0,) * (len(shape) - 2)
 
         return pl.BlockSpec(shape, index)
 
@@ -465,23 +489,36 @@
         operands.append(mixed)
     mixed_spec = pl.BlockSpec(memory_space=pl.ANY)
     mixed_shape = jax.ShapeDtypeStruct(v.shape, BF16)
-    if final_shape is None:
-        state_spec = pl.BlockSpec((together, rows, LEN), lambda i, t: (i, 0, 0))
-        state_shape = jax.ShapeDtypeStruct((count, rows, LEN), jnp.int32)
-    else:
-        if final is not None:
-            in_specs.append(pl.BlockSpec(memory_space=pl.ANY))
-            aliases[1 + len(operands)] = 1
-            operands.append(final)
-        state_spec = pl.BlockSpec((together, heads, LEN, LEN), lambda i, t: (plan.me(t) * turns + i, part, 0, 0))
-        state_shape = jax.ShapeDtypeStruct(final_shape, F32)
+    state_specs, state_shapes = [], []
+
+    def turn_in(number, i):
+        return i if len(aways) == 1 else jnp.clip(i - number * turns, 0, turns - 1)
+
+    for number, away in enumerate(aways):
+        if away:
+            state_specs.append(
+                pl.BlockSpec((together, rows, LEN), lambda i, t, n=number: (turn_in(n, i), 0, 0))
+            )
+            state_shapes.append(jax.ShapeDtypeStruct((count, rows, LEN), jnp.int32))
+        else:
+            if final is not None:
+                in_specs.append(pl.BlockSpec(memory_space=pl.ANY))
+                aliases[1 + len(operands)] = 1 + number
+                operands.append(final)
+            state_specs.append(
+                pl.BlockSpec(
+                    (together, heads, LEN, LEN),
+                    lambda i, t, n=number: (plan.me(t) * turns + turn_in(n, i), part, 0, 0),
+                )
+            )
+            state_shapes.append(jax.ShapeDtypeStruct(final_shape, F32))
     return pl.pallas_call(
-        functools.partial(state_kernel, part, away, plan, len(parents), together),
+        functools.partial(state_kernel, part, aways, plan, len(parents), together),
         grid_spec=pltpu.PrefetchScalarGridSpec(
             num_scalar_prefetch=1,
-            grid=(turns,),
+            grid=(turns * len(aways),),
             in_specs=in_specs,
-            out_specs=[mixed_spec, state_spec],
+            out_specs=[mixed_spec, *state_specs],
             scratch_shapes=[
                 pltpu.VMEM((2, together, rows, LEN), jnp.int32),
                 pltpu.VMEM((2, together, key_heads, 2, LEN, LEN), BF16),
@@ -489,42 +526,79 @@
                 pltpu.SemaphoreType.DMA((2, together)),
             ],
         ),
-        out_shape=[mixed_shape, state_shape],
+        out_shape=[mixed_shape, *state_shapes],
         input_output_aliases=aliases,
         compiler_params=pltpu.CompilerParams(vmem_limit_bytes=VMEM_LIMIT),
         cost_estimate=pl.CostEstimate(flops=1000, bytes_accessed=1000, transcendentals=0),
     )(flat, *operands)
 
 
-def unpack_kernel(flat, packed_ref, old_ref, out_ref):
+def unpack_kernel(turns, flat, *refs):
+    *packed_refs, old_ref, out_ref = refs
     count, heads = out_ref.shape[:2]
-    for e in range(count):
-        steps = load_steps(packed_ref.at[pl.ds(e, 1)], heads)
-        for h in range(heads):
-            out_ref[e, h] = decode(packed_ref[e, h * HALF:(h + 1) * HALF, :]) * steps[h:h + 1, :]
-
-
-def unpack_states(part, away, plan, flat, packed, final):
-    count, rows = packed.shape[:2]
+
+    def unpack(ref):
+        for e in range(count):
+            steps = load_steps(ref.at[pl.ds(e, 1)], heads)
+            for h in range(heads):
+                out_ref[e, h] = decode(ref[e, h * HALF:(h + 1) * HALF, :]) * steps[h:h + 1, :]
+
+    for number, ref in enumerate(packed_refs):
+        if len(packed_refs) == 1:
+            unpack(ref)
+        else:
+            pl.when(pl.program_id(0) // turns == number)(functools.partial(unpack, ref))
+
+
+def unpack_states(part, aways, plan, flat, packed, final):
+    count, rows = packed[0].shape[:2]
     heads = final.shape[1] // PARTS
     block = max(1, count // 2)
     turns = count // block
+
+    def place(i, t):
+        away, turn = turn_of(aways, turns, i)
+        return (plan.peer(t, away) * turns + turn, part, 0, 0)
+
+    def turn_in(number, i):
+        return i if len(aways) == 1 else jnp.clip(i - number * turns, 0, turns - 1)
+
     return pl.pallas_call(
-        unpack_kernel,
+        functools.partial(unpack_kernel, turns),
         grid_spec=pltpu.PrefetchScalarGridSpec(
             num_scalar_prefetch=1,
-            grid=(turns,),
+            grid=(turns * len(aways),),
             in_specs=[
-                pl.BlockSpec((block, rows, LEN), lambda i, t: (i, 0, 0)),
-                pl.BlockSpec(memory_space=pl.ANY),
-            ],
-            out_specs=pl.BlockSpec((block, heads, LEN, LEN), lambda i, t: (plan.peer(t, away) * turns + i, part, 0, 0)),
+                pl.BlockSpec((block, rows, LEN), lambda i, t, n=number: (turn_in(n, i), 0, 0))
+                for number in range(len(aways))
+            ]
+            + [pl.BlockSpec(memory_space=pl.ANY)],
+            out_specs=pl.BlockSpec((block, heads, LEN, LEN), place),
         ),
         out_shape=jax.ShapeDtypeStruct(final.shape, F32),
-        input_output_aliases={2: 0},
+        input_output_aliases={1 + len(aways): 0},
         compiler_params=pltpu.CompilerParams(vmem_limit_bytes=VMEM_LIMIT),
         cost_estimate=pl.CostEstimate(flops=1000, bytes_accessed=1000, transcendentals=0),
-    )(flat, packed, final)
+    )(flat, *packed, final)
+
+
+def turn_kernel(mixed_ref, out_ref):
+    key_heads, pair, length, size = mixed_ref.shape[1:]
+    out_ref[0] = jnp.swapaxes(mixed_ref[0].reshape(key_heads * pair, length, size), 0, 1)
+
+
+def turn_mixed(mixed):
+    count, key_heads, pair, length, size = mixed.shape
+    heads = key_heads * pair
+    return pl.pallas_call(
+        turn_kernel,
+        grid=(count,),
+        in_specs=[pl.BlockSpec((1, key_heads, pair, length, size), lambda i: (i, 0, 0, 0, 0))],
+        out_specs=pl.BlockSpec((1, length, heads, size), lambda i: (i, 0, 0, 0)),
+        out_shape=jax.ShapeDtypeStruct((count, length, heads, size), mixed.dtype),
+        compiler_params=pltpu.CompilerParams(vmem_limit_bytes=VMEM_LIMIT),
+        cost_estimate=pl.CostEstimate(flops=1000, bytes_accessed=1000, transcendentals=0),
+    )(mixed)
 
 
 def shards(
@@ -590,24 +664,40 @@
     final_shape = (per_device, heads, key_dim, key_dim)
     crossing = list(reversed(range(half_way, seq_count)))
     near = list(reversed(range(1, half_way)))
-    turns = [(part, away) for part in range(PARTS) for away in crossing]
-    turns += [(part, away) for part in range(PARTS) for away in near]
-    turns += [(part, 0) for part in range(PARTS)]
     mixed, final = None, None
     arrived = {}
-    for part, away in turns:
-        if part == 1 and away == crossing[0]:
-            rates, mixed, pairs[1] = lax.optimization_barrier((rates, mixed, pairs[1]))
-            pairs[1] = pair_parts(1, 1, plan, flat, q, k, rates, pairs[1])
-        common = (part, away, plan, flat, q, k, v, rates, pairs[part], gathered[part], gain, mixed)
-        if away:
-            mixed, packed = recurrence(*common)
-            arrived[part, away] = swap(packed, away)
-        else:
-            mixed, final = recurrence(*common, final_shape, final)
-    for part, away in [(0, away) for away in crossing + near] + [(1, away) for away in near + crossing]:
-        final = unpack_states(part, away, plan, flat, arrived[part, away], final)
-    mixed_out = jnp.transpose(mixed, (0, 3, 1, 2, 4))
+
+    def work(part, aways, mixed, final):
+        mixed, *states = recurrence(
+            part, aways, plan, flat, q, k, v, rates, pairs[part], gathered[part], gain, mixed, final_shape, final
+        )
+        for away, state in zip(aways, states):
+            if away:
+                arrived[part, away] = swap(state, away)
+            else:
+                final = state
+        return mixed, final
+
+    def gone(mixed, aways):
+        for away in aways:
+            mixed, arrived[0, away] = lax.optimization_barrier((mixed, arrived[0, away]))
+        return mixed
+
+    for away in crossing + near:
+        mixed, final = work(0, [away], mixed, final)
+    rates, mixed, pairs[1] = lax.optimization_barrier((rates, mixed, pairs[1]))
+    pairs[1] = pair_parts(1, 1, plan, flat, q, k, rates, pairs[1])
+    mixed = gone(mixed, crossing[:1])
+    for away in near + crossing:
+        mixed, final = work(1, [away], mixed, final)
+    mixed = gone(mixed, crossing[1:] + near)
+    for part in range(PARTS):
+        mixed, final = work(part, [0], mixed, final)
+    away_first = crossing + near
+    final = unpack_states(0, away_first, plan, flat, [arrived[0, away] for away in away_first], final)
+    for away in near + crossing:
+        final = unpack_states(1, [away], plan, flat, [arrived[1, away]], final)
+    mixed_out = turn_mixed(mixed).reshape(values.shape)
     final_out = final.reshape((per_device, key_heads, 2, key_dim, key_dim))
     return (mixed_out, final_out)
 

time: 178 us -> 175 us (0.983)
  local copies, waits for them, and re-layouts: 19.8 us -> 12.3 us
  waiting for transfers between devices: 29.6 us -> 35.5 us
  Pallas kernels: 107 us -> 105 us
    unnamed x30 -> x25, local copies, waits for them, and re-layouts: 19.7 us -> 12.2 us
    ppermute x12, waiting for transfers between devices: 29.6 us -> 35.5 us  [swap(): return lax.ppermute(tensor, 'seq', [(i, i ^ off) for i in range(seq_count)])]
    pallas_call x14 -> x13, Pallas kernels: 65.3 us -> 63.5 us  [the longest x8 48.8 us: recurrence(): pl.pallas_call(functools.partial(state_kernel, part, aways, plan, len(par...]
  transfers between devices with their start and end apart: 12 -> 12, of which waited for: 5 -> 6; matrix products, arithmetic and copies ran while one was open for 9% -> 5% of each run, Pallas kernels for 59% -> 56%
where the time goes in v3:
time: 175 us
  Pallas kernels  105 us (60%)
  waiting for transfers between devices  35.5 us (20%)
  starting transfers between devices  20.8 us (12%)
  local copies, waits for them, and re-layouts  12.3 us (7%)
    pallas_call x8, Pallas kernels, recurrence(): pl.pallas_call(functools.partial(state_kernel, part, aways, plan, len(par...  48.8 us
    pallas_call x4, Pallas kernels, pair_parts(): pl.pallas_call(functools.partial(pair_kernel, part, first, plan), grid_sp...  41.3 us
    ppermute x12, waiting for transfers between devices, swap(): return lax.ppermute(tensor, 'seq', [(i, i ^ off) for i in range(seq_count)])  35.5 us
    ppermute x12, starting transfers between devices, swap(): return lax.ppermute(tensor, 'seq', [(i, i ^ off) for i in range(seq_count)])  20.8 us
    unnamed x25, local copies, waits for them, and re-layouts  12.2 us
    pallas_call x4, Pallas kernels, unpack_states(): pl.pallas_call(functools.partial(unpack_kernel, turns), grid_spec=pltpu.P...  8.29 us
    pallas_call x1, Pallas kernels, turn_mixed(): pl.pallas_call(turn_kernel, grid=(count,), in_specs=[pl.BlockSpec((1, key...  6.44 us
  transfers between devices with their start and end apart: 12, of which 6 were waited for; matrix products, arithmetic and copies ran while one was open for 5% of the time, Pallas kernels for 56%

profile of v3, /device:TPU:0, one launch (start us, length us, event | category | flops | bytes accessed | tf_op | source)
XLA Modules:
  0.0 175.0 jit_solution(8461085765738474843)
XLA Ops:
  2.8 4.1 %collective-permute-start = (s32[4,264,128]{2,1,0:T(8,128)S(1)}, s32[4,264,128]{2,1,0:T(8,128)}, u32[]{:S(2)}, u32[]{:S(2)}) collective-permute-start(s32[4,264,128]{2,1,0:T(8,128)S(1)} %get-tuple-element.88.refs_12_), channel_id=1, source_target_pairs={{0,8},{4,12},{8,0},{12,4},{1,9},{5,13},{9,1},{13,5},{2,10},{6,14},... | collective-permute-start | bytes 1622024 | tf_op jit(solution)/shard_map/ppermute | solution.py:628
  10.7 3.6 %copy.36 = bf16[16,128,4,128]{3,1,2,0:T(8,128)(2,1)} copy(bf16[16,128,4,128]{3,2,1,0:T(4,128)(2,1)} %param.12) | data formatting | bytes 4194304 | tf_op args[1]
  14.4 3.3 %copy.35 = bf16[16,128,4,2,128]{4,1,3,2,0:T(8,128)(2,1)} copy(bf16[16,128,4,2,128]{4,3,2,1,0:T(2,128)(2,1)S(1)} %copy-done.4) | data formatting | bytes 8388608 | tf_op args[2]
  19.4 10.3 %shard_map.123 = (bf16[16,4,128,128]{3,2,1,0:T(8,128)(2,1)S(1)}, bf16[16,4,256,256]{3,2,1,0:T(8,128)(2,1)S(1)}) custom-call(s32[257]{0:T(512)S(1)} %concatenate.11.flat, bf16[16,4,128,128]{3,2,1,0:T(8,128)(2,1)S(1)} %bitcast.36, bf16[16,4,128,128]{3,2,1,0:T(8,128)(2,1)S(1)} %bitcast.56, f32[16,16,128]{2,1,0:T(8,128)S(1)} %maximum_convert_fusion.rate_ref.refs_3_.refs_9_), custom_call_target="tpu_custom_call" | custom-call | flops 1000 | bytes 1000 | tf_op jit(solution)/shard_map/pallas_call | solution.py:257
  31.6 3.5 %collective-permute-start.3 = (s32[4,264,128]{2,1,0:T(8,128)S(1)}, s32[4,264,128]{2,1,0:T(8,128)S(1)}, u32[]{:S(2)}, u32[]{:S(2)}) collective-permute-start(s32[4,264,128]{2,1,0:T(8,128)S(1)} %get-tuple-element.102.refs_12_), channel_id=1, source_target_pairs={{0,8},{4,12},{8,0},{12,4},{1,9},{5,13},{9,1},{13,5},{2,10},{6,14},... | collective-permute-start | bytes 1622024 | tf_op jit(solution)/shard_map/ppermute | solution.py:628
  35.1 10.3 %shard_map.124 = (bf16[16,4,128,128]{3,2,1,0:T(8,128)(2,1)S(1)}, bf16[16,4,256,256]{3,2,1,0:T(8,128)(2,1)S(1)}) custom-call(s32[257]{0:T(512)S(1)} %concatenate.11.flat, bf16[16,4,128,128]{3,2,1,0:T(8,128)(2,1)S(1)} %bitcast.37, bf16[16,4,128,128]{3,2,1,0:T(8,128)(2,1)S(1)} %bitcast.57, ...), custom_call_target="tpu_custom_call", output_to_operand_aliasing={{0}: (4, {}), {1}: (5, {})} | custom-call | flops 1000 | bytes 1000 | tf_op jit(solution)/shard_map/pallas_call | solution.py:257
  45.5 10.3 %shard_map.125 = (bf16[16,4,128,128]{3,2,1,0:T(8,128)(2,1)S(1)}, bf16[16,4,256,256]{3,2,1,0:T(8,128)(2,1)S(1)}) custom-call(s32[257]{0:T(512)S(1)} %concatenate.11.flat, bf16[16,4,128,128]{3,2,1,0:T(8,128)(2,1)S(1)} %bitcast.38, bf16[16,4,128,128]{3,2,1,0:T(8,128)(2,1)S(1)} %bitcast.58, f32[16,16,128]{2,1,0:T(8,128)S(1)} %maximum_convert_fusion.rate_ref.refs_3_.refs_9_), custom_call_target="tpu_custom_call" | custom-call | flops 1000 | bytes 1000 | tf_op jit(solution)/shard_map/pallas_call | solution.py:257
  56.5 2.4 %collective-permute-done.3.refs_14_ = s32[4,264,128]{2,1,0:T(8,128)S(1)} collective-permute-done((s32[4,264,128]{2,1,0:T(8,128)S(1)}, s32[4,264,128]{2,1,0:T(8,128)S(1)}, u32[]{:S(2)}, u32[]{:S(2)}) %collective-permute-start.3) | collective-permute-done | bytes 540704 | tf_op jit(solution)/shard_map/ppermute | solution.py:628
  58.9 5.8 %shard_map.126 = (bf16[16,4,2,128,128]{4,3,2,1,0:T(8,128)(2,1)S(1)}, s32[4,264,128]{2,1,0:T(8,128)S(1)}) custom-call(s32[257]{0:T(512)S(1)} %concatenate.11.flat, bf16[1,128]{1,0:T(2,128)(2,1)S(1)} %bitcast.77, bf16[16,4,128,128]{3,2,1,0:T(8,128)(2,1)S(1)} %bitcast.39, bf16[16,4,128,128]{3,2,1,0:T(8,128)(2,1)S(1)} %bitcast.59, ...), custom_call_target="tpu_custom_call" | custom-call | flops 1000 | bytes 1000 | tf_op jit(solution)/shard_map/pallas_call | solution.py:515
  64.7 2.6 %collective-permute-start.6 = (s32[4,264,128]{2,1,0:T(8,128)S(1)}, s32[4,264,128]{2,1,0:T(8,128)S(1)}, u32[]{:S(2)}, u32[]{:S(2)}) collective-permute-start(s32[4,264,128]{2,1,0:T(8,128)S(1)} %get-tuple-element.105), channel_id=1, source_target_pairs={{0,12},{4,8},{8,4},{12,0},{1,13},{5,9},{9,5},{13,1},{2,14},{6,10},... | collective-permute-start | bytes 1622024 | tf_op jit(solution)/shard_map/ppermute | solution.py:628
  69.3 6.0 %shard_map.127 = (bf16[16,4,2,128,128]{4,3,2,1,0:T(8,128)(2,1)S(1)}, s32[4,264,128]{2,1,0:T(8,128)S(1)}) custom-call(s32[257]{0:T(512)S(1)} %concatenate.11.flat, bf16[1,128]{1,0:T(2,128)(2,1)S(1)} %bitcast.78, bf16[16,4,128,128]{3,2,1,0:T(8,128)(2,1)S(1)} %bitcast.41, bf16[16,4,128,128]{3,2,1,0:T(8,128)(2,1)S(1)} %bitcast.61, ...), custom_call_target="tpu_custom_call", output_to_operand_aliasing={{0}: (18, {})} | custom-call | flops 1000 | bytes 1000 | tf_op jit(solution)/shard_map/pallas_call | solution.py:515
  75.2 6.1 %shard_map.128 = (bf16[16,4,2,128,128]{4,3,2,1,0:T(8,128)(2,1)S(1)}, s32[4,264,128]{2,1,0:T(8,128)S(1)}) custom-call(s32[257]{0:T(512)S(1)} %concatenate.11.flat, bf16[1,128]{1,0:T(2,128)(2,1)S(1)} %bitcast.79, bf16[16,4,128,128]{3,2,1,0:T(8,128)(2,1)S(1)} %bitcast.43, bf16[16,4,128,128]{3,2,1,0:T(8,128)(2,1)S(1)} %bitcast.63, ...), custom_call_target="tpu_custom_call", output_to_operand_aliasing={{0}: (18, {})} | custom-call | flops 1000 | bytes 1000 | tf_op jit(solution)/shard_map/pallas_call | solution.py:515
  83.3 10.3 %shard_map.129 = (bf16[16,4,128,128]{3,2,1,0:T(8,128)(2,1)S(1)}, bf16[16,4,256,256]{3,2,1,0:T(8,128)(2,1)S(1)}) custom-call(s32[257]{0:T(512)S(1)} %concatenate.11.flat, bf16[16,4,128,128]{3,2,1,0:T(8,128)(2,1)S(1)} %bitcast.45, bf16[16,4,128,128]{3,2,1,0:T(8,128)(2,1)S(1)} %bitcast.65, ...), custom_call_target="tpu_custom_call", output_to_operand_aliasing={{0}: (4, {}), {1}: (5, {})} | custom-call | flops 1000 | bytes 1000 | tf_op jit(solution)/shard_map/pallas_call | solution.py:257
  93.6 8.6 %collective-permute-done.4.refs_13_ = s32[4,264,128]{2,1,0:T(8,128)S(1)} collective-permute-done((s32[4,264,128]{2,1,0:T(8,128)S(1)}, s32[4,264,128]{2,1,0:T(8,128)S(1)}, u32[]{:S(2)}, u32[]{:S(2)}) %collective-permute-start.4) | collective-permute-done | bytes 540704 | tf_op jit(solution)/shard_map/ppermute | solution.py:628
  102.2 11.6 %collective-permute-done.5.refs_15_ = s32[4,264,128]{2,1,0:T(8,128)S(1)} collective-permute-done((s32[4,264,128]{2,1,0:T(8,128)S(1)}, s32[4,264,128]{2,1,0:T(8,128)S(1)}, u32[]{:S(2)}, u32[]{:S(2)}) %collective-permute-start.5) | collective-permute-done | bytes 540704 | tf_op jit(solution)/shard_map/ppermute | solution.py:628
  113.8 5.8 %shard_map.130 = (bf16[16,4,2,128,128]{4,3,2,1,0:T(8,128)(2,1)S(1)}, s32[4,264,128]{2,1,0:T(8,128)S(1)}) custom-call(s32[257]{0:T(512)S(1)} %concatenate.11.flat, bf16[1,128]{1,0:T(2,128)(2,1)S(1)} %bitcast.80, bf16[16,4,128,128]{3,2,1,0:T(8,128)(2,1)S(1)} %bitcast.46, bf16[16,4,128,128]{3,2,1,0:T(8,128)(2,1)S(1)} %bitcast.66, ...), custom_call_target="tpu_custom_call", output_to_operand_aliasing={{0}: (18, {})} | custom-call | flops 1000 | bytes 1000 | tf_op jit(solution)/shard_map/pallas_call | solution.py:515
  119.6 5.8 %shard_map.131 = (bf16[16,4,2,128,128]{4,3,2,1,0:T(8,128)(2,1)S(1)}, s32[4,264,128]{2,1,0:T(8,128)S(1)}) custom-call(s32[257]{0:T(512)S(1)} %concatenate.11.flat, bf16[1,128]{1,0:T(2,128)(2,1)S(1)} %bitcast.81, bf16[16,4,128,128]{3,2,1,0:T(8,128)(2,1)S(1)} %bitcast.48, bf16[16,4,128,128]{3,2,1,0:T(8,128)(2,1)S(1)} %bitcast.68, ...), custom_call_target="tpu_custom_call", output_to_operand_aliasing={{0}: (18, {})} | custom-call | flops 1000 | bytes 1000 | tf_op jit(solution)/shard_map/pallas_call | solution.py:515
  125.4 3.6 %collective-permute-start.10 = (s32[4,264,128]{2,1,0:T(8,128)S(1)}, s32[4,264,128]{2,1,0:T(8,128)S(1)}, u32[]{:S(2)}, u32[]{:S(2)}) collective-permute-start(s32[4,264,128]{2,1,0:T(8,128)S(1)} %get-tuple-element.118), channel_id=1, source_target_pairs={{0,12},{4,8},{8,4},{12,0},{1,13},{5,9},{9,5},{13,1},{2,14},{6,10},... | collective-permute-start | bytes 1622024 | tf_op jit(solution)/shard_map/ppermute | solution.py:628
  129.1 5.8 %shard_map.132 = (bf16[16,4,2,128,128]{4,3,2,1,0:T(8,128)(2,1)S(1)}, s32[4,264,128]{2,1,0:T(8,128)S(1)}) custom-call(s32[257]{0:T(512)S(1)} %concatenate.11.flat, bf16[1,128]{1,0:T(2,128)(2,1)S(1)} %bitcast.82, bf16[16,4,128,128]{3,2,1,0:T(8,128)(2,1)S(1)} %bitcast.50, bf16[16,4,128,128]{3,2,1,0:T(8,128)(2,1)S(1)} %bitcast.70, ...), custom_call_target="tpu_custom_call", output_to_operand_aliasing={{0}: (18, {})} | custom-call | flops 1000 | bytes 1000 | tf_op jit(solution)/shard_map/pallas_call | solution.py:515
  135.8 6.7 %shard_map.133 = (bf16[16,4,2,128,128]{4,3,2,1,0:T(8,128)(2,1)S(1)}, f32[16,8,128,128]{3,2,1,0:T(8,128)}) custom-call(s32[257]{0:T(512)S(1)} %concatenate.11.flat, bf16[1,128]{1,0:T(2,128)(2,1)S(1)} %bitcast.83, bf16[16,4,128,128]{3,2,1,0:T(8,128)(2,1)S(1)} %bitcast.52, bf16[16,4,128,128]{3,2,1,0:T(8,128)(2,1)S(1)} %bitcast.72, ...), custom_call_target="tpu_custom_call", output_to_operand_aliasing={{0}: (18, {})} | custom-call | flops 1000 | bytes 1000 | tf_op jit(solution)/shard_map/pallas_call | solution.py:515
  142.5 6.7 %shard_map.134 = (bf16[16,4,2,128,128]{4,3,2,1,0:T(8,128)(2,1)S(1)}, f32[16,8,128,128]{3,2,1,0:T(8,128)}) custom-call(s32[257]{0:T(512)S(1)} %concatenate.11.flat, bf16[1,128]{1,0:T(2,128)(2,1)S(1)} %bitcast.84, bf16[16,4,128,128]{3,2,1,0:T(8,128)(2,1)S(1)} %bitcast.54, ...), custom_call_target="tpu_custom_call", output_to_operand_aliasing={{0}: (18, {}), {1}: (19, {})} | custom-call | flops 1000 | bytes 1000 | tf_op jit(solution)/shard_map/pallas_call | solution.py:515
  149.2 6.4 %shard_map.135 = bf16[16,128,8,128]{3,2,1,0:T(8,128)(2,1)} custom-call(bf16[16,4,2,128,128]{4,3,2,1,0:T(8,128)(2,1)S(1)} %get-tuple-element.116.mixed_ref), custom_call_target="tpu_custom_call" | custom-call | flops 1000 | bytes 1000 | tf_op jit(solution)/shard_map/pallas_call | solution.py:593
  155.7 3.4 %shard_map.136.refs_1_ = f32[16,8,128,128]{3,2,1,0:T(8,128)} custom-call(s32[257]{0:T(512)S(1)} %concatenate.11.flat, s32[4,264,128]{2,1,0:T(8,128)S(1)} %collective-permute-done.6.refs_0_, s32[4,264,128]{2,1,0:T(8,128)S(1)} %collective-permute-done.7.refs_1_, s32[4,264,128]{2,1,0:T(8,128)S(1)} %collective-permute-done.8.refs_2_, ...), custom_call_target="tpu_custom_call", output_to_operand_aliasing={{}: (4, {})} | custom-call | flops 1000 | bytes 1000 | tf_op jit(solution)/shard_map/pallas_call | solution.py:566
  162.3 11.0 %collective-permute-done.9.refs_0_ = s32[4,264,128]{2,1,0:T(8,128)S(1)} collective-permute-done((s32[4,264,128]{2,1,0:T(8,128)S(1)}, s32[4,264,128]{2,1,0:T(8,128)S(1)}, u32[]{:S(2)}, u32[]{:S(2)}) %collective-permute-start.9) | collective-permute-done | bytes 540704 | tf_op jit(solution)/shard_map/ppermute | solution.py:628
  (45 shorter events, 19.9 us)
Async XLA Ops:
  0.6 1.6 copy-start.2
  2.8 28.2 %collective-permute-start = (s32[4,264,128]{2,1,0:T(8,128)S(1)}, s32[4,264,128]{2,1,0:T(8,128)}, u32[]{:S(2)}, u32[]{:S(2)}) collective-permute-start(s32[4,264,128]{2,1,0:T(8,128)S(1)} %get-tuple-element.88.refs_12_), channel_id=1, source_target_pairs={{0,8},{4,12},{8,0},{12,4},{1,9},{5,13},{9,1},{13,5},{2,10},{6,14},... | collective-permute-start | bytes 1622024 | tf_op jit(solution)/shard_map/ppermute | solution.py:628
  9.1 46.7 %collective-permute-start.1 = (s32[4,264,128]{2,1,0:T(8,128)S(1)}, s32[4,264,128]{2,1,0:T(8,128)}, u32[]{:S(2)}, u32[]{:S(2)}) collective-permute-start(s32[4,264,128]{2,1,0:T(8,128)S(1)} %get-tuple-element.88.refs_12_), channel_id=1, source_target_pairs={{0,4},{4,0},{8,12},{12,8},{1,5},{5,1},{9,13},{13,9},{2,6},{6,2},{1... | collective-permute-start | bytes 1622024 | tf_op jit(solution)/shard_map/ppermute | solution.py:628
  10.7 3.6 %copy-start.4 = (bf16[16,128,4,2,128]{4,3,2,1,0:T(2,128)(2,1)S(1)}, bf16[16,128,4,2,128]{4,3,2,1,0:T(2,128)(2,1)}, u32[]{:S(2)}) copy-start(bf16[16,128,4,2,128]{4,3,2,1,0:T(2,128)(2,1)} %param.13) | copy-start | bytes 12582916
  14.4 3.3 %copy-start.7 = (s32[64]{0:T(128)S(1)}, s32[64]{0:T(128)}, u32[]{:S(2)}) copy-start(s32[64]{0:T(128)} %param.18) | copy-start | bytes 772
  14.4 3.3 %copy-start.8 = (s32[64]{0:T(128)S(1)}, s32[64]{0:T(128)}, u32[]{:S(2)}) copy-start(s32[64]{0:T(128)} %param.19) | copy-start | bytes 772
  14.4 3.3 %copy-start.9 = (s32[64]{0:T(128)S(1)}, s32[64]{0:T(128)}, u32[]{:S(2)}) copy-start(s32[64]{0:T(128)} %param.20) | copy-start | bytes 772
  14.4 3.3 %copy-start.10 = (s32[64]{0:T(128)S(1)}, s32[64]{0:T(128)}, u32[]{:S(2)}) copy-start(s32[64]{0:T(128)} %param.21) | copy-start | bytes 772
  14.4 3.4 %copy-start.5 = (bf16[16,128,4,2]{1,3,2,0:T(2,128)(2,1)S(1)}, bf16[16,128,4,2]{1,3,2,0:T(2,128)(2,1)}, u32[]{:S(2)}) copy-start(bf16[16,128,4,2]{1,3,2,0:T(2,128)(2,1)} %param.15) | copy-start | bytes 98308
  14.4 3.4 %copy-start.6 = (bf16[16,128,4,2]{1,3,2,0:T(2,128)(2,1)S(1)}, bf16[16,128,4,2]{1,3,2,0:T(2,128)(2,1)}, u32[]{:S(2)}) copy-start(bf16[16,128,4,2]{1,3,2,0:T(2,128)(2,1)} %param.14) | copy-start | bytes 98308
  17.8 1.6 copy-start.1
  31.0 25.5 %collective-permute-start.2 = (s32[4,264,128]{2,1,0:T(8,128)}, s32[4,264,128]{2,1,0:T(8,128)S(1)}, u32[]{:S(2)}, u32[]{:S(2)}) collective-permute-start(s32[4,264,128]{2,1,0:T(8,128)} %collective-permute-done.refs_14_), channel_id=1, source_target_pairs={{0,4},{4,0},{8,12},{12,8},{1,5},{5,1},{9,13},{13,9},{2,6},{6,2},{1... | collective-permute-start | bytes 1622024 | tf_op jit(solution)/shard_map/ppermute | solution.py:628
  31.6 27.3 %collective-permute-start.3 = (s32[4,264,128]{2,1,0:T(8,128)S(1)}, s32[4,264,128]{2,1,0:T(8,128)S(1)}, u32[]{:S(2)}, u32[]{:S(2)}) collective-permute-start(s32[4,264,128]{2,1,0:T(8,128)S(1)} %get-tuple-element.102.refs_12_), channel_id=1, source_target_pairs={{0,8},{4,12},{8,0},{12,4},{1,9},{5,13},{9,1},{13,5},{2,10},{6,14},... | collective-permute-start | bytes 1622024 | tf_op jit(solution)/shard_map/ppermute | solution.py:628
  45.5 13.4 %copy-start = (bf16[16,128,4,2,128]{4,1,3,2,0:T(8,128)(2,1)S(1)}, bf16[16,128,4,2,128]{4,1,3,2,0:T(8,128)(2,1)}, u32[]{:S(2)}) copy-start(bf16[16,128,4,2,128]{4,1,3,2,0:T(8,128)(2,1)} %copy.35) | copy-start | bytes 12582916
  45.5 13.4 %copy-start.3 = (bf16[128]{0:T(256)(128)(2,1)S(1)}, bf16[128]{0:T(256)(128)(2,1)}, u32[]{:S(2)}) copy-start(bf16[128]{0:T(256)(128)(2,1)} %param.16) | copy-start | bytes 772
  64.7 28.9 %collective-permute-start.6 = (s32[4,264,128]{2,1,0:T(8,128)S(1)}, s32[4,264,128]{2,1,0:T(8,128)S(1)}, u32[]{:S(2)}, u32[]{:S(2)}) collective-permute-start(s32[4,264,128]{2,1,0:T(8,128)S(1)} %get-tuple-element.105), channel_id=1, source_target_pairs={{0,12},{4,8},{8,4},{12,0},{1,13},{5,9},{9,5},{13,1},{2,14},{6,10},... | collective-permute-start | bytes 1622024 | tf_op jit(solution)/shard_map/ppermute | solution.py:628
  67.3 34.9 %collective-permute-start.4 = (s32[4,264,128]{2,1,0:T(8,128)S(1)}, s32[4,264,128]{2,1,0:T(8,128)S(1)}, u32[]{:S(2)}, u32[]{:S(2)}) collective-permute-start(s32[4,264,128]{2,1,0:T(8,128)S(1)} %get-tuple-element.102.refs_12_), channel_id=1, source_target_pairs={{0,4},{4,0},{8,12},{12,8},{1,5},{5,1},{9,13},{13,9},{2,6},{6,2},{1... | collective-permute-start | bytes 1622024 | tf_op jit(solution)/shard_map/ppermute | solution.py:628
  67.3 46.5 %collective-permute-start.5 = (s32[4,264,128]{2,1,0:T(8,128)S(1)}, s32[4,264,128]{2,1,0:T(8,128)S(1)}, u32[]{:S(2)}, u32[]{:S(2)}) collective-permute-start(s32[4,264,128]{2,1,0:T(8,128)S(1)} %collective-permute-done.3.refs_14_), channel_id=1, source_target_pairs={{0,4},{4,0},{8,12},{12,8},{1,5},{5,1},{9,13},{13,9},{2,6},{6,2},{1... | collective-permute-start | bytes 1622024 | tf_op jit(solution)/shard_map/ppermute | solution.py:628
  81.4 54.4 %collective-permute-start.8 = (s32[4,264,128]{2,1,0:T(8,128)S(1)}, s32[4,264,128]{2,1,0:T(8,128)S(1)}, u32[]{:S(2)}, u32[]{:S(2)}) collective-permute-start(s32[4,264,128]{2,1,0:T(8,128)S(1)} %get-tuple-element.112), channel_id=1, source_target_pairs={{0,4},{4,0},{8,12},{12,8},{1,5},{5,1},{9,13},{13,9},{2,6},{6,2},{1... | collective-permute-start | bytes 1622024 | tf_op jit(solution)/shard_map/ppermute | solution.py:628
  81.5 54.3 %collective-permute-start.7 = (s32[4,264,128]{2,1,0:T(8,128)S(1)}, s32[4,264,128]{2,1,0:T(8,128)S(1)}, u32[]{:S(2)}, u32[]{:S(2)}) collective-permute-start(s32[4,264,128]{2,1,0:T(8,128)S(1)} %get-tuple-element.110), channel_id=1, source_target_pairs={{0,8},{4,12},{8,0},{12,4},{1,9},{5,13},{9,1},{13,5},{2,10},{6,14},... | collective-permute-start | bytes 1622024 | tf_op jit(solution)/shard_map/ppermute | solution.py:628
  125.4 35.3 %collective-permute-start.10 = (s32[4,264,128]{2,1,0:T(8,128)S(1)}, s32[4,264,128]{2,1,0:T(8,128)S(1)}, u32[]{:S(2)}, u32[]{:S(2)}) collective-permute-start(s32[4,264,128]{2,1,0:T(8,128)S(1)} %get-tuple-element.118), channel_id=1, source_target_pairs={{0,12},{4,8},{8,4},{12,0},{1,13},{5,9},{9,5},{13,1},{2,14},{6,10},... | collective-permute-start | bytes 1622024 | tf_op jit(solution)/shard_map/ppermute | solution.py:628
  129.1 30.0 %collective-permute-start.11 = (s32[4,264,128]{2,1,0:T(8,128)S(1)}, s32[4,264,128]{2,1,0:T(8,128)S(1)}, u32[]{:S(2)}, u32[]{:S(2)}) collective-permute-start(s32[4,264,128]{2,1,0:T(8,128)S(1)} %get-tuple-element.119), channel_id=1, source_target_pairs={{0,4},{4,0},{8,12},{12,8},{1,5},{5,1},{9,13},{13,9},{2,6},{6,2},{1... | collective-permute-start | bytes 1622024 | tf_op jit(solution)/shard_map/ppermute | solution.py:628
  134.9 38.5 %collective-permute-start.9 = (s32[4,264,128]{2,1,0:T(8,128)S(1)}, s32[4,264,128]{2,1,0:T(8,128)S(1)}, u32[]{:S(2)}, u32[]{:S(2)}) collective-permute-start(s32[4,264,128]{2,1,0:T(8,128)S(1)} %get-tuple-element.117), channel_id=1, source_target_pairs={{0,8},{4,12},{8,0},{12,4},{1,9},{5,13},{9,1},{13,5},{2,10},{6,14},... | collective-permute-start | bytes 1622024 | tf_op jit(solution)/shard_map/ppermute | solution.py:628

commit v4 on v3

--- a/solution.py
+++ b/solution.py
@@ -683,14 +683,17 @@
             mixed, arrived[0, away] = lax.optimization_barrier((mixed, arrived[0, away]))
         return mixed
 
-    for away in crossing + near:
+    for away in crossing:
         mixed, final = work(0, [away], mixed, final)
     rates, mixed, pairs[1] = lax.optimization_barrier((rates, mixed, pairs[1]))
     pairs[1] = pair_parts(1, 1, plan, flat, q, k, rates, pairs[1])
+    for away in near:
+        mixed, final = work(0, [away], mixed, final)
+    mixed, pairs[1], gathered[1] = lax.optimization_barrier((mixed, pairs[1], gathered[1]))
     mixed = gone(mixed, crossing[:1])
     for away in near + crossing:
         mixed, final = work(1, [away], mixed, final)
-    mixed = gone(mixed, crossing[1:] + near)
+    mixed = gone(mixed, crossing[1:])
     for part in range(PARTS):
         mixed, final = work(part, [0], mixed, final)
     away_first = crossing + near

time: 175 us -> 166 us (0.949)
  waiting for transfers between devices: 35.5 us -> 26.1 us
    ppermute x12, waiting for transfers between devices: 35.5 us -> 26.1 us  [swap(): return lax.ppermute(tensor, 'seq', [(i, i ^ off) for i in range(seq_count)])]
  transfers between devices with their start and end apart: 12 -> 12, of which waited for: 6 -> 5; matrix products, arithmetic and copies ran while one was open for 5% -> 6% of each run, Pallas kernels for 56% -> 62%
where the time goes in v4:
time: 166 us
  Pallas kernels  104 us (63%)
  waiting for transfers between devices  26.1 us (16%)
  starting transfers between devices  22 us (13%)
  local copies, waits for them, and re-layouts  12.3 us (7%)
    pallas_call x8, Pallas kernels, recurrence(): pl.pallas_call(functools.partial(state_kernel, part, aways, plan, len(par...  47.7 us
    pallas_call x4, Pallas kernels, pair_parts(): pl.pallas_call(functools.partial(pair_kernel, part, first, plan), grid_sp...  41.3 us
    ppermute x12, waiting for transfers between devices, swap(): return lax.ppermute(tensor, 'seq', [(i, i ^ off) for i in range(seq_count)])  26.1 us
    ppermute x12, starting transfers between devices, swap(): return lax.ppermute(tensor, 'seq', [(i, i ^ off) for i in range(seq_count)])  22 us
    unnamed x25, local copies, waits for them, and re-layouts  12.2 us
    pallas_call x4, Pallas kernels, unpack_states(): pl.pallas_call(functools.partial(unpack_kernel, turns), grid_spec=pltpu.P...  8.29 us
    pallas_call x1, Pallas kernels, turn_mixed(): pl.pallas_call(turn_kernel, grid=(count,), in_specs=[pl.BlockSpec((1, key...  6.44 us
  transfers between devices with their start and end apart: 12, of which 5 were waited for; matrix products, arithmetic and copies ran while one was open for 6% of the time, Pallas kernels for 62%

profile of v4, /device:TPU:0, one launch (start us, length us, event | category | flops | bytes accessed | tf_op | source)
XLA Modules:
  0.0 165.6 jit_solution(10550484836826037117)
XLA Ops:
  2.8 4.1 %collective-permute-start = (s32[4,264,128]{2,1,0:T(8,128)S(1)}, s32[4,264,128]{2,1,0:T(8,128)}, u32[]{:S(2)}, u32[]{:S(2)}) collective-permute-start(s32[4,264,128]{2,1,0:T(8,128)S(1)} %get-tuple-element.93.refs_12_), channel_id=1, source_target_pairs={{0,8},{4,12},{8,0},{12,4},{1,9},{5,13},{9,1},{13,5},{2,10},{6,14},... | collective-permute-start | bytes 1622024 | tf_op jit(solution)/shard_map/ppermute | solution.py:628
  6.9 2.1 %copy.37 = bf16[16,128,4,128]{3,1,2,0:T(8,128)(2,1)S(1)} copy(bf16[16,128,4,128]{3,2,1,0:T(4,128)(2,1)} %param.11) | data formatting | bytes 4194304 | tf_op args[0]
  10.7 3.6 %copy.36 = bf16[16,128,4,128]{3,1,2,0:T(8,128)(2,1)} copy(bf16[16,128,4,128]{3,2,1,0:T(4,128)(2,1)} %param.12) | data formatting | bytes 4194304 | tf_op args[1]
  14.4 3.3 %copy.35 = bf16[16,128,4,2,128]{4,1,3,2,0:T(8,128)(2,1)} copy(bf16[16,128,4,2,128]{4,3,2,1,0:T(2,128)(2,1)S(1)} %copy-done.4) | data formatting | bytes 8388608 | tf_op args[2]
  19.4 10.3 %shard_map.123 = (bf16[16,4,128,128]{3,2,1,0:T(8,128)(2,1)S(1)}, bf16[16,4,256,256]{3,2,1,0:T(8,128)(2,1)S(1)}) custom-call(s32[257]{0:T(512)S(1)} %concatenate.11.flat, bf16[16,4,128,128]{3,2,1,0:T(8,128)(2,1)S(1)} %bitcast.36, bf16[16,4,128,128]{3,2,1,0:T(8,128)(2,1)S(1)} %bitcast.56, f32[16,16,128]{2,1,0:T(8,128)S(1)} %maximum_convert_fusion.rate_ref.refs_3_.refs_9_), custom_call_target="tpu_custom_call" | custom-call | flops 1000 | bytes 1000 | tf_op jit(solution)/shard_map/pallas_call | solution.py:257
  31.6 3.5 %collective-permute-start.3 = (s32[4,264,128]{2,1,0:T(8,128)S(1)}, s32[4,264,128]{2,1,0:T(8,128)S(1)}, u32[]{:S(2)}, u32[]{:S(2)}) collective-permute-start(s32[4,264,128]{2,1,0:T(8,128)S(1)} %get-tuple-element.112.refs_12_), channel_id=1, source_target_pairs={{0,8},{4,12},{8,0},{12,4},{1,9},{5,13},{9,1},{13,5},{2,10},{6,14},... | collective-permute-start | bytes 1622024 | tf_op jit(solution)/shard_map/ppermute | solution.py:628
  35.1 10.3 %shard_map.124 = (bf16[16,4,128,128]{3,2,1,0:T(8,128)(2,1)S(1)}, bf16[16,4,256,256]{3,2,1,0:T(8,128)(2,1)S(1)}) custom-call(s32[257]{0:T(512)S(1)} %concatenate.11.flat, bf16[16,4,128,128]{3,2,1,0:T(8,128)(2,1)S(1)} %bitcast.37, bf16[16,4,128,128]{3,2,1,0:T(8,128)(2,1)S(1)} %bitcast.57, ...), custom_call_target="tpu_custom_call", output_to_operand_aliasing={{0}: (4, {}), {1}: (5, {})} | custom-call | flops 1000 | bytes 1000 | tf_op jit(solution)/shard_map/pallas_call | solution.py:257
  45.5 10.3 %shard_map.125 = (bf16[16,4,128,128]{3,2,1,0:T(8,128)(2,1)S(1)}, bf16[16,4,256,256]{3,2,1,0:T(8,128)(2,1)S(1)}) custom-call(s32[257]{0:T(512)S(1)} %concatenate.11.flat, bf16[16,4,128,128]{3,2,1,0:T(8,128)(2,1)S(1)} %bitcast.38, bf16[16,4,128,128]{3,2,1,0:T(8,128)(2,1)S(1)} %bitcast.58, f32[16,16,128]{2,1,0:T(8,128)S(1)} %maximum_convert_fusion.rate_ref.refs_3_.refs_9_), custom_call_target="tpu_custom_call" | custom-call | flops 1000 | bytes 1000 | tf_op jit(solution)/shard_map/pallas_call | solution.py:257
  56.5 2.4 %collective-permute-done.3.refs_14_ = s32[4,264,128]{2,1,0:T(8,128)S(1)} collective-permute-done((s32[4,264,128]{2,1,0:T(8,128)S(1)}, s32[4,264,128]{2,1,0:T(8,128)S(1)}, u32[]{:S(2)}, u32[]{:S(2)}) %collective-permute-start.3) | collective-permute-done | bytes 540704 | tf_op jit(solution)/shard_map/ppermute | solution.py:628
  60.9 5.6 %shard_map.126 = (bf16[16,4,2,128,128]{4,3,2,1,0:T(8,128)(2,1)S(1)}, s32[4,264,128]{2,1,0:T(8,128)S(1)}) custom-call(s32[257]{0:T(512)S(1)} %concatenate.11.flat, bf16[1,128]{1,0:T(2,128)(2,1)S(1)} %bitcast.77, bf16[16,4,128,128]{3,2,1,0:T(8,128)(2,1)S(1)} %bitcast.39, bf16[16,4,128,128]{3,2,1,0:T(8,128)(2,1)S(1)} %bitcast.59, ...), custom_call_target="tpu_custom_call" | custom-call | flops 1000 | bytes 1000 | tf_op jit(solution)/shard_map/pallas_call | solution.py:515
  66.5 2.7 %collective-permute-start.6 = (s32[4,264,128]{2,1,0:T(8,128)S(1)}, s32[4,264,128]{2,1,0:T(8,128)S(1)}, u32[]{:S(2)}, u32[]{:S(2)}) collective-permute-start(s32[4,264,128]{2,1,0:T(8,128)S(1)} %get-tuple-element.117), channel_id=1, source_target_pairs={{0,12},{4,8},{8,4},{12,0},{1,13},{5,9},{9,5},{13,1},{2,14},{6,10},... | collective-permute-start | bytes 1622024 | tf_op jit(solution)/shard_map/ppermute | solution.py:628
  69.3 5.8 %shard_map.127 = (bf16[16,4,2,128,128]{4,3,2,1,0:T(8,128)(2,1)S(1)}, s32[4,264,128]{2,1,0:T(8,128)S(1)}) custom-call(s32[257]{0:T(512)S(1)} %concatenate.11.flat, bf16[1,128]{1,0:T(2,128)(2,1)S(1)} %bitcast.78, bf16[16,4,128,128]{3,2,1,0:T(8,128)(2,1)S(1)} %bitcast.41, bf16[16,4,128,128]{3,2,1,0:T(8,128)(2,1)S(1)} %bitcast.61, ...), custom_call_target="tpu_custom_call", output_to_operand_aliasing={{0}: (18, {})} | custom-call | flops 1000 | bytes 1000 | tf_op jit(solution)/shard_map/pallas_call | solution.py:515
  75.1 5.8 %shard_map.128 = (bf16[16,4,2,128,128]{4,3,2,1,0:T(8,128)(2,1)S(1)}, s32[4,264,128]{2,1,0:T(8,128)S(1)}) custom-call(s32[257]{0:T(512)S(1)} %concatenate.11.flat, bf16[1,128]{1,0:T(2,128)(2,1)S(1)} %bitcast.79, bf16[16,4,128,128]{3,2,1,0:T(8,128)(2,1)S(1)} %bitcast.43, bf16[16,4,128,128]{3,2,1,0:T(8,128)(2,1)S(1)} %bitcast.63, ...), custom_call_target="tpu_custom_call", output_to_operand_aliasing={{0}: (18, {})} | custom-call | flops 1000 | bytes 1000 | tf_op jit(solution)/shard_map/pallas_call | solution.py:515
  83.0 10.3 %shard_map.129 = (bf16[16,4,128,128]{3,2,1,0:T(8,128)(2,1)S(1)}, bf16[16,4,256,256]{3,2,1,0:T(8,128)(2,1)S(1)}) custom-call(s32[257]{0:T(512)S(1)} %concatenate.11.flat, bf16[16,4,128,128]{3,2,1,0:T(8,128)(2,1)S(1)} %bitcast.45, bf16[16,4,128,128]{3,2,1,0:T(8,128)(2,1)S(1)} %bitcast.65, ...), custom_call_target="tpu_custom_call", output_to_operand_aliasing={{0}: (4, {}), {1}: (5, {})} | custom-call | flops 1000 | bytes 1000 | tf_op jit(solution)/shard_map/pallas_call | solution.py:257
  93.4 13.3 %collective-permute-done.5.refs_15_ = s32[4,264,128]{2,1,0:T(8,128)S(1)} collective-permute-done((s32[4,264,128]{2,1,0:T(8,128)S(1)}, s32[4,264,128]{2,1,0:T(8,128)S(1)}, u32[]{:S(2)}, u32[]{:S(2)}) %collective-permute-start.5) | collective-permute-done | bytes 540704 | tf_op jit(solution)/shard_map/ppermute | solution.py:628
  106.6 5.8 %shard_map.130 = (bf16[16,4,2,128,128]{4,3,2,1,0:T(8,128)(2,1)S(1)}, s32[4,264,128]{2,1,0:T(8,128)S(1)}) custom-call(s32[257]{0:T(512)S(1)} %concatenate.11.flat, bf16[1,128]{1,0:T(2,128)(2,1)S(1)} %bitcast.80, bf16[16,4,128,128]{3,2,1,0:T(8,128)(2,1)S(1)} %bitcast.46, bf16[16,4,128,128]{3,2,1,0:T(8,128)(2,1)S(1)} %bitcast.66, ...), custom_call_target="tpu_custom_call", output_to_operand_aliasing={{0}: (18, {})} | custom-call | flops 1000 | bytes 1000 | tf_op jit(solution)/shard_map/pallas_call | solution.py:515
  112.5 5.8 %shard_map.131 = (bf16[16,4,2,128,128]{4,3,2,1,0:T(8,128)(2,1)S(1)}, s32[4,264,128]{2,1,0:T(8,128)S(1)}) custom-call(s32[257]{0:T(512)S(1)} %concatenate.11.flat, bf16[1,128]{1,0:T(2,128)(2,1)S(1)} %bitcast.81, bf16[16,4,128,128]{3,2,1,0:T(8,128)(2,1)S(1)} %bitcast.48, bf16[16,4,128,128]{3,2,1,0:T(8,128)(2,1)S(1)} %bitcast.68, ...), custom_call_target="tpu_custom_call", output_to_operand_aliasing={{0}: (18, {})} | custom-call | flops 1000 | bytes 1000 | tf_op jit(solution)/shard_map/pallas_call | solution.py:515
  118.3 4.6 %collective-permute-start.9 = (s32[4,264,128]{2,1,0:T(8,128)S(1)}, s32[4,264,128]{2,1,0:T(8,128)S(1)}, u32[]{:S(2)}, u32[]{:S(2)}) collective-permute-start(s32[4,264,128]{2,1,0:T(8,128)S(1)} %get-tuple-element.128), channel_id=1, source_target_pairs={{0,12},{4,8},{8,4},{12,0},{1,13},{5,9},{9,5},{13,1},{2,14},{6,10},... | collective-permute-start | bytes 1622024 | tf_op jit(solution)/shard_map/ppermute | solution.py:628
  122.9 5.8 %shard_map.132 = (bf16[16,4,2,128,128]{4,3,2,1,0:T(8,128)(2,1)S(1)}, s32[4,264,128]{2,1,0:T(8,128)S(1)}) custom-call(s32[257]{0:T(512)S(1)} %concatenate.11.flat, bf16[1,128]{1,0:T(2,128)(2,1)S(1)} %bitcast.82, bf16[16,4,128,128]{3,2,1,0:T(8,128)(2,1)S(1)} %bitcast.50, bf16[16,4,128,128]{3,2,1,0:T(8,128)(2,1)S(1)} %bitcast.70, ...), custom_call_target="tpu_custom_call", output_to_operand_aliasing={{0}: (18, {})} | custom-call | flops 1000 | bytes 1000 | tf_op jit(solution)/shard_map/pallas_call | solution.py:515
  129.5 6.3 %shard_map.133 = (bf16[16,4,2,128,128]{4,3,2,1,0:T(8,128)(2,1)S(1)}, f32[16,8,128,128]{3,2,1,0:T(8,128)}) custom-call(s32[257]{0:T(512)S(1)} %concatenate.11.flat, bf16[1,128]{1,0:T(2,128)(2,1)S(1)} %bitcast.83, bf16[16,4,128,128]{3,2,1,0:T(8,128)(2,1)S(1)} %bitcast.52, bf16[16,4,128,128]{3,2,1,0:T(8,128)(2,1)S(1)} %bitcast.72, ...), custom_call_target="tpu_custom_call", output_to_operand_aliasing={{0}: (18, {})} | custom-call | flops 1000 | bytes 1000 | tf_op jit(solution)/shard_map/pallas_call | solution.py:515
  135.7 6.7 %shard_map.134 = (bf16[16,4,2,128,128]{4,3,2,1,0:T(8,128)(2,1)S(1)}, f32[16,8,128,128]{3,2,1,0:T(8,128)}) custom-call(s32[257]{0:T(512)S(1)} %concatenate.11.flat, bf16[1,128]{1,0:T(2,128)(2,1)S(1)} %bitcast.84, bf16[16,4,128,128]{3,2,1,0:T(8,128)(2,1)S(1)} %bitcast.54, ...), custom_call_target="tpu_custom_call", output_to_operand_aliasing={{0}: (18, {}), {1}: (19, {})} | custom-call | flops 1000 | bytes 1000 | tf_op jit(solution)/shard_map/pallas_call | solution.py:515
  142.4 6.4 %shard_map.135 = bf16[16,128,8,128]{3,2,1,0:T(8,128)(2,1)} custom-call(bf16[16,4,2,128,128]{4,3,2,1,0:T(8,128)(2,1)S(1)} %get-tuple-element.126.mixed_ref), custom_call_target="tpu_custom_call" | custom-call | flops 1000 | bytes 1000 | tf_op jit(solution)/shard_map/pallas_call | solution.py:593
  148.8 3.4 %shard_map.136.refs_1_ = f32[16,8,128,128]{3,2,1,0:T(8,128)} custom-call(s32[257]{0:T(512)S(1)} %concatenate.11.flat, s32[4,264,128]{2,1,0:T(8,128)S(1)} %collective-permute-done.6.refs_0_, s32[4,264,128]{2,1,0:T(8,128)S(1)} %collective-permute-done.7.refs_1_, s32[4,264,128]{2,1,0:T(8,128)S(1)} %collective-permute-done.11.refs_2_, ...), custom_call_target="tpu_custom_call", output_to_operand_aliasing={{}: (4, {})} | custom-call | flops 1000 | bytes 1000 | tf_op jit(solution)/shard_map/pallas_call | solution.py:566
  155.5 8.4 %collective-permute-done.8.refs_0_ = s32[4,264,128]{2,1,0:T(8,128)S(1)} collective-permute-done((s32[4,264,128]{2,1,0:T(8,128)S(1)}, s32[4,264,128]{2,1,0:T(8,128)S(1)}, u32[]{:S(2)}, u32[]{:S(2)}) %collective-permute-start.8) | collective-permute-done | bytes 540704 | tf_op jit(solution)/shard_map/ppermute | solution.py:628
  (45 shorter events, 17.8 us)
Async XLA Ops:
  0.6 1.6 copy-start.2
  2.8 28.2 %collective-permute-start = (s32[4,264,128]{2,1,0:T(8,128)S(1)}, s32[4,264,128]{2,1,0:T(8,128)}, u32[]{:S(2)}, u32[]{:S(2)}) collective-permute-start(s32[4,264,128]{2,1,0:T(8,128)S(1)} %get-tuple-element.93.refs_12_), channel_id=1, source_target_pairs={{0,8},{4,12},{8,0},{12,4},{1,9},{5,13},{9,1},{13,5},{2,10},{6,14},... | collective-permute-start | bytes 1622024 | tf_op jit(solution)/shard_map/ppermute | solution.py:628
  9.1 46.7 %collective-permute-start.1 = (s32[4,264,128]{2,1,0:T(8,128)S(1)}, s32[4,264,128]{2,1,0:T(8,128)}, u32[]{:S(2)}, u32[]{:S(2)}) collective-permute-start(s32[4,264,128]{2,1,0:T(8,128)S(1)} %get-tuple-element.93.refs_12_), channel_id=1, source_target_pairs={{0,4},{4,0},{8,12},{12,8},{1,5},{5,1},{9,13},{13,9},{2,6},{6,2},{1... | collective-permute-start | bytes 1622024 | tf_op jit(solution)/shard_map/ppermute | solution.py:628
  10.7 3.6 %copy-start.4 = (bf16[16,128,4,2,128]{4,3,2,1,0:T(2,128)(2,1)S(1)}, bf16[16,128,4,2,128]{4,3,2,1,0:T(2,128)(2,1)}, u32[]{:S(2)}) copy-start(bf16[16,128,4,2,128]{4,3,2,1,0:T(2,128)(2,1)} %param.13) | copy-start | bytes 12582916
  14.4 3.3 %copy-start.7 = (s32[64]{0:T(128)S(1)}, s32[64]{0:T(128)}, u32[]{:S(2)}) copy-start(s32[64]{0:T(128)} %param.18) | copy-start | bytes 772
  14.4 3.3 %copy-start.8 = (s32[64]{0:T(128)S(1)}, s32[64]{0:T(128)}, u32[]{:S(2)}) copy-start(s32[64]{0:T(128)} %param.19) | copy-start | bytes 772
  14.4 3.3 %copy-start.9 = (s32[64]{0:T(128)S(1)}, s32[64]{0:T(128)}, u32[]{:S(2)}) copy-start(s32[64]{0:T(128)} %param.20) | copy-start | bytes 772
  14.4 3.3 %copy-start.10 = (s32[64]{0:T(128)S(1)}, s32[64]{0:T(128)}, u32[]{:S(2)}) copy-start(s32[64]{0:T(128)} %param.21) | copy-start | bytes 772
  14.4 3.4 %copy-start.5 = (bf16[16,128,4,2]{1,3,2,0:T(2,128)(2,1)S(1)}, bf16[16,128,4,2]{1,3,2,0:T(2,128)(2,1)}, u32[]{:S(2)}) copy-start(bf16[16,128,4,2]{1,3,2,0:T(2,128)(2,1)} %param.15) | copy-start | bytes 98308
  14.4 3.4 %copy-start.6 = (bf16[16,128,4,2]{1,3,2,0:T(2,128)(2,1)S(1)}, bf16[16,128,4,2]{1,3,2,0:T(2,128)(2,1)}, u32[]{:S(2)}) copy-start(bf16[16,128,4,2]{1,3,2,0:T(2,128)(2,1)} %param.14) | copy-start | bytes 98308
  17.8 1.6 copy-start.1
  31.0 25.5 %collective-permute-start.2 = (s32[4,264,128]{2,1,0:T(8,128)}, s32[4,264,128]{2,1,0:T(8,128)S(1)}, u32[]{:S(2)}, u32[]{:S(2)}) collective-permute-start(s32[4,264,128]{2,1,0:T(8,128)} %collective-permute-done.refs_14_), channel_id=1, source_target_pairs={{0,4},{4,0},{8,12},{12,8},{1,5},{5,1},{9,13},{13,9},{2,6},{6,2},{1... | collective-permute-start | bytes 1622024 | tf_op jit(solution)/shard_map/ppermute | solution.py:628
  31.6 27.3 %collective-permute-start.3 = (s32[4,264,128]{2,1,0:T(8,128)S(1)}, s32[4,264,128]{2,1,0:T(8,128)S(1)}, u32[]{:S(2)}, u32[]{:S(2)}) collective-permute-start(s32[4,264,128]{2,1,0:T(8,128)S(1)} %get-tuple-element.112.refs_12_), channel_id=1, source_target_pairs={{0,8},{4,12},{8,0},{12,4},{1,9},{5,13},{9,1},{13,5},{2,10},{6,14},... | collective-permute-start | bytes 1622024 | tf_op jit(solution)/shard_map/ppermute | solution.py:628
  45.5 15.4 %copy-start = (bf16[16,128,4,2,128]{4,1,3,2,0:T(8,128)(2,1)S(1)}, bf16[16,128,4,2,128]{4,1,3,2,0:T(8,128)(2,1)}, u32[]{:S(2)}) copy-start(bf16[16,128,4,2,128]{4,1,3,2,0:T(8,128)(2,1)} %copy.35) | copy-start | bytes 12582916
  45.5 15.4 %copy-start.3 = (bf16[128]{0:T(256)(128)(2,1)S(1)}, bf16[128]{0:T(256)(128)(2,1)}, u32[]{:S(2)}) copy-start(bf16[128]{0:T(256)(128)(2,1)} %param.16) | copy-start | bytes 772
  58.9 34.5 %collective-permute-start.4 = (s32[4,264,128]{2,1,0:T(8,128)S(1)}, s32[4,264,128]{2,1,0:T(8,128)S(1)}, u32[]{:S(2)}, u32[]{:S(2)}) collective-permute-start(s32[4,264,128]{2,1,0:T(8,128)S(1)} %get-tuple-element.112.refs_12_), channel_id=1, source_target_pairs={{0,4},{4,0},{8,12},{12,8},{1,5},{5,1},{9,13},{13,9},{2,6},{6,2},{1... | collective-permute-start | bytes 1622024 | tf_op jit(solution)/shard_map/ppermute | solution.py:628
  59.4 47.2 %collective-permute-start.5 = (s32[4,264,128]{2,1,0:T(8,128)S(1)}, s32[4,264,128]{2,1,0:T(8,128)S(1)}, u32[]{:S(2)}, u32[]{:S(2)}) collective-permute-start(s32[4,264,128]{2,1,0:T(8,128)S(1)} %collective-permute-done.3.refs_14_), channel_id=1, source_target_pairs={{0,4},{4,0},{8,12},{12,8},{1,5},{5,1},{9,13},{13,9},{2,6},{6,2},{1... | collective-permute-start | bytes 1622024 | tf_op jit(solution)/shard_map/ppermute | solution.py:628
  66.5 40.1 %collective-permute-start.6 = (s32[4,264,128]{2,1,0:T(8,128)S(1)}, s32[4,264,128]{2,1,0:T(8,128)S(1)}, u32[]{:S(2)}, u32[]{:S(2)}) collective-permute-start(s32[4,264,128]{2,1,0:T(8,128)S(1)} %get-tuple-element.117), channel_id=1, source_target_pairs={{0,12},{4,8},{8,4},{12,0},{1,13},{5,9},{9,5},{13,1},{2,14},{6,10},... | collective-permute-start | bytes 1622024 | tf_op jit(solution)/shard_map/ppermute | solution.py:628
  80.9 67.9 %collective-permute-start.11 = (s32[4,264,128]{2,1,0:T(8,128)S(1)}, s32[4,264,128]{2,1,0:T(8,128)S(1)}, u32[]{:S(2)}, u32[]{:S(2)}) collective-permute-start(s32[4,264,128]{2,1,0:T(8,128)S(1)} %get-tuple-element.132), channel_id=1, source_target_pairs={{0,4},{4,0},{8,12},{12,8},{1,5},{5,1},{9,13},{13,9},{2,6},{6,2},{1... | collective-permute-start | bytes 1622024 | tf_op jit(solution)/shard_map/ppermute | solution.py:628
  81.0 48.5 %collective-permute-start.7 = (s32[4,264,128]{2,1,0:T(8,128)S(1)}, s32[4,264,128]{2,1,0:T(8,128)S(1)}, u32[]{:S(2)}, u32[]{:S(2)}) collective-permute-start(s32[4,264,128]{2,1,0:T(8,128)S(1)} %get-tuple-element.122), channel_id=1, source_target_pairs={{0,8},{4,12},{8,0},{12,4},{1,9},{5,13},{9,1},{13,5},{2,10},{6,14},... | collective-permute-start | bytes 1622024 | tf_op jit(solution)/shard_map/ppermute | solution.py:628
  118.3 35.6 %collective-permute-start.9 = (s32[4,264,128]{2,1,0:T(8,128)S(1)}, s32[4,264,128]{2,1,0:T(8,128)S(1)}, u32[]{:S(2)}, u32[]{:S(2)}) collective-permute-start(s32[4,264,128]{2,1,0:T(8,128)S(1)} %get-tuple-element.128), channel_id=1, source_target_pairs={{0,12},{4,8},{8,4},{12,0},{1,13},{5,9},{9,5},{13,1},{2,14},{6,10},... | collective-permute-start | bytes 1622024 | tf_op jit(solution)/shard_map/ppermute | solution.py:628
  122.9 29.3 %collective-permute-start.10 = (s32[4,264,128]{2,1,0:T(8,128)S(1)}, s32[4,264,128]{2,1,0:T(8,128)S(1)}, u32[]{:S(2)}, u32[]{:S(2)}) collective-permute-start(s32[4,264,128]{2,1,0:T(8,128)S(1)} %get-tuple-element.129), channel_id=1, source_target_pairs={{0,4},{4,0},{8,12},{12,8},{1,5},{5,1},{9,13},{13,9},{2,6},{6,2},{1... | collective-permute-start | bytes 1622024 | tf_op jit(solution)/shard_map/ppermute | solution.py:628
  128.7 35.2 %collective-permute-start.8 = (s32[4,264,128]{2,1,0:T(8,128)S(1)}, s32[4,264,128]{2,1,0:T(8,128)S(1)}, u32[]{:S(2)}, u32[]{:S(2)}) collective-permute-start(s32[4,264,128]{2,1,0:T(8,128)S(1)} %get-tuple-element.127), channel_id=1, source_target_pairs={{0,8},{4,12},{8,0},{12,4},{1,9},{5,13},{9,1},{13,5},{2,10},{6,14},... | collective-permute-start | bytes 1622024 | tf_op jit(solution)/shard_map/ppermute | solution.py:628

commit v5 on v4

--- a/solution.py
+++ b/solution.py
@@ -687,9 +687,15 @@
         mixed, final = work(0, [away], mixed, final)
     rates, mixed, pairs[1] = lax.optimization_barrier((rates, mixed, pairs[1]))
     pairs[1] = pair_parts(1, 1, plan, flat, q, k, rates, pairs[1])
+    held_back = []
     for away in near:
-        mixed, final = work(0, [away], mixed, final)
-    mixed, pairs[1], gathered[1] = lax.optimization_barrier((mixed, pairs[1], gathered[1]))
+        mixed, state = recurrence(
+            0, [away], plan, flat, q, k, v, rates, pairs[0], gathered[0], gain, mixed, final_shape, final
+        )
+        held_back.append(state)
+    mixed, pairs[1], gathered[1], held_back = lax.optimization_barrier((mixed, pairs[1], gathered[1], held_back))
+    for away, state in zip(near, held_back):
+        arrived[0, away] = swap(state, away)
     mixed = gone(mixed, crossing[:1])
     for away in near + crossing:
         mixed, final = work(1, [away], mixed, final)

time: 166 us -> 163 us (0.982)
  starting transfers between devices: 22 us -> 18.9 us
    ppermute x12, starting transfers between devices: 22 us -> 18.9 us  [swap(): return lax.ppermute(tensor, 'seq', [(i, i ^ off) for i in range(seq_count)])]
  transfers between devices with their start and end apart: 12 -> 12, of which waited for: 5 -> 5; matrix products, arithmetic and copies ran while one was open for 6% -> 6% of each run, Pallas kernels for 62% -> 63%
where the time goes in v5:
time: 163 us
  Pallas kernels  105 us (64%)
  waiting for transfers between devices  25.2 us (15%)
  starting transfers between devices  18.9 us (12%)
  local copies, waits for them, and re-layouts  12.3 us (8%)
    pallas_call x8, Pallas kernels, recurrence(): pl.pallas_call(functools.partial(state_kernel, part, aways, plan, len(par...  48.8 us
    pallas_call x4, Pallas kernels, pair_parts(): pl.pallas_call(functools.partial(pair_kernel, part, first, plan), grid_sp...  41.3 us
    ppermute x12, waiting for transfers between devices, swap(): return lax.ppermute(tensor, 'seq', [(i, i ^ off) for i in range(seq_count)])  25.2 us
    ppermute x12, starting transfers between devices, swap(): return lax.ppermute(tensor, 'seq', [(i, i ^ off) for i in range(seq_count)])  18.9 us
    unnamed x25, local copies, waits for them, and re-layouts  12.2 us
    pallas_call x4, Pallas kernels, unpack_states(): pl.pallas_call(functools.partial(unpack_kernel, turns), grid_spec=pltpu.P...  8.29 us
    pallas_call x1, Pallas kernels, turn_mixed(): pl.pallas_call(turn_kernel, grid=(count,), in_specs=[pl.BlockSpec((1, key...  6.44 us
  transfers between devices with their start and end apart: 12, of which 5 were waited for; matrix products, arithmetic and copies ran while one was open for 6% of the time, Pallas kernels for 63%

profile of v5, /device:TPU:0, one launch (start us, length us, event | category | flops | bytes accessed | tf_op | source)
XLA Modules:
  0.0 162.7 jit_solution(1698165149242328847)
XLA Ops:
  2.8 4.1 %collective-permute-start = (s32[4,264,128]{2,1,0:T(8,128)S(1)}, s32[4,264,128]{2,1,0:T(8,128)}, u32[]{:S(2)}, u32[]{:S(2)}) collective-permute-start(s32[4,264,128]{2,1,0:T(8,128)S(1)} %get-tuple-element.94.refs_12_), channel_id=1, source_target_pairs={{0,8},{4,12},{8,0},{12,4},{1,9},{5,13},{9,1},{13,5},{2,10},{6,14},... | collective-permute-start | bytes 1622024 | tf_op jit(solution)/shard_map/ppermute | solution.py:628
  6.9 2.1 %copy.37 = bf16[16,128,4,128]{3,1,2,0:T(8,128)(2,1)S(1)} copy(bf16[16,128,4,128]{3,2,1,0:T(4,128)(2,1)} %param.11) | data formatting | bytes 4194304 | tf_op args[0]
  10.7 3.6 %copy.36 = bf16[16,128,4,128]{3,1,2,0:T(8,128)(2,1)} copy(bf16[16,128,4,128]{3,2,1,0:T(4,128)(2,1)} %param.12) | data formatting | bytes 4194304 | tf_op args[1]
  14.4 3.3 %copy.35 = bf16[16,128,4,2,128]{4,1,3,2,0:T(8,128)(2,1)} copy(bf16[16,128,4,2,128]{4,3,2,1,0:T(2,128)(2,1)S(1)} %copy-done.4) | data formatting | bytes 8388608 | tf_op args[2]
  19.4 10.3 %shard_map.123 = (bf16[16,4,128,128]{3,2,1,0:T(8,128)(2,1)S(1)}, bf16[16,4,256,256]{3,2,1,0:T(8,128)(2,1)S(1)}) custom-call(s32[257]{0:T(512)S(1)} %concatenate.11.flat, bf16[16,4,128,128]{3,2,1,0:T(8,128)(2,1)S(1)} %bitcast.36, bf16[16,4,128,128]{3,2,1,0:T(8,128)(2,1)S(1)} %bitcast.56, f32[16,16,128]{2,1,0:T(8,128)S(1)} %maximum_convert_fusion.rate_ref.refs_3_.refs_9_), custom_call_target="tpu_custom_call" | custom-call | flops 1000 | bytes 1000 | tf_op jit(solution)/shard_map/pallas_call | solution.py:257
  31.6 3.5 %collective-permute-start.3 = (s32[4,264,128]{2,1,0:T(8,128)S(1)}, s32[4,264,128]{2,1,0:T(8,128)S(1)}, u32[]{:S(2)}, u32[]{:S(2)}) collective-permute-start(s32[4,264,128]{2,1,0:T(8,128)S(1)} %get-tuple-element.114.refs_12_), channel_id=1, source_target_pairs={{0,8},{4,12},{8,0},{12,4},{1,9},{5,13},{9,1},{13,5},{2,10},{6,14},... | collective-permute-start | bytes 1622024 | tf_op jit(solution)/shard_map/ppermute | solution.py:628
  35.1 10.3 %shard_map.124 = (bf16[16,4,128,128]{3,2,1,0:T(8,128)(2,1)S(1)}, bf16[16,4,256,256]{3,2,1,0:T(8,128)(2,1)S(1)}) custom-call(s32[257]{0:T(512)S(1)} %concatenate.11.flat, bf16[16,4,128,128]{3,2,1,0:T(8,128)(2,1)S(1)} %bitcast.37, bf16[16,4,128,128]{3,2,1,0:T(8,128)(2,1)S(1)} %bitcast.57, ...), custom_call_target="tpu_custom_call", output_to_operand_aliasing={{0}: (4, {}), {1}: (5, {})} | custom-call | flops 1000 | bytes 1000 | tf_op jit(solution)/shard_map/pallas_call | solution.py:257
  45.5 10.3 %shard_map.125 = (bf16[16,4,128,128]{3,2,1,0:T(8,128)(2,1)S(1)}, bf16[16,4,256,256]{3,2,1,0:T(8,128)(2,1)S(1)}) custom-call(s32[257]{0:T(512)S(1)} %concatenate.11.flat, bf16[16,4,128,128]{3,2,1,0:T(8,128)(2,1)S(1)} %bitcast.38, bf16[16,4,128,128]{3,2,1,0:T(8,128)(2,1)S(1)} %bitcast.58, f32[16,16,128]{2,1,0:T(8,128)S(1)} %maximum_convert_fusion.rate_ref.refs_3_.refs_9_), custom_call_target="tpu_custom_call" | custom-call | flops 1000 | bytes 1000 | tf_op jit(solution)/shard_map/pallas_call | solution.py:257
  56.5 2.4 %collective-permute-done.3.refs_14_ = s32[4,264,128]{2,1,0:T(8,128)S(1)} collective-permute-done((s32[4,264,128]{2,1,0:T(8,128)S(1)}, s32[4,264,128]{2,1,0:T(8,128)S(1)}, u32[]{:S(2)}, u32[]{:S(2)}) %collective-permute-start.3) | collective-permute-done | bytes 540704 | tf_op jit(solution)/shard_map/ppermute | solution.py:628
  60.9 6.1 %shard_map.126 = (bf16[16,4,2,128,128]{4,3,2,1,0:T(8,128)(2,1)S(1)}, s32[4,264,128]{2,1,0:T(8,128)S(1)}) custom-call(s32[257]{0:T(512)S(1)} %concatenate.11.flat, bf16[1,128]{1,0:T(2,128)(2,1)S(1)} %bitcast.77, bf16[16,4,128,128]{3,2,1,0:T(8,128)(2,1)S(1)} %bitcast.39, bf16[16,4,128,128]{3,2,1,0:T(8,128)(2,1)S(1)} %bitcast.59, ...), custom_call_target="tpu_custom_call" | custom-call | flops 1000 | bytes 1000 | tf_op jit(solution)/shard_map/pallas_call | solution.py:515
  67.0 2.4 %collective-permute-start.6 = (s32[4,264,128]{2,1,0:T(8,128)S(1)}, s32[4,264,128]{2,1,0:T(8,128)S(1)}, u32[]{:S(2)}, u32[]{:S(2)}) collective-permute-start(s32[4,264,128]{2,1,0:T(8,128)S(1)} %get-tuple-element.119), channel_id=1, source_target_pairs={{0,12},{4,8},{8,4},{12,0},{1,13},{5,9},{9,5},{13,1},{2,14},{6,10},... | collective-permute-start | bytes 1622024 | tf_op jit(solution)/shard_map/ppermute | solution.py:628
  69.4 5.9 %shard_map.127 = (bf16[16,4,2,128,128]{4,3,2,1,0:T(8,128)(2,1)S(1)}, s32[4,264,128]{2,1,0:T(8,128)S(1)}) custom-call(s32[257]{0:T(512)S(1)} %concatenate.11.flat, bf16[1,128]{1,0:T(2,128)(2,1)S(1)} %bitcast.78, bf16[16,4,128,128]{3,2,1,0:T(8,128)(2,1)S(1)} %bitcast.41, bf16[16,4,128,128]{3,2,1,0:T(8,128)(2,1)S(1)} %bitcast.61, ...), custom_call_target="tpu_custom_call", output_to_operand_aliasing={{0}: (18, {})} | custom-call | flops 1000 | bytes 1000 | tf_op jit(solution)/shard_map/pallas_call | solution.py:515
  75.5 6.0 %shard_map.128 = (bf16[16,4,2,128,128]{4,3,2,1,0:T(8,128)(2,1)S(1)}, s32[4,264,128]{2,1,0:T(8,128)S(1)}) custom-call(s32[257]{0:T(512)S(1)} %concatenate.11.flat, bf16[1,128]{1,0:T(2,128)(2,1)S(1)} %bitcast.79, bf16[16,4,128,128]{3,2,1,0:T(8,128)(2,1)S(1)} %bitcast.43, bf16[16,4,128,128]{3,2,1,0:T(8,128)(2,1)S(1)} %bitcast.63, ...), custom_call_target="tpu_custom_call", output_to_operand_aliasing={{0}: (18, {})} | custom-call | flops 1000 | bytes 1000 | tf_op jit(solution)/shard_map/pallas_call | solution.py:515
  81.5 10.3 %shard_map.129 = (bf16[16,4,128,128]{3,2,1,0:T(8,128)(2,1)S(1)}, bf16[16,4,256,256]{3,2,1,0:T(8,128)(2,1)S(1)}) custom-call(s32[257]{0:T(512)S(1)} %concatenate.11.flat, bf16[16,4,128,128]{3,2,1,0:T(8,128)(2,1)S(1)} %bitcast.45, bf16[16,4,128,128]{3,2,1,0:T(8,128)(2,1)S(1)} %bitcast.65, ...), custom_call_target="tpu_custom_call", output_to_operand_aliasing={{0}: (4, {}), {1}: (5, {})} | custom-call | flops 1000 | bytes 1000 | tf_op jit(solution)/shard_map/pallas_call | solution.py:257
  91.8 9.8 %collective-permute-done.5.refs_15_ = s32[4,264,128]{2,1,0:T(8,128)S(1)} collective-permute-done((s32[4,264,128]{2,1,0:T(8,128)S(1)}, s32[4,264,128]{2,1,0:T(8,128)S(1)}, u32[]{:S(2)}, u32[]{:S(2)}) %collective-permute-start.5) | collective-permute-done | bytes 540704 | tf_op jit(solution)/shard_map/ppermute | solution.py:628
  101.6 5.8 %shard_map.130 = (bf16[16,4,2,128,128]{4,3,2,1,0:T(8,128)(2,1)S(1)}, s32[4,264,128]{2,1,0:T(8,128)S(1)}) custom-call(s32[257]{0:T(512)S(1)} %concatenate.11.flat, bf16[1,128]{1,0:T(2,128)(2,1)S(1)} %bitcast.80, bf16[16,4,128,128]{3,2,1,0:T(8,128)(2,1)S(1)} %bitcast.46, bf16[16,4,128,128]{3,2,1,0:T(8,128)(2,1)S(1)} %bitcast.66, ...), custom_call_target="tpu_custom_call", output_to_operand_aliasing={{0}: (18, {})} | custom-call | flops 1000 | bytes 1000 | tf_op jit(solution)/shard_map/pallas_call | solution.py:515
  107.4 5.8 %shard_map.131 = (bf16[16,4,2,128,128]{4,3,2,1,0:T(8,128)(2,1)S(1)}, s32[4,264,128]{2,1,0:T(8,128)S(1)}) custom-call(s32[257]{0:T(512)S(1)} %concatenate.11.flat, bf16[1,128]{1,0:T(2,128)(2,1)S(1)} %bitcast.81, bf16[16,4,128,128]{3,2,1,0:T(8,128)(2,1)S(1)} %bitcast.48, bf16[16,4,128,128]{3,2,1,0:T(8,128)(2,1)S(1)} %bitcast.68, ...), custom_call_target="tpu_custom_call", output_to_operand_aliasing={{0}: (18, {})} | custom-call | flops 1000 | bytes 1000 | tf_op jit(solution)/shard_map/pallas_call | solution.py:515
  115.4 5.8 %shard_map.132 = (bf16[16,4,2,128,128]{4,3,2,1,0:T(8,128)(2,1)S(1)}, s32[4,264,128]{2,1,0:T(8,128)S(1)}) custom-call(s32[257]{0:T(512)S(1)} %concatenate.11.flat, bf16[1,128]{1,0:T(2,128)(2,1)S(1)} %bitcast.82, bf16[16,4,128,128]{3,2,1,0:T(8,128)(2,1)S(1)} %bitcast.50, bf16[16,4,128,128]{3,2,1,0:T(8,128)(2,1)S(1)} %bitcast.70, ...), custom_call_target="tpu_custom_call", output_to_operand_aliasing={{0}: (18, {})} | custom-call | flops 1000 | bytes 1000 | tf_op jit(solution)/shard_map/pallas_call | solution.py:515
  121.3 2.4 %collective-permute-start.8 = (s32[4,264,128]{2,1,0:T(8,128)S(1)}, s32[4,264,128]{2,1,0:T(8,128)S(1)}, u32[]{:S(2)}, u32[]{:S(2)}) collective-permute-start(s32[4,264,128]{2,1,0:T(8,128)S(1)} %get-tuple-element.129), channel_id=1, source_target_pairs={{0,8},{4,12},{8,0},{12,4},{1,9},{5,13},{9,1},{13,5},{2,10},{6,14},... | collective-permute-start | bytes 1622024 | tf_op jit(solution)/shard_map/ppermute | solution.py:628
  123.6 6.6 %shard_map.133 = (bf16[16,4,2,128,128]{4,3,2,1,0:T(8,128)(2,1)S(1)}, f32[16,8,128,128]{3,2,1,0:T(8,128)}) custom-call(s32[257]{0:T(512)S(1)} %concatenate.11.flat, bf16[1,128]{1,0:T(2,128)(2,1)S(1)} %bitcast.83, bf16[16,4,128,128]{3,2,1,0:T(8,128)(2,1)S(1)} %bitcast.52, bf16[16,4,128,128]{3,2,1,0:T(8,128)(2,1)S(1)} %bitcast.72, ...), custom_call_target="tpu_custom_call", output_to_operand_aliasing={{0}: (18, {})} | custom-call | flops 1000 | bytes 1000 | tf_op jit(solution)/shard_map/pallas_call | solution.py:515
  130.2 6.7 %shard_map.134 = (bf16[16,4,2,128,128]{4,3,2,1,0:T(8,128)(2,1)S(1)}, f32[16,8,128,128]{3,2,1,0:T(8,128)}) custom-call(s32[257]{0:T(512)S(1)} %concatenate.11.flat, bf16[1,128]{1,0:T(2,128)(2,1)S(1)} %bitcast.84, bf16[16,4,128,128]{3,2,1,0:T(8,128)(2,1)S(1)} %bitcast.54, ...), custom_call_target="tpu_custom_call", output_to_operand_aliasing={{0}: (18, {}), {1}: (19, {})} | custom-call | flops 1000 | bytes 1000 | tf_op jit(solution)/shard_map/pallas_call | solution.py:515
  136.9 6.4 %shard_map.135 = bf16[16,128,8,128]{3,2,1,0:T(8,128)(2,1)} custom-call(bf16[16,4,2,128,128]{4,3,2,1,0:T(8,128)(2,1)S(1)} %get-tuple-element.128.mixed_ref), custom_call_target="tpu_custom_call" | custom-call | flops 1000 | bytes 1000 | tf_op jit(solution)/shard_map/pallas_call | solution.py:593
  143.3 3.4 %shard_map.136.refs_1_ = f32[16,8,128,128]{3,2,1,0:T(8,128)} custom-call(s32[257]{0:T(512)S(1)} %concatenate.11.flat, s32[4,264,128]{2,1,0:T(8,128)S(1)} %collective-permute-done.6.refs_0_, s32[4,264,128]{2,1,0:T(8,128)S(1)} %collective-permute-done.7.refs_1_, s32[4,264,128]{2,1,0:T(8,128)S(1)} %collective-permute-done.11.refs_2_, ...), custom_call_target="tpu_custom_call", output_to_operand_aliasing={{}: (4, {})} | custom-call | flops 1000 | bytes 1000 | tf_op jit(solution)/shard_map/pallas_call | solution.py:566
  150.0 11.1 %collective-permute-done.8.refs_0_ = s32[4,264,128]{2,1,0:T(8,128)S(1)} collective-permute-done((s32[4,264,128]{2,1,0:T(8,128)S(1)}, s32[4,264,128]{2,1,0:T(8,128)S(1)}, u32[]{:S(2)}, u32[]{:S(2)}) %collective-permute-start.8) | collective-permute-done | bytes 540704 | tf_op jit(solution)/shard_map/ppermute | solution.py:628
  (45 shorter events, 17.2 us)
Async XLA Ops:
  0.6 1.6 copy-start.2
  2.8 28.2 %collective-permute-start = (s32[4,264,128]{2,1,0:T(8,128)S(1)}, s32[4,264,128]{2,1,0:T(8,128)}, u32[]{:S(2)}, u32[]{:S(2)}) collective-permute-start(s32[4,264,128]{2,1,0:T(8,128)S(1)} %get-tuple-element.94.refs_12_), channel_id=1, source_target_pairs={{0,8},{4,12},{8,0},{12,4},{1,9},{5,13},{9,1},{13,5},{2,10},{6,14},... | collective-permute-start | bytes 1622024 | tf_op jit(solution)/shard_map/ppermute | solution.py:628
  9.1 46.7 %collective-permute-start.1 = (s32[4,264,128]{2,1,0:T(8,128)S(1)}, s32[4,264,128]{2,1,0:T(8,128)}, u32[]{:S(2)}, u32[]{:S(2)}) collective-permute-start(s32[4,264,128]{2,1,0:T(8,128)S(1)} %get-tuple-element.94.refs_12_), channel_id=1, source_target_pairs={{0,4},{4,0},{8,12},{12,8},{1,5},{5,1},{9,13},{13,9},{2,6},{6,2},{1... | collective-permute-start | bytes 1622024 | tf_op jit(solution)/shard_map/ppermute | solution.py:628
  10.7 3.6 %copy-start.4 = (bf16[16,128,4,2,128]{4,3,2,1,0:T(2,128)(2,1)S(1)}, bf16[16,128,4,2,128]{4,3,2,1,0:T(2,128)(2,1)}, u32[]{:S(2)}) copy-start(bf16[16,128,4,2,128]{4,3,2,1,0:T(2,128)(2,1)} %param.13) | copy-start | bytes 12582916
  14.4 3.3 %copy-start.7 = (s32[64]{0:T(128)S(1)}, s32[64]{0:T(128)}, u32[]{:S(2)}) copy-start(s32[64]{0:T(128)} %param.18) | copy-start | bytes 772
  14.4 3.3 %copy-start.8 = (s32[64]{0:T(128)S(1)}, s32[64]{0:T(128)}, u32[]{:S(2)}) copy-start(s32[64]{0:T(128)} %param.19) | copy-start | bytes 772
  14.4 3.3 %copy-start.9 = (s32[64]{0:T(128)S(1)}, s32[64]{0:T(128)}, u32[]{:S(2)}) copy-start(s32[64]{0:T(128)} %param.20) | copy-start | bytes 772
  14.4 3.3 %copy-start.10 = (s32[64]{0:T(128)S(1)}, s32[64]{0:T(128)}, u32[]{:S(2)}) copy-start(s32[64]{0:T(128)} %param.21) | copy-start | bytes 772
  14.4 3.4 %copy-start.5 = (bf16[16,128,4,2]{1,3,2,0:T(2,128)(2,1)S(1)}, bf16[16,128,4,2]{1,3,2,0:T(2,128)(2,1)}, u32[]{:S(2)}) copy-start(bf16[16,128,4,2]{1,3,2,0:T(2,128)(2,1)} %param.15) | copy-start | bytes 98308
  14.4 3.4 %copy-start.6 = (bf16[16,128,4,2]{1,3,2,0:T(2,128)(2,1)S(1)}, bf16[16,128,4,2]{1,3,2,0:T(2,128)(2,1)}, u32[]{:S(2)}) copy-start(bf16[16,128,4,2]{1,3,2,0:T(2,128)(2,1)} %param.14) | copy-start | bytes 98308
  17.8 1.6 copy-start.1
  31.0 25.5 %collective-permute-start.2 = (s32[4,264,128]{2,1,0:T(8,128)}, s32[4,264,128]{2,1,0:T(8,128)S(1)}, u32[]{:S(2)}, u32[]{:S(2)}) collective-permute-start(s32[4,264,128]{2,1,0:T(8,128)} %collective-permute-done.refs_14_), channel_id=1, source_target_pairs={{0,4},{4,0},{8,12},{12,8},{1,5},{5,1},{9,13},{13,9},{2,6},{6,2},{1... | collective-permute-start | bytes 1622024 | tf_op jit(solution)/shard_map/ppermute | solution.py:628
  31.6 27.3 %collective-permute-start.3 = (s32[4,264,128]{2,1,0:T(8,128)S(1)}, s32[4,264,128]{2,1,0:T(8,128)S(1)}, u32[]{:S(2)}, u32[]{:S(2)}) collective-permute-start(s32[4,264,128]{2,1,0:T(8,128)S(1)} %get-tuple-element.114.refs_12_), channel_id=1, source_target_pairs={{0,8},{4,12},{8,0},{12,4},{1,9},{5,13},{9,1},{13,5},{2,10},{6,14},... | collective-permute-start | bytes 1622024 | tf_op jit(solution)/shard_map/ppermute | solution.py:628
  45.5 15.4 %copy-start = (bf16[16,128,4,2,128]{4,1,3,2,0:T(8,128)(2,1)S(1)}, bf16[16,128,4,2,128]{4,1,3,2,0:T(8,128)(2,1)}, u32[]{:S(2)}) copy-start(bf16[16,128,4,2,128]{4,1,3,2,0:T(8,128)(2,1)} %copy.35) | copy-start | bytes 12582916
  45.5 15.4 %copy-start.3 = (bf16[128]{0:T(256)(128)(2,1)S(1)}, bf16[128]{0:T(256)(128)(2,1)}, u32[]{:S(2)}) copy-start(bf16[128]{0:T(256)(128)(2,1)} %param.16) | copy-start | bytes 772
  58.9 33.0 %collective-permute-start.4 = (s32[4,264,128]{2,1,0:T(8,128)S(1)}, s32[4,264,128]{2,1,0:T(8,128)S(1)}, u32[]{:S(2)}, u32[]{:S(2)}) collective-permute-start(s32[4,264,128]{2,1,0:T(8,128)S(1)} %get-tuple-element.114.refs_12_), channel_id=1, source_target_pairs={{0,4},{4,0},{8,12},{12,8},{1,5},{5,1},{9,13},{13,9},{2,6},{6,2},{1... | collective-permute-start | bytes 1622024 | tf_op jit(solution)/shard_map/ppermute | solution.py:628
  59.4 42.2 %collective-permute-start.5 = (s32[4,264,128]{2,1,0:T(8,128)S(1)}, s32[4,264,128]{2,1,0:T(8,128)S(1)}, u32[]{:S(2)}, u32[]{:S(2)}) collective-permute-start(s32[4,264,128]{2,1,0:T(8,128)S(1)} %collective-permute-done.3.refs_14_), channel_id=1, source_target_pairs={{0,4},{4,0},{8,12},{12,8},{1,5},{5,1},{9,13},{13,9},{2,6},{6,2},{1... | collective-permute-start | bytes 1622024 | tf_op jit(solution)/shard_map/ppermute | solution.py:628
  67.0 34.6 %collective-permute-start.6 = (s32[4,264,128]{2,1,0:T(8,128)S(1)}, s32[4,264,128]{2,1,0:T(8,128)S(1)}, u32[]{:S(2)}, u32[]{:S(2)}) collective-permute-start(s32[4,264,128]{2,1,0:T(8,128)S(1)} %get-tuple-element.119), channel_id=1, source_target_pairs={{0,12},{4,8},{8,4},{12,0},{1,13},{5,9},{9,5},{13,1},{2,14},{6,10},... | collective-permute-start | bytes 1622024 | tf_op jit(solution)/shard_map/ppermute | solution.py:628
  75.4 48.2 %collective-permute-start.7 = (s32[4,264,128]{2,1,0:T(8,128)S(1)}, s32[4,264,128]{2,1,0:T(8,128)S(1)}, u32[]{:S(2)}, u32[]{:S(2)}) collective-permute-start(s32[4,264,128]{2,1,0:T(8,128)S(1)} %get-tuple-element.124), channel_id=1, source_target_pairs={{0,8},{4,12},{8,0},{12,4},{1,9},{5,13},{9,1},{13,5},{2,10},{6,14},... | collective-permute-start | bytes 1622024 | tf_op jit(solution)/shard_map/ppermute | solution.py:628
  101.6 41.7 %collective-permute-start.11 = (s32[4,264,128]{2,1,0:T(8,128)S(1)}, s32[4,264,128]{2,1,0:T(8,128)S(1)}, u32[]{:S(2)}, u32[]{:S(2)}) collective-permute-start(s32[4,264,128]{2,1,0:T(8,128)S(1)} %get-tuple-element.134), channel_id=1, source_target_pairs={{0,4},{4,0},{8,12},{12,8},{1,5},{5,1},{9,13},{13,9},{2,6},{6,2},{1... | collective-permute-start | bytes 1622024 | tf_op jit(solution)/shard_map/ppermute | solution.py:628
  113.3 35.1 %collective-permute-start.9 = (s32[4,264,128]{2,1,0:T(8,128)S(1)}, s32[4,264,128]{2,1,0:T(8,128)S(1)}, u32[]{:S(2)}, u32[]{:S(2)}) collective-permute-start(s32[4,264,128]{2,1,0:T(8,128)S(1)} %get-tuple-element.130), channel_id=1, source_target_pairs={{0,12},{4,8},{8,4},{12,0},{1,13},{5,9},{9,5},{13,1},{2,14},{6,10},... | collective-permute-start | bytes 1622024 | tf_op jit(solution)/shard_map/ppermute | solution.py:628
  114.0 32.8 %collective-permute-start.10 = (s32[4,264,128]{2,1,0:T(8,128)S(1)}, s32[4,264,128]{2,1,0:T(8,128)S(1)}, u32[]{:S(2)}, u32[]{:S(2)}) collective-permute-start(s32[4,264,128]{2,1,0:T(8,128)S(1)} %get-tuple-element.131), channel_id=1, source_target_pairs={{0,4},{4,0},{8,12},{12,8},{1,5},{5,1},{9,13},{13,9},{2,6},{6,2},{1... | collective-permute-start | bytes 1622024 | tf_op jit(solution)/shard_map/ppermute | solution.py:628
  121.3 39.8 %collective-permute-start.8 = (s32[4,264,128]{2,1,0:T(8,128)S(1)}, s32[4,264,128]{2,1,0:T(8,128)S(1)}, u32[]{:S(2)}, u32[]{:S(2)}) collective-permute-start(s32[4,264,128]{2,1,0:T(8,128)S(1)} %get-tuple-element.129), channel_id=1, source_target_pairs={{0,8},{4,12},{8,0},{12,4},{1,9},{5,13},{9,1},{13,5},{2,10},{6,14},... | collective-permute-start | bytes 1622024 | tf_op jit(solution)/shard_map/ppermute | solution.py:628

commit v6 on v5

--- a/solution.py
+++ b/solution.py
@@ -683,18 +683,18 @@
             mixed, arrived[0, away] = lax.optimization_barrier((mixed, arrived[0, away]))
         return mixed
 
-    for away in crossing:
-        mixed, final = work(0, [away], mixed, final)
-    rates, mixed, pairs[1] = lax.optimization_barrier((rates, mixed, pairs[1]))
-    pairs[1] = pair_parts(1, 1, plan, flat, q, k, rates, pairs[1])
+    mixed, final = work(0, crossing[:1], mixed, final)
     held_back = []
-    for away in near:
+    for away in crossing[1:] + near:
+        if away == near[0]:
+            rates, mixed, pairs[1] = lax.optimization_barrier((rates, mixed, pairs[1]))
+            pairs[1] = pair_parts(1, 1, plan, flat, q, k, rates, pairs[1])
         mixed, state = recurrence(
             0, [away], plan, flat, q, k, v, rates, pairs[0], gathered[0], gain, mixed, final_shape, final
         )
         held_back.append(state)
     mixed, pairs[1], gathered[1], held_back = lax.optimization_barrier((mixed, pairs[1], gathered[1], held_back))
-    for away, state in zip(near, held_back):
+    for away, state in zip(crossing[1:] + near, held_back):
         arrived[0, away] = swap(state, away)
     mixed = gone(mixed, crossing[:1])
     for away in near + crossing:

time: 163 us -> 167 us (1.025)
  waiting for transfers between devices: 25.2 us -> 28.1 us
  starting transfers between devices: 18.9 us -> 20.9 us
    ppermute x12, waiting for transfers between devices: 25.2 us -> 28.1 us  [swap(): return lax.ppermute(tensor, 'seq', [(i, i ^ off) for i in range(seq_count)])]
    ppermute x12, starting transfers between devices: 18.9 us -> 20.9 us  [swap(): return lax.ppermute(tensor, 'seq', [(i, i ^ off) for i in range(seq_count)])]
  transfers between devices with their start and end apart: 12 -> 12, of which waited for: 5 -> 6; matrix products, arithmetic and copies ran while one was open for 6% -> 5% of each run, Pallas kernels for 63% -> 61%
where the time goes in v6:
time: 167 us
  Pallas kernels  105 us (63%)
  waiting for transfers between devices  28.1 us (17%)
  starting transfers between devices  20.9 us (13%)
  local copies, waits for them, and re-layouts  12.3 us (7%)
    pallas_call x8, Pallas kernels, recurrence(): pl.pallas_call(functools.partial(state_kernel, part, aways, plan, len(par...  48.3 us
    pallas_call x4, Pallas kernels, pair_parts(): pl.pallas_call(functools.partial(pair_kernel, part, first, plan), grid_sp...  41.3 us
    ppermute x12, waiting for transfers between devices, swap(): return lax.ppermute(tensor, 'seq', [(i, i ^ off) for i in range(seq_count)])  28.1 us
    ppermute x12, starting transfers between devices, swap(): return lax.ppermute(tensor, 'seq', [(i, i ^ off) for i in range(seq_count)])  20.9 us
    unnamed x25, local copies, waits for them, and re-layouts  12.2 us
    pallas_call x4, Pallas kernels, unpack_states(): pl.pallas_call(functools.partial(unpack_kernel, turns), grid_spec=pltpu.P...  8.29 us
    pallas_call x1, Pallas kernels, turn_mixed(): pl.pallas_call(turn_kernel, grid=(count,), in_specs=[pl.BlockSpec((1, key...  6.44 us
  transfers between devices with their start and end apart: 12, of which 6 were waited for; matrix products, arithmetic and copies ran while one was open for 5% of the time, Pallas kernels for 61%

profile of v6, /device:TPU:0, one launch (start us, length us, event | category | flops | bytes accessed | tf_op | source)
XLA Modules:
  0.0 167.2 jit_solution(15079382880093460635)
XLA Ops:
  2.8 4.1 %collective-permute-start = (s32[4,264,128]{2,1,0:T(8,128)S(1)}, s32[4,264,128]{2,1,0:T(8,128)}, u32[]{:S(2)}, u32[]{:S(2)}) collective-permute-start(s32[4,264,128]{2,1,0:T(8,128)S(1)} %get-tuple-element.95.refs_12_), channel_id=1, source_target_pairs={{0,8},{4,12},{8,0},{12,4},{1,9},{5,13},{9,1},{13,5},{2,10},{6,14},... | collective-permute-start | bytes 1622024 | tf_op jit(solution)/shard_map/ppermute | solution.py:628
  10.7 3.6 %copy.36 = bf16[16,128,4,128]{3,1,2,0:T(8,128)(2,1)} copy(bf16[16,128,4,128]{3,2,1,0:T(4,128)(2,1)} %param.12) | data formatting | bytes 4194304 | tf_op args[1]
  14.4 3.3 %copy.35 = bf16[16,128,4,2,128]{4,1,3,2,0:T(8,128)(2,1)} copy(bf16[16,128,4,2,128]{4,3,2,1,0:T(2,128)(2,1)S(1)} %copy-done.4) | data formatting | bytes 8388608 | tf_op args[2]
  19.4 10.3 %shard_map.123 = (bf16[16,4,128,128]{3,2,1,0:T(8,128)(2,1)S(1)}, bf16[16,4,256,256]{3,2,1,0:T(8,128)(2,1)S(1)}) custom-call(s32[257]{0:T(512)S(1)} %concatenate.11.flat, bf16[16,4,128,128]{3,2,1,0:T(8,128)(2,1)S(1)} %bitcast.36, bf16[16,4,128,128]{3,2,1,0:T(8,128)(2,1)S(1)} %bitcast.56, f32[16,16,128]{2,1,0:T(8,128)S(1)} %maximum_convert_fusion.rate_ref.refs_3_.refs_9_), custom_call_target="tpu_custom_call" | custom-call | flops 1000 | bytes 1000 | tf_op jit(solution)/shard_map/pallas_call | solution.py:257
  31.6 3.5 %collective-permute-start.3 = (s32[4,264,128]{2,1,0:T(8,128)S(1)}, s32[4,264,128]{2,1,0:T(8,128)S(1)}, u32[]{:S(2)}, u32[]{:S(2)}) collective-permute-start(s32[4,264,128]{2,1,0:T(8,128)S(1)} %get-tuple-element.116.refs_12_), channel_id=1, source_target_pairs={{0,8},{4,12},{8,0},{12,4},{1,9},{5,13},{9,1},{13,5},{2,10},{6,14},... | collective-permute-start | bytes 1622024 | tf_op jit(solution)/shard_map/ppermute | solution.py:628
  35.1 10.3 %shard_map.124 = (bf16[16,4,128,128]{3,2,1,0:T(8,128)(2,1)S(1)}, bf16[16,4,256,256]{3,2,1,0:T(8,128)(2,1)S(1)}) custom-call(s32[257]{0:T(512)S(1)} %concatenate.11.flat, bf16[16,4,128,128]{3,2,1,0:T(8,128)(2,1)S(1)} %bitcast.37, bf16[16,4,128,128]{3,2,1,0:T(8,128)(2,1)S(1)} %bitcast.57, ...), custom_call_target="tpu_custom_call", output_to_operand_aliasing={{0}: (4, {}), {1}: (5, {})} | custom-call | flops 1000 | bytes 1000 | tf_op jit(solution)/shard_map/pallas_call | solution.py:257
  45.5 10.3 %shard_map.125 = (bf16[16,4,128,128]{3,2,1,0:T(8,128)(2,1)S(1)}, bf16[16,4,256,256]{3,2,1,0:T(8,128)(2,1)S(1)}) custom-call(s32[257]{0:T(512)S(1)} %concatenate.11.flat, bf16[16,4,128,128]{3,2,1,0:T(8,128)(2,1)S(1)} %bitcast.38, bf16[16,4,128,128]{3,2,1,0:T(8,128)(2,1)S(1)} %bitcast.58, f32[16,16,128]{2,1,0:T(8,128)S(1)} %maximum_convert_fusion.rate_ref.refs_3_.refs_9_), custom_call_target="tpu_custom_call" | custom-call | flops 1000 | bytes 1000 | tf_op jit(solution)/shard_map/pallas_call | solution.py:257
  56.5 2.4 %collective-permute-done.3.refs_14_ = s32[4,264,128]{2,1,0:T(8,128)S(1)} collective-permute-done((s32[4,264,128]{2,1,0:T(8,128)S(1)}, s32[4,264,128]{2,1,0:T(8,128)S(1)}, u32[]{:S(2)}, u32[]{:S(2)}) %collective-permute-start.3) | collective-permute-done | bytes 540704 | tf_op jit(solution)/shard_map/ppermute | solution.py:628
  60.9 5.9 %shard_map.126 = (bf16[16,4,2,128,128]{4,3,2,1,0:T(8,128)(2,1)S(1)}, s32[4,264,128]{2,1,0:T(8,128)S(1)}) custom-call(s32[257]{0:T(512)S(1)} %concatenate.11.flat, bf16[1,128]{1,0:T(2,128)(2,1)S(1)} %bitcast.77, bf16[16,4,128,128]{3,2,1,0:T(8,128)(2,1)S(1)} %bitcast.39, bf16[16,4,128,128]{3,2,1,0:T(8,128)(2,1)S(1)} %bitcast.59, ...), custom_call_target="tpu_custom_call" | custom-call | flops 1000 | bytes 1000 | tf_op jit(solution)/shard_map/pallas_call | solution.py:515
  66.8 2.3 %collective-permute-start.6 = (s32[4,264,128]{2,1,0:T(8,128)S(1)}, s32[4,264,128]{2,1,0:T(8,128)S(1)}, u32[]{:S(2)}, u32[]{:S(2)}) collective-permute-start(s32[4,264,128]{2,1,0:T(8,128)S(1)} %get-tuple-element.121), channel_id=1, source_target_pairs={{0,12},{4,8},{8,4},{12,0},{1,13},{5,9},{9,5},{13,1},{2,14},{6,10},... | collective-permute-start | bytes 1622024 | tf_op jit(solution)/shard_map/ppermute | solution.py:628
  69.1 5.8 %shard_map.127 = (bf16[16,4,2,128,128]{4,3,2,1,0:T(8,128)(2,1)S(1)}, s32[4,264,128]{2,1,0:T(8,128)S(1)}) custom-call(s32[257]{0:T(512)S(1)} %concatenate.11.flat, bf16[1,128]{1,0:T(2,128)(2,1)S(1)} %bitcast.78, bf16[16,4,128,128]{3,2,1,0:T(8,128)(2,1)S(1)} %bitcast.41, bf16[16,4,128,128]{3,2,1,0:T(8,128)(2,1)S(1)} %bitcast.61, ...), custom_call_target="tpu_custom_call", output_to_operand_aliasing={{0}: (18, {})} | custom-call | flops 1000 | bytes 1000 | tf_op jit(solution)/shard_map/pallas_call | solution.py:515
  75.0 6.0 %shard_map.128 = (bf16[16,4,2,128,128]{4,3,2,1,0:T(8,128)(2,1)S(1)}, s32[4,264,128]{2,1,0:T(8,128)S(1)}) custom-call(s32[257]{0:T(512)S(1)} %concatenate.11.flat, bf16[1,128]{1,0:T(2,128)(2,1)S(1)} %bitcast.79, bf16[16,4,128,128]{3,2,1,0:T(8,128)(2,1)S(1)} %bitcast.43, bf16[16,4,128,128]{3,2,1,0:T(8,128)(2,1)S(1)} %bitcast.63, ...), custom_call_target="tpu_custom_call", output_to_operand_aliasing={{0}: (18, {})} | custom-call | flops 1000 | bytes 1000 | tf_op jit(solution)/shard_map/pallas_call | solution.py:515
  81.0 10.3 %shard_map.129 = (bf16[16,4,128,128]{3,2,1,0:T(8,128)(2,1)S(1)}, bf16[16,4,256,256]{3,2,1,0:T(8,128)(2,1)S(1)}) custom-call(s32[257]{0:T(512)S(1)} %concatenate.11.flat, bf16[16,4,128,128]{3,2,1,0:T(8,128)(2,1)S(1)} %bitcast.45, bf16[16,4,128,128]{3,2,1,0:T(8,128)(2,1)S(1)} %bitcast.65, ...), custom_call_target="tpu_custom_call", output_to_operand_aliasing={{0}: (4, {}), {1}: (5, {})} | custom-call | flops 1000 | bytes 1000 | tf_op jit(solution)/shard_map/pallas_call | solution.py:257
  91.4 2.2 %collective-permute-start.11 = (s32[4,264,128]{2,1,0:T(8,128)S(1)}, s32[4,264,128]{2,1,0:T(8,128)S(1)}, u32[]{:S(2)}, u32[]{:S(2)}) collective-permute-start(s32[4,264,128]{2,1,0:T(8,128)S(1)} %get-tuple-element.136), channel_id=1, source_target_pairs={{0,4},{4,0},{8,12},{12,8},{1,5},{5,1},{9,13},{13,9},{2,6},{6,2},{1... | collective-permute-start | bytes 1622024 | tf_op jit(solution)/shard_map/ppermute | solution.py:628
  93.6 4.2 %collective-permute-done.6.refs_0_ = s32[4,264,128]{2,1,0:T(8,128)S(1)} collective-permute-done((s32[4,264,128]{2,1,0:T(8,128)S(1)}, s32[4,264,128]{2,1,0:T(8,128)S(1)}, u32[]{:S(2)}, u32[]{:S(2)}) %collective-permute-start.6) | collective-permute-done | bytes 540704 | tf_op jit(solution)/shard_map/ppermute | solution.py:628
  97.7 5.8 %shard_map.130 = (bf16[16,4,2,128,128]{4,3,2,1,0:T(8,128)(2,1)S(1)}, s32[4,264,128]{2,1,0:T(8,128)S(1)}) custom-call(s32[257]{0:T(512)S(1)} %concatenate.11.flat, bf16[1,128]{1,0:T(2,128)(2,1)S(1)} %bitcast.80, bf16[16,4,128,128]{3,2,1,0:T(8,128)(2,1)S(1)} %bitcast.46, bf16[16,4,128,128]{3,2,1,0:T(8,128)(2,1)S(1)} %bitcast.66, ...), custom_call_target="tpu_custom_call", output_to_operand_aliasing={{0}: (18, {})} | custom-call | flops 1000 | bytes 1000 | tf_op jit(solution)/shard_map/pallas_call | solution.py:515
  103.5 5.8 %shard_map.131 = (bf16[16,4,2,128,128]{4,3,2,1,0:T(8,128)(2,1)S(1)}, s32[4,264,128]{2,1,0:T(8,128)S(1)}) custom-call(s32[257]{0:T(512)S(1)} %concatenate.11.flat, bf16[1,128]{1,0:T(2,128)(2,1)S(1)} %bitcast.81, bf16[16,4,128,128]{3,2,1,0:T(8,128)(2,1)S(1)} %bitcast.48, bf16[16,4,128,128]{3,2,1,0:T(8,128)(2,1)S(1)} %bitcast.68, ...), custom_call_target="tpu_custom_call", output_to_operand_aliasing={{0}: (18, {})} | custom-call | flops 1000 | bytes 1000 | tf_op jit(solution)/shard_map/pallas_call | solution.py:515
  111.4 5.8 %shard_map.132 = (bf16[16,4,2,128,128]{4,3,2,1,0:T(8,128)(2,1)S(1)}, s32[4,264,128]{2,1,0:T(8,128)S(1)}) custom-call(s32[257]{0:T(512)S(1)} %concatenate.11.flat, bf16[1,128]{1,0:T(2,128)(2,1)S(1)} %bitcast.82, bf16[16,4,128,128]{3,2,1,0:T(8,128)(2,1)S(1)} %bitcast.50, bf16[16,4,128,128]{3,2,1,0:T(8,128)(2,1)S(1)} %bitcast.70, ...), custom_call_target="tpu_custom_call", output_to_operand_aliasing={{0}: (18, {})} | custom-call | flops 1000 | bytes 1000 | tf_op jit(solution)/shard_map/pallas_call | solution.py:515
  117.2 2.5 %collective-permute-start.8 = (s32[4,264,128]{2,1,0:T(8,128)S(1)}, s32[4,264,128]{2,1,0:T(8,128)S(1)}, u32[]{:S(2)}, u32[]{:S(2)}) collective-permute-start(s32[4,264,128]{2,1,0:T(8,128)S(1)} %get-tuple-element.131), channel_id=1, source_target_pairs={{0,8},{4,12},{8,0},{12,4},{1,9},{5,13},{9,1},{13,5},{2,10},{6,14},... | collective-permute-start | bytes 1622024 | tf_op jit(solution)/shard_map/ppermute | solution.py:628
  121.0 6.4 %shard_map.133 = (bf16[16,4,2,128,128]{4,3,2,1,0:T(8,128)(2,1)S(1)}, f32[16,8,128,128]{3,2,1,0:T(8,128)}) custom-call(s32[257]{0:T(512)S(1)} %concatenate.11.flat, bf16[1,128]{1,0:T(2,128)(2,1)S(1)} %bitcast.83, bf16[16,4,128,128]{3,2,1,0:T(8,128)(2,1)S(1)} %bitcast.52, bf16[16,4,128,128]{3,2,1,0:T(8,128)(2,1)S(1)} %bitcast.72, ...), custom_call_target="tpu_custom_call", output_to_operand_aliasing={{0}: (18, {})} | custom-call | flops 1000 | bytes 1000 | tf_op jit(solution)/shard_map/pallas_call | solution.py:515
  127.4 6.7 %shard_map.134 = (bf16[16,4,2,128,128]{4,3,2,1,0:T(8,128)(2,1)S(1)}, f32[16,8,128,128]{3,2,1,0:T(8,128)}) custom-call(s32[257]{0:T(512)S(1)} %concatenate.11.flat, bf16[1,128]{1,0:T(2,128)(2,1)S(1)} %bitcast.84, bf16[16,4,128,128]{3,2,1,0:T(8,128)(2,1)S(1)} %bitcast.54, ...), custom_call_target="tpu_custom_call", output_to_operand_aliasing={{0}: (18, {}), {1}: (19, {})} | custom-call | flops 1000 | bytes 1000 | tf_op jit(solution)/shard_map/pallas_call | solution.py:515
  134.1 6.4 %shard_map.135 = bf16[16,128,8,128]{3,2,1,0:T(8,128)(2,1)} custom-call(bf16[16,4,2,128,128]{4,3,2,1,0:T(8,128)(2,1)S(1)} %get-tuple-element.130.mixed_ref), custom_call_target="tpu_custom_call" | custom-call | flops 1000 | bytes 1000 | tf_op jit(solution)/shard_map/pallas_call | solution.py:593
  140.5 3.4 %shard_map.136.refs_1_ = f32[16,8,128,128]{3,2,1,0:T(8,128)} custom-call(s32[257]{0:T(512)S(1)} %concatenate.11.flat, s32[4,264,128]{2,1,0:T(8,128)S(1)} %collective-permute-done.6.refs_0_, s32[4,264,128]{2,1,0:T(8,128)S(1)} %collective-permute-done.7.refs_1_, s32[4,264,128]{2,1,0:T(8,128)S(1)} %collective-permute-done.11.refs_2_, ...), custom_call_target="tpu_custom_call", output_to_operand_aliasing={{}: (4, {})} | custom-call | flops 1000 | bytes 1000 | tf_op jit(solution)/shard_map/pallas_call | solution.py:566
  147.2 18.4 %collective-permute-done.8.refs_0_ = s32[4,264,128]{2,1,0:T(8,128)S(1)} collective-permute-done((s32[4,264,128]{2,1,0:T(8,128)S(1)}, s32[4,264,128]{2,1,0:T(8,128)S(1)}, u32[]{:S(2)}, u32[]{:S(2)}) %collective-permute-start.8) | collective-permute-done | bytes 540704 | tf_op jit(solution)/shard_map/ppermute | solution.py:628
  (45 shorter events, 20.5 us)
Async XLA Ops:
  0.6 1.6 copy-start.2
  2.8 28.2 %collective-permute-start = (s32[4,264,128]{2,1,0:T(8,128)S(1)}, s32[4,264,128]{2,1,0:T(8,128)}, u32[]{:S(2)}, u32[]{:S(2)}) collective-permute-start(s32[4,264,128]{2,1,0:T(8,128)S(1)} %get-tuple-element.95.refs_12_), channel_id=1, source_target_pairs={{0,8},{4,12},{8,0},{12,4},{1,9},{5,13},{9,1},{13,5},{2,10},{6,14},... | collective-permute-start | bytes 1622024 | tf_op jit(solution)/shard_map/ppermute | solution.py:628
  9.1 46.7 %collective-permute-start.1 = (s32[4,264,128]{2,1,0:T(8,128)S(1)}, s32[4,264,128]{2,1,0:T(8,128)}, u32[]{:S(2)}, u32[]{:S(2)}) collective-permute-start(s32[4,264,128]{2,1,0:T(8,128)S(1)} %get-tuple-element.95.refs_12_), channel_id=1, source_target_pairs={{0,4},{4,0},{8,12},{12,8},{1,5},{5,1},{9,13},{13,9},{2,6},{6,2},{1... | collective-permute-start | bytes 1622024 | tf_op jit(solution)/shard_map/ppermute | solution.py:628
  10.7 3.6 %copy-start.4 = (bf16[16,128,4,2,128]{4,3,2,1,0:T(2,128)(2,1)S(1)}, bf16[16,128,4,2,128]{4,3,2,1,0:T(2,128)(2,1)}, u32[]{:S(2)}) copy-start(bf16[16,128,4,2,128]{4,3,2,1,0:T(2,128)(2,1)} %param.13) | copy-start | bytes 12582916
  14.4 3.3 %copy-start.7 = (s32[64]{0:T(128)S(1)}, s32[64]{0:T(128)}, u32[]{:S(2)}) copy-start(s32[64]{0:T(128)} %param.18) | copy-start | bytes 772
  14.4 3.3 %copy-start.8 = (s32[64]{0:T(128)S(1)}, s32[64]{0:T(128)}, u32[]{:S(2)}) copy-start(s32[64]{0:T(128)} %param.19) | copy-start | bytes 772
  14.4 3.3 %copy-start.9 = (s32[64]{0:T(128)S(1)}, s32[64]{0:T(128)}, u32[]{:S(2)}) copy-start(s32[64]{0:T(128)} %param.20) | copy-start | bytes 772
  14.4 3.3 %copy-start.10 = (s32[64]{0:T(128)S(1)}, s32[64]{0:T(128)}, u32[]{:S(2)}) copy-start(s32[64]{0:T(128)} %param.21) | copy-start | bytes 772
  14.4 3.4 %copy-start.5 = (bf16[16,128,4,2]{1,3,2,0:T(2,128)(2,1)S(1)}, bf16[16,128,4,2]{1,3,2,0:T(2,128)(2,1)}, u32[]{:S(2)}) copy-start(bf16[16,128,4,2]{1,3,2,0:T(2,128)(2,1)} %param.15) | copy-start | bytes 98308
  14.4 3.4 %copy-start.6 = (bf16[16,128,4,2]{1,3,2,0:T(2,128)(2,1)S(1)}, bf16[16,128,4,2]{1,3,2,0:T(2,128)(2,1)}, u32[]{:S(2)}) copy-start(bf16[16,128,4,2]{1,3,2,0:T(2,128)(2,1)} %param.14) | copy-start | bytes 98308
  17.8 1.6 copy-start.1
  31.0 25.5 %collective-permute-start.2 = (s32[4,264,128]{2,1,0:T(8,128)}, s32[4,264,128]{2,1,0:T(8,128)S(1)}, u32[]{:S(2)}, u32[]{:S(2)}) collective-permute-start(s32[4,264,128]{2,1,0:T(8,128)} %collective-permute-done.refs_14_), channel_id=1, source_target_pairs={{0,4},{4,0},{8,12},{12,8},{1,5},{5,1},{9,13},{13,9},{2,6},{6,2},{1... | collective-permute-start | bytes 1622024 | tf_op jit(solution)/shard_map/ppermute | solution.py:628
  31.6 27.3 %collective-permute-start.3 = (s32[4,264,128]{2,1,0:T(8,128)S(1)}, s32[4,264,128]{2,1,0:T(8,128)S(1)}, u32[]{:S(2)}, u32[]{:S(2)}) collective-permute-start(s32[4,264,128]{2,1,0:T(8,128)S(1)} %get-tuple-element.116.refs_12_), channel_id=1, source_target_pairs={{0,8},{4,12},{8,0},{12,4},{1,9},{5,13},{9,1},{13,5},{2,10},{6,14},... | collective-permute-start | bytes 1622024 | tf_op jit(solution)/shard_map/ppermute | solution.py:628
  45.5 15.4 %copy-start = (bf16[16,128,4,2,128]{4,1,3,2,0:T(8,128)(2,1)S(1)}, bf16[16,128,4,2,128]{4,1,3,2,0:T(8,128)(2,1)}, u32[]{:S(2)}) copy-start(bf16[16,128,4,2,128]{4,1,3,2,0:T(8,128)(2,1)} %copy.35) | copy-start | bytes 12582916
  45.5 15.4 %copy-start.3 = (bf16[128]{0:T(256)(128)(2,1)S(1)}, bf16[128]{0:T(256)(128)(2,1)}, u32[]{:S(2)}) copy-start(bf16[128]{0:T(256)(128)(2,1)} %param.16) | copy-start | bytes 772
  58.9 32.5 %collective-permute-start.4 = (s32[4,264,128]{2,1,0:T(8,128)S(1)}, s32[4,264,128]{2,1,0:T(8,128)S(1)}, u32[]{:S(2)}, u32[]{:S(2)}) collective-permute-start(s32[4,264,128]{2,1,0:T(8,128)S(1)} %get-tuple-element.116.refs_12_), channel_id=1, source_target_pairs={{0,4},{4,0},{8,12},{12,8},{1,5},{5,1},{9,13},{13,9},{2,6},{6,2},{1... | collective-permute-start | bytes 1622024 | tf_op jit(solution)/shard_map/ppermute | solution.py:628
  59.4 31.9 %collective-permute-start.5 = (s32[4,264,128]{2,1,0:T(8,128)S(1)}, s32[4,264,128]{2,1,0:T(8,128)S(1)}, u32[]{:S(2)}, u32[]{:S(2)}) collective-permute-start(s32[4,264,128]{2,1,0:T(8,128)S(1)} %collective-permute-done.3.refs_14_), channel_id=1, source_target_pairs={{0,4},{4,0},{8,12},{12,8},{1,5},{5,1},{9,13},{13,9},{2,6},{6,2},{1... | collective-permute-start | bytes 1622024 | tf_op jit(solution)/shard_map/ppermute | solution.py:628
  66.8 30.9 %collective-permute-start.6 = (s32[4,264,128]{2,1,0:T(8,128)S(1)}, s32[4,264,128]{2,1,0:T(8,128)S(1)}, u32[]{:S(2)}, u32[]{:S(2)}) collective-permute-start(s32[4,264,128]{2,1,0:T(8,128)S(1)} %get-tuple-element.121), channel_id=1, source_target_pairs={{0,12},{4,8},{8,4},{12,0},{1,13},{5,9},{9,5},{13,1},{2,14},{6,10},... | collective-permute-start | bytes 1622024 | tf_op jit(solution)/shard_map/ppermute | solution.py:628
  91.3 29.6 %collective-permute-start.7 = (s32[4,264,128]{2,1,0:T(8,128)S(1)}, s32[4,264,128]{2,1,0:T(8,128)S(1)}, u32[]{:S(2)}, u32[]{:S(2)}) collective-permute-start(s32[4,264,128]{2,1,0:T(8,128)S(1)} %get-tuple-element.126), channel_id=1, source_target_pairs={{0,8},{4,12},{8,0},{12,4},{1,9},{5,13},{9,1},{13,5},{2,10},{6,14},... | collective-permute-start | bytes 1622024 | tf_op jit(solution)/shard_map/ppermute | solution.py:628
  91.4 49.1 %collective-permute-start.11 = (s32[4,264,128]{2,1,0:T(8,128)S(1)}, s32[4,264,128]{2,1,0:T(8,128)S(1)}, u32[]{:S(2)}, u32[]{:S(2)}) collective-permute-start(s32[4,264,128]{2,1,0:T(8,128)S(1)} %get-tuple-element.136), channel_id=1, source_target_pairs={{0,4},{4,0},{8,12},{12,8},{1,5},{5,1},{9,13},{13,9},{2,6},{6,2},{1... | collective-permute-start | bytes 1622024 | tf_op jit(solution)/shard_map/ppermute | solution.py:628
  109.4 36.2 %collective-permute-start.9 = (s32[4,264,128]{2,1,0:T(8,128)S(1)}, s32[4,264,128]{2,1,0:T(8,128)S(1)}, u32[]{:S(2)}, u32[]{:S(2)}) collective-permute-start(s32[4,264,128]{2,1,0:T(8,128)S(1)} %get-tuple-element.132), channel_id=1, source_target_pairs={{0,12},{4,8},{8,4},{12,0},{1,13},{5,9},{9,5},{13,1},{2,14},{6,10},... | collective-permute-start | bytes 1622024 | tf_op jit(solution)/shard_map/ppermute | solution.py:628
  111.4 32.5 %collective-permute-start.10 = (s32[4,264,128]{2,1,0:T(8,128)S(1)}, s32[4,264,128]{2,1,0:T(8,128)S(1)}, u32[]{:S(2)}, u32[]{:S(2)}) collective-permute-start(s32[4,264,128]{2,1,0:T(8,128)S(1)} %get-tuple-element.133), channel_id=1, source_target_pairs={{0,4},{4,0},{8,12},{12,8},{1,5},{5,1},{9,13},{13,9},{2,6},{6,2},{1... | collective-permute-start | bytes 1622024 | tf_op jit(solution)/shard_map/ppermute | solution.py:628
  117.2 48.3 %collective-permute-start.8 = (s32[4,264,128]{2,1,0:T(8,128)S(1)}, s32[4,264,128]{2,1,0:T(8,128)S(1)}, u32[]{:S(2)}, u32[]{:S(2)}) collective-permute-start(s32[4,264,128]{2,1,0:T(8,128)S(1)} %get-tuple-element.131), channel_id=1, source_target_pairs={{0,8},{4,12},{8,0},{12,4},{1,9},{5,13},{9,1},{13,5},{2,10},{6,14},... | collective-permute-start | bytes 1622024 | tf_op jit(solution)/shard_map/ppermute | solution.py:628

commit v7 on v5

--- a/solution.py
+++ b/solution.py
@@ -697,14 +697,14 @@
     for away, state in zip(near, held_back):
         arrived[0, away] = swap(state, away)
     mixed = gone(mixed, crossing[:1])
-    for away in near + crossing:
+    for away in crossing + near:
         mixed, final = work(1, [away], mixed, final)
     mixed = gone(mixed, crossing[1:])
     for part in range(PARTS):
         mixed, final = work(part, [0], mixed, final)
     away_first = crossing + near
     final = unpack_states(0, away_first, plan, flat, [arrived[0, away] for away in away_first], final)
-    for away in near + crossing:
+    for away in crossing + near:
         final = unpack_states(1, [away], plan, flat, [arrived[1, away]], final)
     mixed_out = turn_mixed(mixed).reshape(values.shape)
     final_out = final.reshape((per_device, key_heads, 2, key_dim, key_dim))

time: 163 us -> 164 us (level)
  the two profiles are of different devices: /device:TPU:0 before, /device:TPU:12 now
where the time goes in v7:
time: 164 us
  Pallas kernels  106 us (65%)
  waiting for transfers between devices  25.5 us (16%)
  starting transfers between devices  19.5 us (12%)
  local copies, waits for them, and re-layouts  12.3 us (8%)
    pallas_call x8, Pallas kernels, recurrence(): pl.pallas_call(functools.partial(state_kernel, part, aways, plan, len(par...  48.9 us
    pallas_call x4, Pallas kernels, pair_parts(): pl.pallas_call(functools.partial(pair_kernel, part, first, plan), grid_sp...  41.3 us
    ppermute x12, waiting for transfers between devices, swap(): return lax.ppermute(tensor, 'seq', [(i, i ^ off) for i in range(seq_count)])  25.5 us
    ppermute x12, starting transfers between devices, swap(): return lax.ppermute(tensor, 'seq', [(i, i ^ off) for i in range(seq_count)])  19.5 us
    unnamed x25, local copies, waits for them, and re-layouts  12.2 us
    pallas_call x4, Pallas kernels, unpack_states(): pl.pallas_call(functools.partial(unpack_kernel, turns), grid_spec=pltpu.P...  8.29 us
    pallas_call x1, Pallas kernels, turn_mixed(): pl.pallas_call(turn_kernel, grid=(count,), in_specs=[pl.BlockSpec((1, key...  6.44 us
  transfers between devices with their start and end apart: 12, of which 5 were waited for; matrix products, arithmetic and copies ran while one was open for 6% of the time, Pallas kernels for 63%

profile of v7, /device:TPU:12, one launch (start us, length us, event | category | flops | bytes accessed | tf_op | source)
XLA Modules:
  0.0 163.7 jit_solution(1495312394988596404)
XLA Ops:
  2.8 2.7 %collective-permute-start = (s32[4,264,128]{2,1,0:T(8,128)S(1)}, s32[4,264,128]{2,1,0:T(8,128)}, u32[]{:S(2)}, u32[]{:S(2)}) collective-permute-start(s32[4,264,128]{2,1,0:T(8,128)S(1)} %get-tuple-element.94.refs_12_), channel_id=1, source_target_pairs={{0,8},{4,12},{8,0},{12,4},{1,9},{5,13},{9,1},{13,5},{2,10},{6,14},... | collective-permute-start | bytes 1622024 | tf_op jit(solution)/shard_map/ppermute | solution.py:628
  5.5 2.1 %copy.37 = bf16[16,128,4,128]{3,1,2,0:T(8,128)(2,1)S(1)} copy(bf16[16,128,4,128]{3,2,1,0:T(4,128)(2,1)} %param.11) | data formatting | bytes 4194304 | tf_op args[0]
  8.2 3.6 %copy.36 = bf16[16,128,4,128]{3,1,2,0:T(8,128)(2,1)} copy(bf16[16,128,4,128]{3,2,1,0:T(4,128)(2,1)} %param.12) | data formatting | bytes 4194304 | tf_op args[1]
  11.8 3.3 %copy.35 = bf16[16,128,4,2,128]{4,1,3,2,0:T(8,128)(2,1)} copy(bf16[16,128,4,2,128]{4,3,2,1,0:T(2,128)(2,1)S(1)} %copy-done.4) | data formatting | bytes 8388608 | tf_op args[2]
  16.8 10.3 %shard_map.123 = (bf16[16,4,128,128]{3,2,1,0:T(8,128)(2,1)S(1)}, bf16[16,4,256,256]{3,2,1,0:T(8,128)(2,1)S(1)}) custom-call(s32[257]{0:T(512)S(1)} %concatenate.11.flat, bf16[16,4,128,128]{3,2,1,0:T(8,128)(2,1)S(1)} %bitcast.36, bf16[16,4,128,128]{3,2,1,0:T(8,128)(2,1)S(1)} %bitcast.56, f32[16,16,128]{2,1,0:T(8,128)S(1)} %maximum_convert_fusion.rate_ref.refs_3_.refs_9_), custom_call_target="tpu_custom_call" | custom-call | flops 1000 | bytes 1000 | tf_op jit(solution)/shard_map/pallas_call | solution.py:257
  32.1 10.3 %shard_map.124 = (bf16[16,4,128,128]{3,2,1,0:T(8,128)(2,1)S(1)}, bf16[16,4,256,256]{3,2,1,0:T(8,128)(2,1)S(1)}) custom-call(s32[257]{0:T(512)S(1)} %concatenate.11.flat, bf16[16,4,128,128]{3,2,1,0:T(8,128)(2,1)S(1)} %bitcast.37, bf16[16,4,128,128]{3,2,1,0:T(8,128)(2,1)S(1)} %bitcast.57, ...), custom_call_target="tpu_custom_call", output_to_operand_aliasing={{0}: (4, {}), {1}: (5, {})} | custom-call | flops 1000 | bytes 1000 | tf_op jit(solution)/shard_map/pallas_call | solution.py:257
  42.5 10.3 %shard_map.125 = (bf16[16,4,128,128]{3,2,1,0:T(8,128)(2,1)S(1)}, bf16[16,4,256,256]{3,2,1,0:T(8,128)(2,1)S(1)}) custom-call(s32[257]{0:T(512)S(1)} %concatenate.11.flat, bf16[16,4,128,128]{3,2,1,0:T(8,128)(2,1)S(1)} %bitcast.38, bf16[16,4,128,128]{3,2,1,0:T(8,128)(2,1)S(1)} %bitcast.58, f32[16,16,128]{2,1,0:T(8,128)S(1)} %maximum_convert_fusion.rate_ref.refs_3_.refs_9_), custom_call_target="tpu_custom_call" | custom-call | flops 1000 | bytes 1000 | tf_op jit(solution)/shard_map/pallas_call | solution.py:257
  53.1 3.2 %collective-permute-done.3.refs_14_ = s32[4,264,128]{2,1,0:T(8,128)S(1)} collective-permute-done((s32[4,264,128]{2,1,0:T(8,128)S(1)}, s32[4,264,128]{2,1,0:T(8,128)S(1)}, u32[]{:S(2)}, u32[]{:S(2)}) %collective-permute-start.3) | collective-permute-done | bytes 540704 | tf_op jit(solution)/shard_map/ppermute | solution.py:628
  58.4 6.1 %shard_map.126 = (bf16[16,4,2,128,128]{4,3,2,1,0:T(8,128)(2,1)S(1)}, s32[4,264,128]{2,1,0:T(8,128)S(1)}) custom-call(s32[257]{0:T(512)S(1)} %concatenate.11.flat, bf16[1,128]{1,0:T(2,128)(2,1)S(1)} %bitcast.77, bf16[16,4,128,128]{3,2,1,0:T(8,128)(2,1)S(1)} %bitcast.39, bf16[16,4,128,128]{3,2,1,0:T(8,128)(2,1)S(1)} %bitcast.59, ...), custom_call_target="tpu_custom_call" | custom-call | flops 1000 | bytes 1000 | tf_op jit(solution)/shard_map/pallas_call | solution.py:515
  65.4 5.9 %shard_map.127 = (bf16[16,4,2,128,128]{4,3,2,1,0:T(8,128)(2,1)S(1)}, s32[4,264,128]{2,1,0:T(8,128)S(1)}) custom-call(s32[257]{0:T(512)S(1)} %concatenate.11.flat, bf16[1,128]{1,0:T(2,128)(2,1)S(1)} %bitcast.78, bf16[16,4,128,128]{3,2,1,0:T(8,128)(2,1)S(1)} %bitcast.41, bf16[16,4,128,128]{3,2,1,0:T(8,128)(2,1)S(1)} %bitcast.61, ...), custom_call_target="tpu_custom_call", output_to_operand_aliasing={{0}: (18, {})} | custom-call | flops 1000 | bytes 1000 | tf_op jit(solution)/shard_map/pallas_call | solution.py:515
  71.3 2.9 %collective-permute-start.7 = (s32[4,264,128]{2,1,0:T(8,128)S(1)}, s32[4,264,128]{2,1,0:T(8,128)S(1)}, u32[]{:S(2)}, u32[]{:S(2)}) collective-permute-start(s32[4,264,128]{2,1,0:T(8,128)S(1)} %get-tuple-element.124), channel_id=1, source_target_pairs={{0,8},{4,12},{8,0},{12,4},{1,9},{5,13},{9,1},{13,5},{2,10},{6,14},... | collective-permute-start | bytes 1622024 | tf_op jit(solution)/shard_map/ppermute | solution.py:628
  74.2 6.0 %shard_map.128 = (bf16[16,4,2,128,128]{4,3,2,1,0:T(8,128)(2,1)S(1)}, s32[4,264,128]{2,1,0:T(8,128)S(1)}) custom-call(s32[257]{0:T(512)S(1)} %concatenate.11.flat, bf16[1,128]{1,0:T(2,128)(2,1)S(1)} %bitcast.79, bf16[16,4,128,128]{3,2,1,0:T(8,128)(2,1)S(1)} %bitcast.43, bf16[16,4,128,128]{3,2,1,0:T(8,128)(2,1)S(1)} %bitcast.63, ...), custom_call_target="tpu_custom_call", output_to_operand_aliasing={{0}: (18, {})} | custom-call | flops 1000 | bytes 1000 | tf_op jit(solution)/shard_map/pallas_call | solution.py:515
  80.2 10.3 %shard_map.129 = (bf16[16,4,128,128]{3,2,1,0:T(8,128)(2,1)S(1)}, bf16[16,4,256,256]{3,2,1,0:T(8,128)(2,1)S(1)}) custom-call(s32[257]{0:T(512)S(1)} %concatenate.11.flat, bf16[16,4,128,128]{3,2,1,0:T(8,128)(2,1)S(1)} %bitcast.45, bf16[16,4,128,128]{3,2,1,0:T(8,128)(2,1)S(1)} %bitcast.65, ...), custom_call_target="tpu_custom_call", output_to_operand_aliasing={{0}: (4, {}), {1}: (5, {})} | custom-call | flops 1000 | bytes 1000 | tf_op jit(solution)/shard_map/pallas_call | solution.py:257
  90.6 7.3 %collective-permute-done.5.refs_15_ = s32[4,264,128]{2,1,0:T(8,128)S(1)} collective-permute-done((s32[4,264,128]{2,1,0:T(8,128)S(1)}, s32[4,264,128]{2,1,0:T(8,128)S(1)}, u32[]{:S(2)}, u32[]{:S(2)}) %collective-permute-start.5) | collective-permute-done | bytes 540704 | tf_op jit(solution)/shard_map/ppermute | solution.py:628
  97.8 2.5 %collective-permute-start.11 = (s32[4,264,128]{2,1,0:T(8,128)S(1)}, s32[4,264,128]{2,1,0:T(8,128)S(1)}, u32[]{:S(2)}, u32[]{:S(2)}) collective-permute-start(s32[4,264,128]{2,1,0:T(8,128)S(1)} %get-tuple-element.134), channel_id=1, source_target_pairs={{0,4},{4,0},{8,12},{12,8},{1,5},{5,1},{9,13},{13,9},{2,6},{6,2},{1... | collective-permute-start | bytes 1622024 | tf_op jit(solution)/shard_map/ppermute | solution.py:628
  100.3 5.8 %shard_map.130 = (bf16[16,4,2,128,128]{4,3,2,1,0:T(8,128)(2,1)S(1)}, s32[4,264,128]{2,1,0:T(8,128)S(1)}) custom-call(s32[257]{0:T(512)S(1)} %concatenate.11.flat, bf16[1,128]{1,0:T(2,128)(2,1)S(1)} %bitcast.80, bf16[16,4,128,128]{3,2,1,0:T(8,128)(2,1)S(1)} %bitcast.46, bf16[16,4,128,128]{3,2,1,0:T(8,128)(2,1)S(1)} %bitcast.66, ...), custom_call_target="tpu_custom_call", output_to_operand_aliasing={{0}: (18, {})} | custom-call | flops 1000 | bytes 1000 | tf_op jit(solution)/shard_map/pallas_call | solution.py:515
  106.1 5.8 %shard_map.131 = (bf16[16,4,2,128,128]{4,3,2,1,0:T(8,128)(2,1)S(1)}, s32[4,264,128]{2,1,0:T(8,128)S(1)}) custom-call(s32[257]{0:T(512)S(1)} %concatenate.11.flat, bf16[1,128]{1,0:T(2,128)(2,1)S(1)} %bitcast.81, bf16[16,4,128,128]{3,2,1,0:T(8,128)(2,1)S(1)} %bitcast.48, bf16[16,4,128,128]{3,2,1,0:T(8,128)(2,1)S(1)} %bitcast.68, ...), custom_call_target="tpu_custom_call", output_to_operand_aliasing={{0}: (18, {})} | custom-call | flops 1000 | bytes 1000 | tf_op jit(solution)/shard_map/pallas_call | solution.py:515
  113.5 5.8 %shard_map.132 = (bf16[16,4,2,128,128]{4,3,2,1,0:T(8,128)(2,1)S(1)}, s32[4,264,128]{2,1,0:T(8,128)S(1)}) custom-call(s32[257]{0:T(512)S(1)} %concatenate.11.flat, bf16[1,128]{1,0:T(2,128)(2,1)S(1)} %bitcast.82, bf16[16,4,128,128]{3,2,1,0:T(8,128)(2,1)S(1)} %bitcast.50, bf16[16,4,128,128]{3,2,1,0:T(8,128)(2,1)S(1)} %bitcast.70, ...), custom_call_target="tpu_custom_call", output_to_operand_aliasing={{0}: (18, {})} | custom-call | flops 1000 | bytes 1000 | tf_op jit(solution)/shard_map/pallas_call | solution.py:515
  119.3 3.0 %collective-permute-start.8 = (s32[4,264,128]{2,1,0:T(8,128)S(1)}, s32[4,264,128]{2,1,0:T(8,128)S(1)}, u32[]{:S(2)}, u32[]{:S(2)}) collective-permute-start(s32[4,264,128]{2,1,0:T(8,128)S(1)} %get-tuple-element.129), channel_id=1, source_target_pairs={{0,4},{4,0},{8,12},{12,8},{1,5},{5,1},{9,13},{13,9},{2,6},{6,2},{1... | collective-permute-start | bytes 1622024 | tf_op jit(solution)/shard_map/ppermute | solution.py:628
  122.3 6.7 %shard_map.133 = (bf16[16,4,2,128,128]{4,3,2,1,0:T(8,128)(2,1)S(1)}, f32[16,8,128,128]{3,2,1,0:T(8,128)}) custom-call(s32[257]{0:T(512)S(1)} %concatenate.11.flat, bf16[1,128]{1,0:T(2,128)(2,1)S(1)} %bitcast.83, bf16[16,4,128,128]{3,2,1,0:T(8,128)(2,1)S(1)} %bitcast.52, bf16[16,4,128,128]{3,2,1,0:T(8,128)(2,1)S(1)} %bitcast.72, ...), custom_call_target="tpu_custom_call", output_to_operand_aliasing={{0}: (18, {})} | custom-call | flops 1000 | bytes 1000 | tf_op jit(solution)/shard_map/pallas_call | solution.py:515
  129.1 6.7 %shard_map.134 = (bf16[16,4,2,128,128]{4,3,2,1,0:T(8,128)(2,1)S(1)}, f32[16,8,128,128]{3,2,1,0:T(8,128)}) custom-call(s32[257]{0:T(512)S(1)} %concatenate.11.flat, bf16[1,128]{1,0:T(2,128)(2,1)S(1)} %bitcast.84, bf16[16,4,128,128]{3,2,1,0:T(8,128)(2,1)S(1)} %bitcast.54, ...), custom_call_target="tpu_custom_call", output_to_operand_aliasing={{0}: (18, {}), {1}: (19, {})} | custom-call | flops 1000 | bytes 1000 | tf_op jit(solution)/shard_map/pallas_call | solution.py:515
  135.7 6.4 %shard_map.135 = bf16[16,128,8,128]{3,2,1,0:T(8,128)(2,1)} custom-call(bf16[16,4,2,128,128]{4,3,2,1,0:T(8,128)(2,1)S(1)} %get-tuple-element.128.mixed_ref), custom_call_target="tpu_custom_call" | custom-call | flops 1000 | bytes 1000 | tf_op jit(solution)/shard_map/pallas_call | solution.py:593
  142.2 3.4 %shard_map.136.refs_1_ = f32[16,8,128,128]{3,2,1,0:T(8,128)} custom-call(s32[257]{0:T(512)S(1)} %concatenate.11.flat, s32[4,264,128]{2,1,0:T(8,128)S(1)} %collective-permute-done.6.refs_0_, s32[4,264,128]{2,1,0:T(8,128)S(1)} %collective-permute-done.7.refs_1_, s32[4,264,128]{2,1,0:T(8,128)S(1)} %collective-permute-done.11.refs_2_, ...), custom_call_target="tpu_custom_call", output_to_operand_aliasing={{}: (4, {})} | custom-call | flops 1000 | bytes 1000 | tf_op jit(solution)/shard_map/pallas_call | solution.py:566
  145.6 13.2 %collective-permute-done.10.refs_0_ = s32[4,264,128]{2,1,0:T(8,128)S(1)} collective-permute-done((s32[4,264,128]{2,1,0:T(8,128)S(1)}, s32[4,264,128]{2,1,0:T(8,128)S(1)}, u32[]{:S(2)}, u32[]{:S(2)}) %collective-permute-start.10) | collective-permute-done | bytes 540704 | tf_op jit(solution)/shard_map/ppermute | solution.py:628
  (45 shorter events, 19.0 us)
Async XLA Ops:
  0.6 1.6 copy-start.2
  2.8 25.7 %collective-permute-start = (s32[4,264,128]{2,1,0:T(8,128)S(1)}, s32[4,264,128]{2,1,0:T(8,128)}, u32[]{:S(2)}, u32[]{:S(2)}) collective-permute-start(s32[4,264,128]{2,1,0:T(8,128)S(1)} %get-tuple-element.94.refs_12_), channel_id=1, source_target_pairs={{0,8},{4,12},{8,0},{12,4},{1,9},{5,13},{9,1},{13,5},{2,10},{6,14},... | collective-permute-start | bytes 1622024 | tf_op jit(solution)/shard_map/ppermute | solution.py:628
  7.6 45.2 %collective-permute-start.1 = (s32[4,264,128]{2,1,0:T(8,128)S(1)}, s32[4,264,128]{2,1,0:T(8,128)}, u32[]{:S(2)}, u32[]{:S(2)}) collective-permute-start(s32[4,264,128]{2,1,0:T(8,128)S(1)} %get-tuple-element.94.refs_12_), channel_id=1, source_target_pairs={{0,4},{4,0},{8,12},{12,8},{1,5},{5,1},{9,13},{13,9},{2,6},{6,2},{1... | collective-permute-start | bytes 1622024 | tf_op jit(solution)/shard_map/ppermute | solution.py:628
  8.2 3.6 %copy-start.4 = (bf16[16,128,4,2,128]{4,3,2,1,0:T(2,128)(2,1)S(1)}, bf16[16,128,4,2,128]{4,3,2,1,0:T(2,128)(2,1)}, u32[]{:S(2)}) copy-start(bf16[16,128,4,2,128]{4,3,2,1,0:T(2,128)(2,1)} %param.13) | copy-start | bytes 12582916
  11.8 3.3 %copy-start.7 = (s32[64]{0:T(128)S(1)}, s32[64]{0:T(128)}, u32[]{:S(2)}) copy-start(s32[64]{0:T(128)} %param.18) | copy-start | bytes 772
  11.8 3.3 %copy-start.8 = (s32[64]{0:T(128)S(1)}, s32[64]{0:T(128)}, u32[]{:S(2)}) copy-start(s32[64]{0:T(128)} %param.19) | copy-start | bytes 772
  11.8 3.3 %copy-start.9 = (s32[64]{0:T(128)S(1)}, s32[64]{0:T(128)}, u32[]{:S(2)}) copy-start(s32[64]{0:T(128)} %param.20) | copy-start | bytes 772
  11.8 3.3 %copy-start.10 = (s32[64]{0:T(128)S(1)}, s32[64]{0:T(128)}, u32[]{:S(2)}) copy-start(s32[64]{0:T(128)} %param.21) | copy-start | bytes 772
  11.8 3.4 %copy-start.5 = (bf16[16,128,4,2]{1,3,2,0:T(2,128)(2,1)S(1)}, bf16[16,128,4,2]{1,3,2,0:T(2,128)(2,1)}, u32[]{:S(2)}) copy-start(bf16[16,128,4,2]{1,3,2,0:T(2,128)(2,1)} %param.15) | copy-start | bytes 98308
  11.8 3.4 %copy-start.6 = (bf16[16,128,4,2]{1,3,2,0:T(2,128)(2,1)S(1)}, bf16[16,128,4,2]{1,3,2,0:T(2,128)(2,1)}, u32[]{:S(2)}) copy-start(bf16[16,128,4,2]{1,3,2,0:T(2,128)(2,1)} %param.14) | copy-start | bytes 98308
  15.2 1.6 copy-start.1
  28.5 24.6 %collective-permute-start.2 = (s32[4,264,128]{2,1,0:T(8,128)}, s32[4,264,128]{2,1,0:T(8,128)S(1)}, u32[]{:S(2)}, u32[]{:S(2)}) collective-permute-start(s32[4,264,128]{2,1,0:T(8,128)} %collective-permute-done.refs_14_), channel_id=1, source_target_pairs={{0,4},{4,0},{8,12},{12,8},{1,5},{5,1},{9,13},{13,9},{2,6},{6,2},{1... | collective-permute-start | bytes 1622024 | tf_op jit(solution)/shard_map/ppermute | solution.py:628
  30.1 26.3 %collective-permute-start.3 = (s32[4,264,128]{2,1,0:T(8,128)S(1)}, s32[4,264,128]{2,1,0:T(8,128)S(1)}, u32[]{:S(2)}, u32[]{:S(2)}) collective-permute-start(s32[4,264,128]{2,1,0:T(8,128)S(1)} %get-tuple-element.114.refs_12_), channel_id=1, source_target_pairs={{0,8},{4,12},{8,0},{12,4},{1,9},{5,13},{9,1},{13,5},{2,10},{6,14},... | collective-permute-start | bytes 1622024 | tf_op jit(solution)/shard_map/ppermute | solution.py:628
  42.4 16.0 %copy-start = (bf16[16,128,4,2,128]{4,1,3,2,0:T(8,128)(2,1)S(1)}, bf16[16,128,4,2,128]{4,1,3,2,0:T(8,128)(2,1)}, u32[]{:S(2)}) copy-start(bf16[16,128,4,2,128]{4,1,3,2,0:T(8,128)(2,1)} %copy.35) | copy-start | bytes 12582916
  42.5 16.0 %copy-start.3 = (bf16[128]{0:T(256)(128)(2,1)S(1)}, bf16[128]{0:T(256)(128)(2,1)}, u32[]{:S(2)}) copy-start(bf16[128]{0:T(256)(128)(2,1)} %param.16) | copy-start | bytes 772
  56.4 34.2 %collective-permute-start.4 = (s32[4,264,128]{2,1,0:T(8,128)S(1)}, s32[4,264,128]{2,1,0:T(8,128)S(1)}, u32[]{:S(2)}, u32[]{:S(2)}) collective-permute-start(s32[4,264,128]{2,1,0:T(8,128)S(1)} %get-tuple-element.114.refs_12_), channel_id=1, source_target_pairs={{0,4},{4,0},{8,12},{12,8},{1,5},{5,1},{9,13},{13,9},{2,6},{6,2},{1... | collective-permute-start | bytes 1622024 | tf_op jit(solution)/shard_map/ppermute | solution.py:628
  57.9 40.0 %collective-permute-start.5 = (s32[4,264,128]{2,1,0:T(8,128)S(1)}, s32[4,264,128]{2,1,0:T(8,128)S(1)}, u32[]{:S(2)}, u32[]{:S(2)}) collective-permute-start(s32[4,264,128]{2,1,0:T(8,128)S(1)} %collective-permute-done.3.refs_14_), channel_id=1, source_target_pairs={{0,4},{4,0},{8,12},{12,8},{1,5},{5,1},{9,13},{13,9},{2,6},{6,2},{1... | collective-permute-start | bytes 1622024 | tf_op jit(solution)/shard_map/ppermute | solution.py:628
  64.5 35.8 %collective-permute-start.6 = (s32[4,264,128]{2,1,0:T(8,128)S(1)}, s32[4,264,128]{2,1,0:T(8,128)S(1)}, u32[]{:S(2)}, u32[]{:S(2)}) collective-permute-start(s32[4,264,128]{2,1,0:T(8,128)S(1)} %get-tuple-element.119), channel_id=1, source_target_pairs={{0,12},{4,8},{8,4},{12,0},{1,13},{5,9},{9,5},{13,1},{2,14},{6,10},... | collective-permute-start | bytes 1622024 | tf_op jit(solution)/shard_map/ppermute | solution.py:628
  71.3 51.0 %collective-permute-start.7 = (s32[4,264,128]{2,1,0:T(8,128)S(1)}, s32[4,264,128]{2,1,0:T(8,128)S(1)}, u32[]{:S(2)}, u32[]{:S(2)}) collective-permute-start(s32[4,264,128]{2,1,0:T(8,128)S(1)} %get-tuple-element.124), channel_id=1, source_target_pairs={{0,8},{4,12},{8,0},{12,4},{1,9},{5,13},{9,1},{13,5},{2,10},{6,14},... | collective-permute-start | bytes 1622024 | tf_op jit(solution)/shard_map/ppermute | solution.py:628
  97.8 44.3 %collective-permute-start.11 = (s32[4,264,128]{2,1,0:T(8,128)S(1)}, s32[4,264,128]{2,1,0:T(8,128)S(1)}, u32[]{:S(2)}, u32[]{:S(2)}) collective-permute-start(s32[4,264,128]{2,1,0:T(8,128)S(1)} %get-tuple-element.134), channel_id=1, source_target_pairs={{0,4},{4,0},{8,12},{12,8},{1,5},{5,1},{9,13},{13,9},{2,6},{6,2},{1... | collective-permute-start | bytes 1622024 | tf_op jit(solution)/shard_map/ppermute | solution.py:628
  112.0 48.5 %collective-permute-start.9 = (s32[4,264,128]{2,1,0:T(8,128)S(1)}, s32[4,264,128]{2,1,0:T(8,128)S(1)}, u32[]{:S(2)}, u32[]{:S(2)}) collective-permute-start(s32[4,264,128]{2,1,0:T(8,128)S(1)} %get-tuple-element.130), channel_id=1, source_target_pairs={{0,8},{4,12},{8,0},{12,4},{1,9},{5,13},{9,1},{13,5},{2,10},{6,14},... | collective-permute-start | bytes 1622024 | tf_op jit(solution)/shard_map/ppermute | solution.py:628
  112.1 46.7 %collective-permute-start.10 = (s32[4,264,128]{2,1,0:T(8,128)S(1)}, s32[4,264,128]{2,1,0:T(8,128)S(1)}, u32[]{:S(2)}, u32[]{:S(2)}) collective-permute-start(s32[4,264,128]{2,1,0:T(8,128)S(1)} %get-tuple-element.131), channel_id=1, source_target_pairs={{0,12},{4,8},{8,4},{12,0},{1,13},{5,9},{9,5},{13,1},{2,14},{6,10},... | collective-permute-start | bytes 1622024 | tf_op jit(solution)/shard_map/ppermute | solution.py:628
  119.3 42.7 %collective-permute-start.8 = (s32[4,264,128]{2,1,0:T(8,128)S(1)}, s32[4,264,128]{2,1,0:T(8,128)S(1)}, u32[]{:S(2)}, u32[]{:S(2)}) collective-permute-start(s32[4,264,128]{2,1,0:T(8,128)S(1)} %get-tuple-element.129), channel_id=1, source_target_pairs={{0,4},{4,0},{8,12},{12,8},{1,5},{5,1},{9,13},{13,9},{2,6},{6,2},{1... | collective-permute-start | bytes 1622024 | tf_op jit(solution)/shard_map/ppermute | solution.py:628
